TPU v7x, 32 devices: a whole 2x2x4 slice. The times are simulated.
32 devices in a mesh: ctx: 8 (over z, y), head: 4 (over x, core).
Axes of the slice: x: 2, y: 2, z: 4, core: 2. Of those that a mesh axis runs over, the one named last changes fastest.
Arguments:
- queries: bfloat16 [2048, 4096], P('ctx', 'head'), may hold values from -10 to 10
- key_states: bfloat16 [2048, 256], P('ctx'), may hold values from -10 to 10
- value_states: bfloat16 [2048, 256], P('ctx'), may hold values from -6 to 6
- vertical_blocks: int32 [32, 4], P('head'), may hold values from 0 to 15, as said below
- slash_offsets: int32 [32, 4], P('head'), may hold values from 0 to 15, as said below
- positions: int32 [2048], P('ctx'), may hold values from 0 to 32767, as said below
- out_weight: bfloat16 [4096, 16384], P('head', 'ctx'), may hold values from -0.5 to 0.5
Outputs:
- projected: bfloat16 [2048, 16384], P('head', 'ctx')
Inputs may be any that keep to these rules, and one draw needn't show every extreme that they name: `vertical_blocks`: each head's 4 vertical blocks are distinct. `slash_offsets`: each head's 4 offsets are distinct and the first of them is 0. `positions`: positions rise by one inside each block of 128 tokens; block b starts at a multiple of 128 at or after b * 2048 and before (b + 1) * 2048.
All inputs are finite; a program needn't handle non-finite values.
Results may differ from a plain program's by a relative error of at most 0.025.
Values may be sent and summed in bfloat16 or wider, within the bound.
No kernel may reach another device: no remote copies, remote signals or barrier semaphores. Data moves between devices by JAX's collectives and lax.ppermute only.
A program may use at most 64 MiB of HBM per device.

v0:
```python
import math

import jax
import jax.numpy as jnp
from jax import lax
from jax.sharding import PartitionSpec as P

HD = 128
GROUP = 16
BLK = 128


def rotate_heads(states, positions):
    half_width = states.shape[-1] // 2
    exponents = jnp.arange(half_width, dtype=jnp.float32) * (2.0 / states.shape[-1])
    inverse_freq = 500000.0 ** (-exponents)
    angles = positions.astype(jnp.float32)[:, None] * inverse_freq[None, :]
    cosine = jnp.cos(angles)[:, None, :]
    sine_part = jnp.sin(angles)[:, None, :]
    front_half = states[..., :half_width]
    back_half = states[..., half_width:]
    return jnp.concatenate(
        [front_half * cosine - back_half * sine_part, back_half * cosine + front_half * sine_part],
        axis=-1,
    )


def per_device(
    queries, key_states, value_states, vertical_blocks, slash_offsets, positions, out_weight
):
    local_tokens = queries.shape[0]
    local_heads = queries.shape[1] // HD
    head_index = lax.axis_index("head")
    ctx_index = lax.axis_index("ctx")
    shared_head = head_index * local_heads // GROUP
    own_keys = lax.dynamic_slice_in_dim(key_states, shared_head * HD, HD, 1)
    own_values = lax.dynamic_slice_in_dim(value_states, shared_head * HD, HD, 1)
    rotated_own = rotate_heads(own_keys.astype(jnp.float32)[:, None, :], positions)[:, 0, :].astype(
        jnp.bfloat16
    )
    all_keys, all_values = (
        lax.all_gather(rotated_own, "ctx", axis=0, tiled=True),
        lax.all_gather(own_values, "ctx", axis=0, tiled=True),
    )
    query_rot = rotate_heads(
        queries.astype(jnp.float32).reshape(local_tokens, local_heads, HD), positions
    ).astype(jnp.bfloat16)
    query_blocks = local_tokens // BLK
    key_count = all_keys.shape[0] // BLK
    block_ids = ctx_index * query_blocks + jnp.arange(query_blocks, dtype=jnp.int32)
    vert_slots = jnp.broadcast_to(
        vertical_blocks[:, None, :], (local_heads, query_blocks, vertical_blocks.shape[1])
    )
    vert_valid = vert_slots <= block_ids[None, :, None]
    slash_slots = block_ids[None, :, None] - slash_offsets[:, None, :]
    repeated = jnp.any(slash_slots[..., None] == vertical_blocks[:, None, None, :], axis=-1)
    slash_valid = (slash_slots >= 0) & jnp.logical_not(repeated)
    slot_blocks = jnp.concatenate([vert_slots, slash_slots], axis=-1)
    slot_valid = jnp.concatenate([vert_valid, slash_valid], axis=-1)
    safe_blocks = jnp.clip(slot_blocks, 0, key_count - 1)
    key_tiles = all_keys.reshape(key_count, BLK, HD)[safe_blocks]
    value_tiles = all_values.reshape(key_count, BLK, HD)[safe_blocks]
    query_tiles = query_rot.reshape(query_blocks, BLK, local_heads, HD).transpose(2, 0, 1, 3)
    scores = jnp.einsum(
        "hqrd,hqskd->hqrsk", query_tiles, key_tiles, preferred_element_type=jnp.float32
    ) / math.sqrt(HD)
    diagonal = (slot_blocks == block_ids[None, :, None])[:, :, None, :, None]
    causal_pairs = (jnp.arange(BLK)[None, :] <= jnp.arange(BLK)[:, None])[None, None, :, None, :]
    allowed = slot_valid[:, :, None, :, None] & (jnp.logical_not(diagonal) | causal_pairs)
    masked = jnp.where(allowed, scores, -1e30)
    row_max = jnp.max(masked, axis=(3, 4), keepdims=True)
    exponentials = jnp.exp(masked - row_max)
    weights = (exponentials / jnp.sum(exponentials, axis=(3, 4), keepdims=True)).astype(
        jnp.bfloat16
    )
    attended = jnp.einsum(
        "hqrsk,hqskd->hqrd", weights, value_tiles, preferred_element_type=jnp.float32
    ).astype(jnp.bfloat16)
    head_out = attended.transpose(1, 2, 0, 3).reshape(local_tokens, local_heads * HD)
    partial_terms = jnp.dot(
        lax.all_gather(head_out, "ctx", axis=0, tiled=True),
        out_weight,
        preferred_element_type=jnp.float32,
    )
    projected = lax.psum_scatter(
        partial_terms.astype(jnp.bfloat16), "head", scatter_dimension=0, tiled=True
    )
    return projected


def solution(mesh):
    placed = (
        P("ctx", "head"),
        P("ctx", None),
        P("ctx", None),
        P("head", None),
        P("head", None),
        P("ctx"),
        P("head", "ctx"),
    )
    return jax.shard_map(
        per_device, mesh=mesh, in_specs=placed, out_specs=P("head", "ctx"), check_vma=False
    )
```

profile of v0, /device:TPU:0, one launch (start us, length us, event | category | flops | bytes accessed | tf_op | source)
XLA Modules:
  0.0 264.0 jit_solution(10191480663979347812)
XLA Ops:
  6.5 0.0 copy-start
  6.5 0.0 all-gather.3.cloned.1.call-start
  6.6 0.6 iota_compare_fusion
  7.2 0.3 copy-done
  7.5 0.1 copy.56
  7.6 0.7 convert_element_type.25
  8.3 0.5 multiply_cosine_fusion
  8.8 0.3 fusion.14
  9.2 33.0 %all-gather = bf16[2048,1,128]{0,2,1:T(8,128)(2,1)S(1)} all-gather(bf16[256,1,128]{0,2,1:T(8,128)(2,1)S(1)} %pad_maximum_fusion), channel_id=2, replica_groups=mesh['ctx'=8,'head'=4] {'ctx'}, dimensions={0}, use_global_device_ids=true | all-gather | bytes 589824 | tf_op jit(solution)/shard_map/all_gather | solution.py:42
  42.2 0.3 copy.53
  42.4 0.0 copy-start.3
  42.5 0.8 broadcast_subtract_fusion
  43.3 0.7 broadcast_in_dim.15
  44.0 0.1 copy.46
  44.0 0.1 reshape.189
  44.1 0.7 compare_reduce_fusion
  44.8 0.8 broadcast_compare_fusion
  45.6 0.1 copy.41
  45.7 0.7 broadcast_in_dim.12
  46.4 0.1 fusion.17
  46.5 0.1 copy.42
  46.6 1.1 convert_bitcast_fusion
  47.7 0.2 copy.57
  48.0 0.3 fusion.21
  48.3 0.0 copy-done.3
  48.3 31.3 %all_gather.10 = bf16[2048,128]{1,0:T(8,128)(2,1)S(1)} all-gather(bf16[256,128]{1,0:T(8,128)(2,1)S(1)} %constant_dynamic-slice_fusion), channel_id=1, replica_groups=mesh['ctx'=8,'head'=4] {'ctx'}, dimensions={0}, use_global_device_ids=true | all-gather | bytes 589824 | tf_op jit(solution)/shard_map/all_gather | solution.py:43
  79.6 3.1 %gather_fusion = bf16[128,128,128]{2,1,0:T(8,128)(2,1)} fusion(bf16[16,128,128]{2,1,0:T(8,128)(2,1)S(1)} %bitcast.43, s32[1024]{0:T(1024)S(1)} %pad_clamp_fusion), kind=kCustom, calls=%fused_computation | custom fusion | bytes 8389120 | tf_op jit(solution)/shard_map/gather | solution.py:61
  82.7 0.0 copy-start.2
  82.7 3.0 %gather_fusion.1 = bf16[128,128,128]{2,1,0:T(8,128)(2,1)} fusion(bf16[16,128,128]{2,1,0:T(8,128)(2,1)S(1)} %bitcast.44, s32[1024]{0:T(1024)S(1)} %pad_clamp_fusion), kind=kCustom, calls=%fused_computation.1 | custom fusion | bytes 8389120 | tf_op jit(solution)/shard_map/gather | solution.py:62
  85.7 0.4 subtract_convert_fusion
  86.1 0.0 copy-done.2
  86.1 3.9 %fusion.1 = (f32[8,2,128]{2,1,0:T(2,128)S(1)}, f32[8,2,128,8,128]{2,4,3,1,0:T(8,128)S(1)}) fusion(pred[128,128]{0,1:T(8,128)(4,1)S(1)} %copy-done.2, pred[8,2,8]{2,1,0:T(4,128)(4,1)S(1)} %copy.42, pred[8,2,8]{2,1,0:T(4,128)(4,1)S(1)} %copy.41, bf16[8,2,8,128,128]{4,3,2,1,0:T(8,128)(2,1)} %bitcast.47, bf16[2,128,8,64]{3,1,0,2:T(8,128)(2,1)S(1)} %bitcast.51, ...), kind=kOutput, calls=%fused_computation.7 | convolution fusion | flops 548403200 | bytes 13132032 | tf_op jit(solution)/shard_map/hqrd,hqskd->hqrsk/dot_general | solution.py:64
  90.0 0.0 copy-start.1
  90.0 3.0 %fusion = f32[8,2,128]{2,1,0:T(2,128)S(1)} fusion(f32[8,2,128,8,128]{2,4,3,1,0:T(8,128)S(1)} %get-tuple-element.18, f32[8,2,128]{2,1,0:T(2,128)S(1)} %get-tuple-element.17, pred[128,128]{0,1:T(8,128)(4,1)S(1)} %copy-done.2, pred[8,2,8]{2,1,0:T(4,128)(4,1)S(1)} %copy.42, pred[8,2,8]{2,1,0:T(4,128)(4,1)S(1)} %copy.41), kind=kLoop, calls=%fused_computation.6 | loop fusion | flops 12580864 | bytes 8421632 | tf_op jit(solution)/shard_map/reduce_sum | solution.py:73
  93.1 0.0 copy-done.1
  93.1 3.8 %fusion.5 = bf16[2,128,8,128]{3,1,0,2:T(8,128)(2,1)S(1)} fusion(bf16[8,2,8,128,128]{4,3,2,1,0:T(8,128)(2,1)S(1)} %bitcast.46, f32[8,2,128,8,128]{2,4,3,1,0:T(8,128)S(1)} %get-tuple-element.18, f32[8,2,128]{2,1,0:T(2,128)S(1)} %fusion, f32[8,2,128]{2,1,0:T(2,128)S(1)} %get-tuple-element.17, pred[128,128]{0,1:T(8,128)(4,1)S(1)} %copy-done.2, ...), kind=kOutput, calls=%fused_computation.11 | convolution fusion | flops 551813120 | bytes 13140224 | tf_op jit(solution)/shard_map/hqrsk,hqskd->hqrd/dot_general | solution.py:76
  96.9 0.3 copy.49
  97.3 0.9 copy.64
  98.2 0.0 all-gather.3.cloned.1.call-update
  98.2 0.2 reduce-scatter.2.cloned.1.call-start
  98.4 74.5 %all-gather.3.cloned.1.call-done = bf16[2048,1024]{1,0:T(8,128)(2,1)} async-done(((bf16[256,1024]{1,0:T(8,128)(2,1)}), bf16[2048,1024]{1,0:T(8,128)(2,1)}) %all-gather.3.cloned.1.call-update) | async-done | bytes 4194320 | tf_op jit(solution)/shard_map/all_gather | solution.py:81
  173.0 14.0 %convolution_convert_fusion = bf16[2048,2048]{1,0:T(8,128)(2,1)} fusion(bf16[2048,1024]{1,0:T(8,128)(2,1)} %all-gather.3.cloned.1.call-done, bf16[1024,2048]{1,0:T(8,128)(2,1)} %param.13), kind=kOutput, calls=%fused_computation.5 | convolution fusion | flops 8594128896 | bytes 16777216 | tf_op jit(solution)/shard_map/dot_general | solution.py:80
  187.0 0.0 reduce-scatter.2.cloned.1.call-update
  187.0 70.1 %reduce-scatter.2.cloned.1.call-done = bf16[512,2048]{1,0:T(8,128)(2,1)} async-done(((bf16[2048,2048]{1,0:T(8,128)(2,1)}), bf16[512,2048]{1,0:T(8,128)(2,1)}) %reduce-scatter.2.cloned.1.call-update) | async-done | bytes 2097168 | tf_op jit(solution)/shard_map/reduce_scatter | solution.py:85
  (9 shorter events, 0.1 us)
Async XLA Ops:
  6.5 0.9 copy-start
  6.5 166.4 %all-gather.3.cloned.1.call-start = ((), (), s32[]{:S(2)}) async-start(), calls=%async_computation.1 | async-start | bytes 4718592 | tf_op jit(solution)/shard_map/all_gather | solution.py:81
  42.4 5.9 %copy-start.3 = (bf16[256,256]{1,0:T(8,128)(2,1)S(1)}, bf16[256,256]{1,0:T(8,128)(2,1)}, u32[]{:S(2)}) copy-start(bf16[256,256]{1,0:T(8,128)(2,1)} %param.9) | copy-start | bytes 393220
  82.7 3.4 %copy-start.2 = (pred[128,128]{0,1:T(8,128)(4,1)S(1)}, pred[128,128]{0,1:T(8,128)(4,1)}, u32[]{:S(2)}) copy-start(pred[128,128]{0,1:T(8,128)(4,1)} %iota_compare_fusion) | copy-start | bytes 49156
  90.0 3.1 %copy-start.1 = (bf16[128,128,128]{2,1,0:T(8,128)(2,1)S(1)}, bf16[128,128,128]{2,1,0:T(8,128)(2,1)}, u32[]{:S(2)}) copy-start(bf16[128,128,128]{2,1,0:T(8,128)(2,1)} %gather_fusion.1) | copy-start | bytes 12582916
  98.2 158.9 %reduce-scatter.2.cloned.1.call-start = ((), (), s32[]{:S(2)}) async-start(), calls=%async_computation.2 | async-start | bytes 10485760 | tf_op jit(solution)/shard_map/reduce_scatter | solution.py:85
Sparse Core Ops, SparseCore 0:
  98.3 74.5 all-gather.2
  187.1 69.9 reduce-scatter.1
where the time goes:
time: 264 us
  waiting for transfers between devices  145 us (55%)
  blocking collectives  64.3 us (24%)
  matrix products  21.8 us (8%)
  between operations  13.6 us (5%)
  local copies, waits for them, and re-layouts  10.3 us (4%)
  other arithmetic  9.18 us (3%)
    all_gather x1, waiting for transfers between devices, per_device(): lax.all_gather(head_out, 'ctx', axis=0, tiled=True)  74.5 us
    reduce_scatter x1, waiting for transfers between devices, per_device(): lax.psum_scatter(partial_terms.astype(jnp.bfloat16), 'head', scatter_dime...  70.1 us
    all_gather x1, blocking collectives, per_device(): lax.all_gather(rotated_own, 'ctx', axis=0, tiled=True)  33 us
    all_gather x1, blocking collectives, per_device(): lax.all_gather(own_values, 'ctx', axis=0, tiled=True)  31.3 us
    dot_general x1, matrix products, per_device(): jnp.dot(lax.all_gather(head_out, 'ctx', axis=0, tiled=True), out_weight,...  14 us
  transfers between devices with their start and end apart: 2, of which 2 were waited for; matrix products, arithmetic and copies ran while one was open for 0% of the time, Pallas kernels for 0%

commit v1 on v0

v1 whole, which is shorter than its diff:
```python
import functools
import math

import jax
import jax.numpy as jnp
from jax import lax
from jax.experimental import pallas as pl
from jax.experimental.pallas import tpu as pltpu
from jax.sharding import PartitionSpec as P

HD = 128
GROUP = 16
BLK = 128
NEG = -1e30
SCALE = math.log2(math.e) / math.sqrt(HD)


def rotation_tables(positions):
    half = HD // 2
    exponents = jnp.arange(half, dtype=jnp.float32) * (2.0 / HD)
    inverse_freq = 500000.0 ** (-exponents)
    angles = positions.astype(jnp.float32)[:, None] * inverse_freq[None, :]
    cosine, sine = jnp.cos(angles), jnp.sin(angles)
    return jnp.concatenate([cosine, cosine], axis=1), jnp.concatenate([-sine, sine], axis=1)


def rotate(states, cosine, sine):
    states = states.astype(jnp.float32)
    return states * cosine + pltpu.roll(states, HD // 2, 1) * sine


def key_kernel(place, keys, values, cosine, sine, out):
    first = pl.multiple_of(place[0] * BLK, BLK)
    lane = pl.multiple_of(place[1] * HD, HD)
    rows = pl.ds(first, BLK)
    rotated = rotate(keys[rows, pl.ds(lane, HD)], cosine[rows, :], sine[rows, :])
    out[:, :HD] = rotated.astype(out.dtype)
    out[:, HD:] = values[rows, pl.ds(lane, HD)]


def attention_kernel(place, vertical, slash, queries, cosine, sine, own, other, out):
    head = pl.program_id(0)
    ctx, core = place[0], place[1]
    tri = (
        lax.broadcasted_iota(jnp.int32, (BLK, BLK), 1)
        <= lax.broadcasted_iota(jnp.int32, (BLK, BLK), 0)
    )
    verts = [vertical[head, i] for i in range(vertical.shape[1])]
    query_blocks = queries.shape[0] // BLK
    for local in range(query_blocks):
        block = ctx * query_blocks + local
        rows = pl.ds(local * BLK, BLK)
        rot = rotate(queries[rows, :], cosine[rows, :], sine[rows, :]).astype(jnp.bfloat16)
        slots = [(block, None)]
        for v in verts:
            slots.append((v, v < block))
        for j in range(1, slash.shape[1]):
            u = block - slash[head, j]
            ok = u >= 0
            for v in verts:
                ok = jnp.logical_and(ok, u != v)
            slots.append((jnp.maximum(u, 0), ok))
        tiles, scores = [], []
        for u, ok in slots:
            start = pl.multiple_of(((u // 2) ^ ctx) * BLK, BLK)
            mine = (u % 2) == core
            tile = jnp.where(mine, own[pl.ds(start, BLK), :], other[pl.ds(start, BLK), :])
            s = lax.dot_general(
                rot, tile[:, :HD], (((1,), (1,)), ((), ())), preferred_element_type=jnp.float32
            )
            s = jnp.where(tri, s, NEG) if ok is None else s + jnp.where(ok, 0.0, NEG)
            tiles.append(tile)
            scores.append(s)
        top = functools.reduce(jnp.maximum, scores)
        top = jnp.max(top, axis=1, keepdims=True)
        total, acc = None, None
        for s, tile in zip(scores, tiles):
            e = jnp.exp2((s - top) * SCALE)
            total = e if total is None else total + e
            o = jnp.dot(e.astype(jnp.bfloat16), tile[:, HD:], preferred_element_type=jnp.float32)
            acc = o if acc is None else acc + o
        total = jnp.sum(total, axis=1, keepdims=True)
        out[rows, :] = (acc / total).astype(out.dtype)


def attend(ctx, core, vertical, slash, queries, cosine, sine, own, other):
    tokens, width = queries.shape
    heads = width // HD
    whole = lambda a: pl.BlockSpec(a.shape, lambda h, *_: (0, 0))
    return pl.pallas_call(
        attention_kernel,
        grid_spec=pltpu.PrefetchScalarGridSpec(
            num_scalar_prefetch=3,
            grid=(heads,),
            in_specs=[
                pl.BlockSpec((tokens, HD), lambda h, *_: (0, h)),
                whole(cosine),
                whole(sine),
                whole(own),
                whole(other),
            ],
            out_specs=pl.BlockSpec((tokens, HD), lambda h, *_: (0, h)),
        ),
        out_shape=jax.ShapeDtypeStruct((tokens, width), jnp.bfloat16),
        name="attention",
    )(jnp.stack([ctx, core]), vertical, slash, queries, cosine, sine, own, other)


def pack_keys(core, shared_head, key_states, value_states, cosine, sine):
    vmem = pl.BlockSpec(memory_space=pltpu.VMEM)
    return pl.pallas_call(
        key_kernel,
        in_specs=[pl.BlockSpec(memory_space=pltpu.SMEM)] + [vmem] * 4,
        out_specs=vmem,
        out_shape=jax.ShapeDtypeStruct((BLK, 2 * HD), jnp.bfloat16),
        name="pack_keys",
    )(jnp.stack([core, shared_head]), key_states, value_states, cosine, sine)


def route(table):
    pairs = []
    for y in range(2):
        for x in range(2):
            for (z, c), (z2, c2) in table.items():
                if x == 1:
                    z, c, z2, c2 = 3 - z, 1 - c, 3 - z2, 1 - c2
                pairs.append((((z * 2 + y) * 2 + x) * 2 + c, ((z2 * 2 + y) * 2 + x) * 2 + c2))
    return sorted(pairs)


HOP_1 = {(2, 0): (1, 0), (3, 1): (2, 1), (0, 0): (2, 0), (1, 1): (0, 1)}
HOP_2 = {(3, 1): (1, 1), (2, 0): (3, 0), (1, 1): (2, 1), (0, 0): (1, 0)}
HOP_3 = {(1, 0): (0, 0), (1, 1): (0, 1), (2, 0): (3, 0), (2, 1): (3, 1)}


def routed(head_out, out_weight, ctx_index, head_index):
    both = ("ctx", "head")
    z, y, x, core = ctx_index // 2, ctx_index % 2, head_index // 2, head_index % 2
    far = jnp.where(x == 0, z, 3 - z)
    lane = jnp.where(x == 0, core, 1 - core)
    swap_core = [(i, i ^ 1) for i in range(4)]
    swap_x = [(i, i ^ 2) for i in range(4)]
    swap_y = [(i, i ^ 1) for i in range(8)]
    weight = jnp.concatenate([out_weight, lax.ppermute(out_weight, "head", swap_core)], axis=0)
    block = jnp.concatenate([head_out, lax.ppermute(head_out, "head", swap_core)], axis=1)
    hop_1 = lax.ppermute(block, both, route(HOP_1))
    hop_2 = lax.ppermute(block, both, route(HOP_2))
    inner = jnp.where(lane == 0, hop_1, hop_2)
    hop_3 = lax.ppermute(inner, both, route(HOP_3))
    early = jnp.where(z % 2 == core, block, jnp.where(far % 2 == 0, hop_1, hop_2))
    late = jnp.where((far == 1) | (far == 2), inner, hop_3)
    first = far >= 2
    sent = jnp.where(first, early, late)
    kept = jnp.where(first, late, early)
    sent_y = lax.ppermute(sent, "ctx", swap_y)
    kept_y = lax.ppermute(kept, "ctx", swap_y)

    def project(rows):
        return jnp.dot(rows, weight, preferred_element_type=jnp.float32)

    come = lax.ppermute(project(sent).astype(jnp.bfloat16), "head", swap_x)
    come_y = lax.ppermute(project(sent_y).astype(jnp.bfloat16), "head", swap_x)
    rows = block.shape[0]
    own = (project(kept) + come.astype(jnp.float32)).astype(jnp.bfloat16)
    own_y = (project(kept_y) + come_y.astype(jnp.float32)).astype(jnp.bfloat16)
    out = jnp.zeros((2 * rows, out_weight.shape[1]), jnp.bfloat16)
    out = lax.dynamic_update_slice(out, own, (y * rows, 0))
    return lax.dynamic_update_slice(out, own_y, ((1 - y) * rows, 0))


def collected(head_out, out_weight):
    rows = lax.all_gather(head_out, "ctx", axis=0, tiled=True)
    partial_terms = jnp.dot(rows, out_weight, preferred_element_type=jnp.float32)
    return lax.psum_scatter(
        partial_terms.astype(jnp.bfloat16), "head", scatter_dimension=0, tiled=True
    )


def per_device(
    ctx_size,
    head_size,
    queries,
    key_states,
    value_states,
    vertical_blocks,
    slash_offsets,
    positions,
    out_weight,
):
    local_heads = queries.shape[1] // HD
    head_index = lax.axis_index("head")
    ctx_index = lax.axis_index("ctx")
    core = head_index % 2
    shared_head = head_index * local_heads // GROUP
    cosine, sine = rotation_tables(positions)
    piece = pack_keys(core, shared_head, key_states, value_states, cosine, sine)
    pieces = [piece] + [
        lax.ppermute(piece, "ctx", [(i, i ^ d) for i in range(ctx_size)])
        for d in range(1, ctx_size)
    ]
    own = jnp.concatenate(pieces, axis=0)
    other = lax.ppermute(own, "head", [(i, i ^ 1) for i in range(head_size)])
    head_out = attend(
        ctx_index, core, vertical_blocks, slash_offsets, queries, cosine, sine, own, other
    )
    if (ctx_size, head_size) == (8, 4):
        return routed(head_out, out_weight, ctx_index, head_index)
    return collected(head_out, out_weight)


def solution(mesh):
    placed = (
        P("ctx", "head"),
        P("ctx", None),
        P("ctx", None),
        P("head", None),
        P("head", None),
        P("ctx"),
        P("head", "ctx"),
    )
    return jax.shard_map(
        functools.partial(per_device, mesh.shape["ctx"], mesh.shape["head"]),
        mesh=mesh,
        in_specs=placed,
        out_specs=P("head", "ctx"),
        check_vma=False,
    )
```

time: 264 us -> 158 us (0.60)
  blocking collectives: 64.3 us -> 0 us
  waiting for transfers between devices: 145 us -> 87.2 us
  starting transfers between devices: 0.22 us -> 21.9 us
  Pallas kernels: 0 us -> 14.4 us
  between operations: 13.6 us -> 0.35 us
  matrix products: 21.8 us -> 16.5 us
  other arithmetic: 9.18 us -> 6.03 us
    ppermute x0 -> x17, waiting for transfers between devices: none -> 87.2 us  [the longest x1 21.8 us: routed(): hop_3 = lax.ppermute(inner, both, route(HOP_3))]
    all_gather x1 -> x0, waiting for transfers between devices: 74.5 us -> none  [per_device(): lax.all_gather(head_out, 'ctx', axis=0, tiled=True)]
    reduce_scatter x1 -> x0, waiting for transfers between devices: 70.1 us -> none  [per_device(): lax.psum_scatter(partial_terms.astype(jnp.bfloat16), 'head', scatter_dime...]
    all_gather x2 -> x0, blocking collectives: 64.3 us -> none  [the longest x1 33 us: per_device(): lax.all_gather(rotated_own, 'ctx', axis=0, tiled=True)]
    ppermute x0 -> x17, starting transfers between devices: none -> 21.9 us  [the longest x7 12.5 us: per_device(): lax.ppermute(piece, 'ctx', [(i, i ^ d) for i in range(ctx_size)])]
    pallas_call x0 -> x2, Pallas kernels: none -> 14.4 us  [the longest x1 12.6 us: attend(): pl.pallas_call(attention_kernel, grid_spec=pltpu.PrefetchScalarGridSpec(n...]
    unnamed x11 -> x32, local copies, waits for them, and re-layouts: 1.49 us -> 8.06 us
    gather x2 -> x0, local copies, waits for them, and re-layouts: 6.08 us -> none  [the longest x1 3.06 us: per_device(): key_tiles = all_keys.reshape(key_count, BLK, HD)[safe_blocks]]
  transfers between devices with their start and end apart: 2 -> 17, of which waited for: 2 -> 10; matrix products, arithmetic and copies ran while one was open for 0% -> 16% of each run, Pallas kernels for 0% -> 8%
where the time goes in v1:
time: 158 us; the launch traced here: 157 us
  waiting for transfers between devices  87.2 us (55%)
  starting transfers between devices  21.9 us (14%)
  matrix products  16.5 us (10%)
  Pallas kernels  14.4 us (9%)
  local copies, waits for them, and re-layouts  10.8 us (7%)
  other arithmetic  6.03 us (4%)
    ppermute x1, waiting for transfers between devices, routed(): hop_3 = lax.ppermute(inner, both, route(HOP_3))  21.8 us
    ppermute x1, waiting for transfers between devices, routed(): sent_y = lax.ppermute(sent, 'ctx', swap_y)  17.5 us
    dot_general x4, matrix products, project(): return jnp.dot(rows, weight, preferred_element_type=jnp.float32)  16.5 us
    pallas_call x1, Pallas kernels, attend(): pl.pallas_call(attention_kernel, grid_spec=pltpu.PrefetchScalarGridSpec(n...  12.6 us
    ppermute x7, starting transfers between devices, per_device(): lax.ppermute(piece, 'ctx', [(i, i ^ d) for i in range(ctx_size)])  12.5 us
    ppermute x1, waiting for transfers between devices, routed(): hop_2 = lax.ppermute(block, both, route(HOP_2))  11.2 us
    ppermute x1, waiting for transfers between devices, routed(): hop_1 = lax.ppermute(block, both, route(HOP_1))  10.9 us
    unnamed x32, local copies, waits for them, and re-layouts  8.06 us
  transfers between devices with their start and end apart: 17, of which 10 were waited for; matrix products, arithmetic and copies ran while one was open for 16% of the time, Pallas kernels for 8%

profile of v1, /device:TPU:0, one launch (start us, length us, event | category | flops | bytes accessed | tf_op | source)
XLA Modules:
  0.0 157.2 jit_solution(6315532878242259636)
XLA Ops:
  0.0 0.7 convert_element_type.21
  0.7 0.5 fusion.4
  1.3 0.6 pad_add_fusion.1.place
  1.9 0.9 pad_maximum_fusion.1
  2.7 1.8 %pack_keys.1 = bf16[128,256]{1,0:T(8,128)(2,1)} custom-call(s32[2]{0:T(128)} %pad_add_fusion.1.place, bf16[256,256]{1,0:T(8,128)(2,1)} %keys.1, bf16[256,256]{1,0:T(8,128)(2,1)} %values.1, f32[256,128]{1,0:T(8,128)} %get-tuple-element.10.cosine, f32[256,128]{1,0:T(8,128)} %get-tuple-element.11.sine), custom_call_target="tpu_custom_call" | custom-call | tf_op jit(solution)/shard_map/pack_keys/pallas_call | solution.py:111
  4.6 3.0 %collective-permute-start = (bf16[128,256]{1,0:T(8,128)(2,1)}, bf16[128,256]{1,0:T(8,128)(2,1)S(1)}, u32[]{:S(2)}, u32[]{:S(2)}) collective-permute-start(bf16[128,256]{1,0:T(8,128)(2,1)} %pack_keys.1), channel_id=1, source_target_pairs={{0,4},{4,0},{8,12},{12,8},{16,20},{20,16},{24,28},{28,24},{1,5},{5... | collective-permute-start | bytes 196616 | tf_op jit(solution)/shard_map/ppermute | solution.py:198
  7.5 1.6 %collective-permute-start.1 = (bf16[128,256]{1,0:T(8,128)(2,1)}, bf16[128,256]{1,0:T(8,128)(2,1)S(1)}, u32[]{:S(2)}, u32[]{:S(2)}) collective-permute-start(bf16[128,256]{1,0:T(8,128)(2,1)} %pack_keys.1), channel_id=1, source_target_pairs={{0,8},{4,12},{8,0},{12,4},{16,24},{20,28},{24,16},{28,20},{1,9},{5... | collective-permute-start | bytes 196616 | tf_op jit(solution)/shard_map/ppermute | solution.py:198
  9.1 3.0 %collective-permute-start.3 = (bf16[128,256]{1,0:T(8,128)(2,1)}, bf16[128,256]{1,0:T(8,128)(2,1)S(1)}, u32[]{:S(2)}, u32[]{:S(2)}) collective-permute-start(bf16[128,256]{1,0:T(8,128)(2,1)} %pack_keys.1), channel_id=1, source_target_pairs={{0,16},{4,20},{8,24},{12,28},{16,0},{20,4},{24,8},{28,12},{1,17},{... | collective-permute-start | bytes 196616 | tf_op jit(solution)/shard_map/ppermute | solution.py:198
  12.1 1.3 collective-permute-start.4
  13.4 0.9 constant_dynamic-update-slice_fusion.7
  14.3 3.6 %collective-permute-start.5 = (bf16[128,256]{1,0:T(8,128)(2,1)}, bf16[128,256]{1,0:T(8,128)(2,1)S(1)}, u32[]{:S(2)}, u32[]{:S(2)}) collective-permute-start(bf16[128,256]{1,0:T(8,128)(2,1)} %pack_keys.1), channel_id=1, source_target_pairs={{0,24},{4,28},{8,16},{12,20},{16,8},{20,12},{24,0},{28,4},{1,25},{... | collective-permute-start | bytes 196616 | tf_op jit(solution)/shard_map/ppermute | solution.py:198
  17.9 0.1 collective-permute-start.6
  18.0 4.5 %collective-permute-done.4 = bf16[128,256]{1,0:T(8,128)(2,1)S(1)} collective-permute-done((bf16[128,256]{1,0:T(8,128)(2,1)}, bf16[128,256]{1,0:T(8,128)(2,1)S(1)}, u32[]{:S(2)}, u32[]{:S(2)}) %collective-permute-start.4) | collective-permute-done | bytes 65568 | tf_op jit(solution)/shard_map/ppermute | solution.py:198
  22.5 2.7 %collective-permute-done.6 = bf16[128,256]{1,0:T(8,128)(2,1)S(1)} collective-permute-done((bf16[128,256]{1,0:T(8,128)(2,1)}, bf16[128,256]{1,0:T(8,128)(2,1)S(1)}, u32[]{:S(2)}, u32[]{:S(2)}) %collective-permute-start.6) | collective-permute-done | bytes 65568 | tf_op jit(solution)/shard_map/ppermute | solution.py:198
  25.2 0.1 collective-permute-start.7
  25.3 0.5 collective-permute-start.12
  25.8 1.3 copy.8.vertical
  27.1 1.3 copy.9.slash
  28.5 0.6 pad_add_fusion.place
  29.1 0.8 copy-done.8
  29.9 12.6 %attention.1 = bf16[256,1024]{1,0:T(8,128)(2,1)} custom-call(s32[2]{0:T(128)} %pad_add_fusion.place, s32[8,4]{1,0:T(8,128)} %copy.8.vertical, s32[8,4]{1,0:T(8,128)} %copy.9.slash, bf16[256,1024]{1,0:T(8,128)(2,1)} %queries.1, f32[256,128]{1,0:T(8,128)} %get-tuple-element.10.cosine, f32[256,128]{1,0:T(8,128)} %get-tuple-element.11.sine, ...), custom_call_target="tpu_custom_call" | custom-call | tf_op jit(solution)/shard_map/attention/pallas_call | solution.py:90
  42.5 0.1 collective-permute-start.8
  42.6 2.0 %collective-permute-done.8 = bf16[256,1024]{1,0:T(8,128)(2,1)S(1)} collective-permute-done((bf16[256,1024]{1,0:T(8,128)(2,1)}, bf16[256,1024]{1,0:T(8,128)(2,1)S(1)}, u32[]{:S(2)}, u32[]{:S(2)}) %collective-permute-start.8) | collective-permute-done | bytes 524320 | tf_op jit(solution)/shard_map/ppermute | solution.py:145
  44.7 1.3 pad_maximum_fusion
  46.0 3.8 %collective-permute-start.9 = (bf16[256,2048]{1,0:T(8,128)(2,1)S(1)}, bf16[256,2048]{1,0:T(8,128)(2,1)S(1)}, u32[]{:S(2)}, u32[]{:S(2)}) collective-permute-start(bf16[256,2048]{1,0:T(8,128)(2,1)S(1)} %pad_maximum_fusion), channel_id=1, source_target_pairs={{0,16},{2,10},{4,20},{6,14},{9,1},{11,19},{13,5},{15,23},{16,8},{1... | collective-permute-start | bytes 3145736 | tf_op jit(solution)/shard_map/ppermute | solution.py:146
  49.8 1.4 collective-permute-start.10
  51.1 10.9 %collective-permute-done.9 = bf16[256,2048]{1,0:T(8,128)(2,1)S(1)} collective-permute-done((bf16[256,2048]{1,0:T(8,128)(2,1)S(1)}, bf16[256,2048]{1,0:T(8,128)(2,1)S(1)}, u32[]{:S(2)}, u32[]{:S(2)}) %collective-permute-start.9) | collective-permute-done | bytes 1048608 | tf_op jit(solution)/shard_map/ppermute | solution.py:146
  62.0 11.2 %collective-permute-done.10 = bf16[256,2048]{1,0:T(8,128)(2,1)S(1)} collective-permute-done((bf16[256,2048]{1,0:T(8,128)(2,1)S(1)}, bf16[256,2048]{1,0:T(8,128)(2,1)S(1)}, u32[]{:S(2)}, u32[]{:S(2)}) %collective-permute-start.10) | collective-permute-done | bytes 1048608 | tf_op jit(solution)/shard_map/ppermute | solution.py:147
  73.3 1.0 copy-done.1
  74.2 0.1 broadcast_select_fusion
  74.3 1.5 collective-permute-start.11
  75.9 0.0 copy-start.2
  75.9 2.6 %constant_dynamic-update-slice_fusion.9 = bf16[2048,2048]{1,0:T(8,128)(2,1)S(1)} fusion(bf16[1024,2048]{1,0:T(8,128)(2,1)} %param.13), kind=kLoop, calls=%fused_computation.28 | loop fusion | bytes 8388608
  78.6 21.8 %collective-permute-done.11 = bf16[256,2048]{1,0:T(8,128)(2,1)S(1)} collective-permute-done((bf16[256,2048]{1,0:T(8,128)(2,1)S(1)}, bf16[256,2048]{1,0:T(8,128)(2,1)S(1)}, u32[]{:S(2)}, u32[]{:S(2)}) %collective-permute-start.11) | collective-permute-done | bytes 1048608 | tf_op jit(solution)/shard_map/ppermute | solution.py:149
  100.4 1.0 broadcast_select_fusion.2
  101.5 0.6 collective-permute-start.15
  102.0 2.5 %constant_dynamic-update-slice_fusion.8 = bf16[2048,2048]{1,0:T(8,128)(2,1)S(1)} fusion(bf16[2048,2048]{1,0:T(8,128)(2,1)S(1)} %constant_dynamic-update-slice_fusion.9, bf16[1024,2048]{1,0:T(8,128)(2,1)} %collective-permute-done.12), kind=kLoop, calls=%fused_computation.27 | loop fusion | bytes 8388608 | tf_op jit(solution)/shard_map/concatenate | solution.py:144
  104.5 3.7 %convolution_convert_fusion.1 = bf16[256,2048]{1,0:T(8,128)(2,1)} fusion(bf16[256,2048]{1,0:T(8,128)(2,1)S(1)} %get-tuple-element.5, bf16[2048,2048]{1,0:T(8,128)(2,1)S(1)} %constant_dynamic-update-slice_fusion.8), kind=kOutput, calls=%fused_computation.7 | convolution fusion | flops 2148007936 | bytes 10485760 | tf_op jit(solution)/shard_map/dot_general | solution.py:159
  108.3 0.3 broadcast_select_fusion.3
  108.5 1.6 %collective-permute-start.14 = (bf16[256,2048]{1,0:T(8,128)(2,1)S(1)}, bf16[256,2048]{1,0:T(8,128)(2,1)S(1)}, u32[]{:S(2)}, u32[]{:S(2)}) collective-permute-start(bf16[256,2048]{1,0:T(8,128)(2,1)S(1)} %broadcast_select_fusion.3), channel_id=1, source_target_pairs={{0,4},{4,0},{8,12},{12,8},{16,20},{20,16},{24,28},{28,24},{1,5},{5... | collective-permute-start | bytes 3145736 | tf_op jit(solution)/shard_map/ppermute | solution.py:156
  110.1 17.5 %collective-permute-done.15 = bf16[256,2048]{1,0:T(8,128)(2,1)S(1)} collective-permute-done((bf16[256,2048]{1,0:T(8,128)(2,1)S(1)}, bf16[256,2048]{1,0:T(8,128)(2,1)S(1)}, u32[]{:S(2)}, u32[]{:S(2)}) %collective-permute-start.15) | collective-permute-done | bytes 1048608 | tf_op jit(solution)/shard_map/ppermute | solution.py:155
  127.6 3.4 %convolution_convert_fusion = bf16[256,2048]{1,0:T(8,128)(2,1)} fusion(bf16[256,2048]{1,0:T(8,128)(2,1)S(1)} %collective-permute-done.15, bf16[2048,2048]{1,0:T(8,128)(2,1)S(1)} %constant_dynamic-update-slice_fusion.8), kind=kOutput, calls=%fused_computation.6 | convolution fusion | flops 2148007936 | bytes 10485760 | tf_op jit(solution)/shard_map/dot_general | solution.py:159
  131.0 3.5 %collective-permute-done.13 = bf16[256,2048]{1,0:T(8,128)(2,1)} collective-permute-done((bf16[256,2048]{1,0:T(8,128)(2,1)}, bf16[256,2048]{1,0:T(8,128)(2,1)}, u32[]{:S(2)}, u32[]{:S(2)}) %collective-permute-start.13) | collective-permute-done | bytes 1048608 | tf_op jit(solution)/shard_map/ppermute | solution.py:161
  134.5 0.2 broadcast_in_dim.2
  134.8 6.1 %fusion.1 = bf16[512,2048]{1,0:T(8,128)(2,1)S(1)} fusion(bf16[512,2048]{1,0:T(8,128)(2,1)S(1)} %broadcast_in_dim.2, s32[]{:T(128)S(6)} %select_n.99, bf16[256,2048]{1,0:T(8,128)(2,1)S(1)} %broadcast_select_fusion.3, bf16[2048,2048]{1,0:T(8,128)(2,1)} %copy-done.4, bf16[256,2048]{1,0:T(8,128)(2,1)} %collective-permute-done.13), kind=kOutput, calls=%fused_computation.3 | convolution fusion | flops 2149056512 | bytes 11534340 | tf_op jit(solution)/shard_map/dot_general | solution.py:159
  140.9 6.3 %collective-permute-done.14 = bf16[256,2048]{1,0:T(8,128)(2,1)S(1)} collective-permute-done((bf16[256,2048]{1,0:T(8,128)(2,1)S(1)}, bf16[256,2048]{1,0:T(8,128)(2,1)S(1)}, u32[]{:S(2)}, u32[]{:S(2)}) %collective-permute-start.14) | collective-permute-done | bytes 1048608 | tf_op jit(solution)/shard_map/ppermute | solution.py:156
  147.2 6.6 %collective-permute-done.16 = bf16[256,2048]{1,0:T(8,128)(2,1)S(1)} collective-permute-done((bf16[256,2048]{1,0:T(8,128)(2,1)}, bf16[256,2048]{1,0:T(8,128)(2,1)S(1)}, u32[]{:S(2)}, u32[]{:S(2)}) %collective-permute-start.16) | collective-permute-done | bytes 1048608 | tf_op jit(solution)/shard_map/ppermute | solution.py:162
  153.9 3.3 %fusion.3 = bf16[512,2048]{1,0:T(8,128)(2,1)} fusion(bf16[512,2048]{1,0:T(8,128)(2,1)} %copy-done.3, s32[]{:T(128)S(6)} %select_n.100, bf16[256,2048]{1,0:T(8,128)(2,1)S(1)} %collective-permute-done.14, bf16[2048,2048]{1,0:T(8,128)(2,1)S(1)} %bitcast.12, bf16[256,2048]{1,0:T(8,128)(2,1)S(1)} %collective-permute-done.16), kind=kOutput, calls=%fused_computation.5 | convolution fusion | flops 2149056512 | bytes 11534340 | tf_op jit(solution)/shard_map/dot_general | solution.py:159
  (38 shorter events, 0.1 us)
Async XLA Ops:
  4.6 9.7 %collective-permute-start = (bf16[128,256]{1,0:T(8,128)(2,1)}, bf16[128,256]{1,0:T(8,128)(2,1)S(1)}, u32[]{:S(2)}, u32[]{:S(2)}) collective-permute-start(bf16[128,256]{1,0:T(8,128)(2,1)} %pack_keys.1), channel_id=1, source_target_pairs={{0,4},{4,0},{8,12},{12,8},{16,20},{20,16},{24,28},{28,24},{1,5},{5... | collective-permute-start | bytes 196616 | tf_op jit(solution)/shard_map/ppermute | solution.py:198
  7.5 10.3 %collective-permute-start.1 = (bf16[128,256]{1,0:T(8,128)(2,1)}, bf16[128,256]{1,0:T(8,128)(2,1)S(1)}, u32[]{:S(2)}, u32[]{:S(2)}) collective-permute-start(bf16[128,256]{1,0:T(8,128)(2,1)} %pack_keys.1), channel_id=1, source_target_pairs={{0,8},{4,12},{8,0},{12,4},{16,24},{20,28},{24,16},{28,20},{1,9},{5... | collective-permute-start | bytes 196616 | tf_op jit(solution)/shard_map/ppermute | solution.py:198
  9.1 8.9 %collective-permute-start.2 = (bf16[128,256]{1,0:T(8,128)(2,1)}, bf16[128,256]{1,0:T(8,128)(2,1)S(1)}, u32[]{:S(2)}, u32[]{:S(2)}) collective-permute-start(bf16[128,256]{1,0:T(8,128)(2,1)} %pack_keys.1), channel_id=1, source_target_pairs={{0,12},{4,8},{8,4},{12,0},{16,28},{20,24},{24,20},{28,16},{1,13},{... | collective-permute-start | bytes 196616 | tf_op jit(solution)/shard_map/ppermute | solution.py:198
  9.1 8.9 %collective-permute-start.3 = (bf16[128,256]{1,0:T(8,128)(2,1)}, bf16[128,256]{1,0:T(8,128)(2,1)S(1)}, u32[]{:S(2)}, u32[]{:S(2)}) collective-permute-start(bf16[128,256]{1,0:T(8,128)(2,1)} %pack_keys.1), channel_id=1, source_target_pairs={{0,16},{4,20},{8,24},{12,28},{16,0},{20,4},{24,8},{28,12},{1,17},{... | collective-permute-start | bytes 196616 | tf_op jit(solution)/shard_map/ppermute | solution.py:198
  12.1 10.4 %collective-permute-start.4 = (bf16[128,256]{1,0:T(8,128)(2,1)}, bf16[128,256]{1,0:T(8,128)(2,1)S(1)}, u32[]{:S(2)}, u32[]{:S(2)}) collective-permute-start(bf16[128,256]{1,0:T(8,128)(2,1)} %pack_keys.1), channel_id=1, source_target_pairs={{0,20},{4,16},{8,28},{12,24},{16,4},{20,0},{24,12},{28,8},{1,21},{... | collective-permute-start | bytes 196616 | tf_op jit(solution)/shard_map/ppermute | solution.py:198
  14.3 8.3 %collective-permute-start.5 = (bf16[128,256]{1,0:T(8,128)(2,1)}, bf16[128,256]{1,0:T(8,128)(2,1)S(1)}, u32[]{:S(2)}, u32[]{:S(2)}) collective-permute-start(bf16[128,256]{1,0:T(8,128)(2,1)} %pack_keys.1), channel_id=1, source_target_pairs={{0,24},{4,28},{8,16},{12,20},{16,8},{20,12},{24,0},{28,4},{1,25},{... | collective-permute-start | bytes 196616 | tf_op jit(solution)/shard_map/ppermute | solution.py:198
  17.9 7.3 %collective-permute-start.6 = (bf16[128,256]{1,0:T(8,128)(2,1)}, bf16[128,256]{1,0:T(8,128)(2,1)S(1)}, u32[]{:S(2)}, u32[]{:S(2)}) collective-permute-start(bf16[128,256]{1,0:T(8,128)(2,1)} %pack_keys.1), channel_id=1, source_target_pairs={{0,28},{4,24},{8,20},{12,16},{16,12},{20,8},{24,4},{28,0},{1,29},{... | collective-permute-start | bytes 196616 | tf_op jit(solution)/shard_map/ppermute | solution.py:198
  25.2 3.9 %copy-start.7 = (bf16[1024,256]{1,0:T(8,128)(2,1)}, bf16[1024,256]{1,0:T(8,128)(2,1)S(1)}, u32[]{:S(2)}) copy-start(bf16[1024,256]{1,0:T(8,128)(2,1)S(1)} %constant_dynamic-update-slice_fusion.own) | copy-start | bytes 1572868
  25.2 3.9 %collective-permute-start.7 = (bf16[1024,256]{1,0:T(8,128)(2,1)S(1)}, bf16[1024,256]{1,0:T(8,128)(2,1)S(1)}, u32[]{:S(2)}, u32[]{:S(2)}) collective-permute-start(bf16[1024,256]{1,0:T(8,128)(2,1)S(1)} %constant_dynamic-update-slice_fusion.own), channel_id=1, source_target_pairs={{0,1},{1,0},{2,3},{3,2},{4,5},{5,4},{6,7},{7,6},{8,9},{9,8},{10,11... | collective-permute-start | bytes 1572872 | tf_op jit(solution)/shard_map/ppermute | solution.py:202
  25.3 76.7 %collective-permute-start.12 = (bf16[1024,2048]{1,0:T(8,128)(2,1)}, bf16[1024,2048]{1,0:T(8,128)(2,1)}, u32[]{:S(2)}, u32[]{:S(2)}) collective-permute-start(bf16[1024,2048]{1,0:T(8,128)(2,1)} %param.13), channel_id=1, source_target_pairs={{0,1},{1,0},{2,3},{3,2},{4,5},{5,4},{6,7},{7,6},{8,9},{9,8},{10,11... | collective-permute-start | bytes 12582920 | tf_op jit(solution)/shard_map/ppermute | solution.py:144
  29.1 0.8 copy-start.8
  42.5 2.1 %collective-permute-start.8 = (bf16[256,1024]{1,0:T(8,128)(2,1)}, bf16[256,1024]{1,0:T(8,128)(2,1)S(1)}, u32[]{:S(2)}, u32[]{:S(2)}) collective-permute-start(bf16[256,1024]{1,0:T(8,128)(2,1)} %attention.1), channel_id=1, source_target_pairs={{0,1},{1,0},{2,3},{3,2},{4,5},{5,4},{6,7},{7,6},{8,9},{9,8},{10,11... | collective-permute-start | bytes 1572872 | tf_op jit(solution)/shard_map/ppermute | solution.py:145
  44.7 1.3 copy-start.5
  46.0 16.0 %collective-permute-start.9 = (bf16[256,2048]{1,0:T(8,128)(2,1)S(1)}, bf16[256,2048]{1,0:T(8,128)(2,1)S(1)}, u32[]{:S(2)}, u32[]{:S(2)}) collective-permute-start(bf16[256,2048]{1,0:T(8,128)(2,1)S(1)} %pad_maximum_fusion), channel_id=1, source_target_pairs={{0,16},{2,10},{4,20},{6,14},{9,1},{11,19},{13,5},{15,23},{16,8},{1... | collective-permute-start | bytes 3145736 | tf_op jit(solution)/shard_map/ppermute | solution.py:146
  49.8 23.5 %collective-permute-start.10 = (bf16[256,2048]{1,0:T(8,128)(2,1)S(1)}, bf16[256,2048]{1,0:T(8,128)(2,1)S(1)}, u32[]{:S(2)}, u32[]{:S(2)}) collective-permute-start(bf16[256,2048]{1,0:T(8,128)(2,1)S(1)} %pad_maximum_fusion), channel_id=1, source_target_pairs={{0,8},{2,18},{4,12},{6,22},{9,17},{11,3},{13,21},{15,7},{16,24},{1... | collective-permute-start | bytes 3145736 | tf_op jit(solution)/shard_map/ppermute | solution.py:147
  73.3 1.0 copy-start.1
  74.3 26.1 %collective-permute-start.11 = (bf16[256,2048]{1,0:T(8,128)(2,1)S(1)}, bf16[256,2048]{1,0:T(8,128)(2,1)S(1)}, u32[]{:S(2)}, u32[]{:S(2)}) collective-permute-start(bf16[256,2048]{1,0:T(8,128)(2,1)S(1)} %broadcast_select_fusion), channel_id=1, source_target_pairs={{8,0},{9,1},{10,2},{11,3},{12,4},{13,5},{14,6},{15,7},{16,24},{17,... | collective-permute-start | bytes 3145736 | tf_op jit(solution)/shard_map/ppermute | solution.py:149
  75.9 24.5 %copy-start = (bf16[256,1024]{1,0:T(8,128)(2,1)S(1)}, bf16[256,1024]{1,0:T(8,128)(2,1)}, u32[]{:S(2)}) copy-start(bf16[256,1024]{1,0:T(8,128)(2,1)} %attention.1) | copy-start | bytes 1572868
  75.9 24.5 %copy-start.2 = (bf16[256,2048]{1,0:T(8,128)(2,1)S(1)}, bf16[256,2048]{1,0:T(8,128)(2,1)}, u32[]{:S(2)}) copy-start(bf16[256,2048]{1,0:T(8,128)(2,1)} %copy-done.1) | copy-start | bytes 3145732
  75.9 24.5 %copy-start.6 = (bf16[256,1024]{1,0:T(8,128)(2,1)S(1)}, bf16[256,1024]{1,0:T(8,128)(2,1)}, u32[]{:S(2)}) copy-start(bf16[256,1024]{1,0:T(8,128)(2,1)} %copy-done.5) | copy-start | bytes 1572868
  101.5 26.2 %collective-permute-start.15 = (bf16[256,2048]{1,0:T(8,128)(2,1)S(1)}, bf16[256,2048]{1,0:T(8,128)(2,1)S(1)}, u32[]{:S(2)}, u32[]{:S(2)}) collective-permute-start(bf16[256,2048]{1,0:T(8,128)(2,1)S(1)} %get-tuple-element.5), channel_id=1, source_target_pairs={{0,4},{4,0},{8,12},{12,8},{16,20},{20,16},{24,28},{28,24},{1,5},{5... | collective-permute-start | bytes 3145736 | tf_op jit(solution)/shard_map/ppermute | solution.py:155
  104.5 23.1 %copy-start.4 = (bf16[2048,2048]{1,0:T(8,128)(2,1)}, bf16[2048,2048]{1,0:T(8,128)(2,1)S(1)}, u32[]{:S(2)}) copy-start(bf16[2048,2048]{1,0:T(8,128)(2,1)S(1)} %constant_dynamic-update-slice_fusion.8) | copy-start | bytes 25165828
  108.3 26.3 %collective-permute-start.13 = (bf16[256,2048]{1,0:T(8,128)(2,1)}, bf16[256,2048]{1,0:T(8,128)(2,1)}, u32[]{:S(2)}, u32[]{:S(2)}) collective-permute-start(bf16[256,2048]{1,0:T(8,128)(2,1)} %convolution_convert_fusion.1), channel_id=1, source_target_pairs={{0,2},{1,3},{2,0},{3,1},{4,6},{5,7},{6,4},{7,5},{8,10},{9,11},{10,... | collective-permute-start | bytes 3145736 | tf_op jit(solution)/shard_map/ppermute | solution.py:161
  108.5 38.7 %collective-permute-start.14 = (bf16[256,2048]{1,0:T(8,128)(2,1)S(1)}, bf16[256,2048]{1,0:T(8,128)(2,1)S(1)}, u32[]{:S(2)}, u32[]{:S(2)}) collective-permute-start(bf16[256,2048]{1,0:T(8,128)(2,1)S(1)} %broadcast_select_fusion.3), channel_id=1, source_target_pairs={{0,4},{4,0},{8,12},{12,8},{16,20},{20,16},{24,28},{28,24},{1,5},{5... | collective-permute-start | bytes 3145736 | tf_op jit(solution)/shard_map/ppermute | solution.py:156
  131.0 22.9 %collective-permute-start.16 = (bf16[256,2048]{1,0:T(8,128)(2,1)}, bf16[256,2048]{1,0:T(8,128)(2,1)S(1)}, u32[]{:S(2)}, u32[]{:S(2)}) collective-permute-start(bf16[256,2048]{1,0:T(8,128)(2,1)} %convolution_convert_fusion), channel_id=1, source_target_pairs={{0,2},{1,3},{2,0},{3,1},{4,6},{5,7},{6,4},{7,5},{8,10},{9,11},{10,... | collective-permute-start | bytes 3145736 | tf_op jit(solution)/shard_map/ppermute | solution.py:162
  134.5 19.4 %slice-start = ((s8[8388608]{0:T(1024)(128)(4,1)}), s8[4194304]{0:T(1024)(128)(4,1)S(1)}, s32[]{:S(2)}) async-start(s8[8388608]{0:T(1024)(128)(4,1)} %bitcast.11), calls=%async_computation | async-start | bytes 8388608
  134.8 19.1 %slice-start.1 = ((s8[8388608]{0:T(1024)(128)(4,1)}), s8[4194304]{0:T(1024)(128)(4,1)S(1)}, s32[]{:S(2)}) async-start(s8[8388608]{0:T(1024)(128)(4,1)} %bitcast.11), calls=%async_computation.1 | async-start | bytes 8388608
  140.9 13.0 %copy-start.3 = (bf16[512,2048]{1,0:T(8,128)(2,1)}, bf16[512,2048]{1,0:T(8,128)(2,1)S(1)}, u32[]{:S(2)}) copy-start(bf16[512,2048]{1,0:T(8,128)(2,1)S(1)} %fusion.1) | copy-start | bytes 6291460

commit v2 on v1

v2 whole, which is shorter than its diff:
```python
import functools
import math

import jax
import jax.numpy as jnp
from jax import lax
from jax.experimental import pallas as pl
from jax.experimental.pallas import tpu as pltpu
from jax.sharding import PartitionSpec as P

HD = 128
GROUP = 16
BLK = 128
NEG = -1e30
GRANT = 20 << 20
SCALE = math.log2(math.e) / math.sqrt(HD)
VMEM = pl.BlockSpec(memory_space=pltpu.VMEM)
SMEM = pl.BlockSpec(memory_space=pltpu.SMEM)


def rotation_tables(positions):
    half = HD // 2
    exponents = jnp.arange(half, dtype=jnp.float32) * (2.0 / HD)
    inverse_freq = 500000.0 ** (-exponents)
    angles = positions.astype(jnp.float32)[:, None] * inverse_freq[None, :]
    cosine, sine = jnp.cos(angles), jnp.sin(angles)
    return jnp.concatenate([cosine, cosine], axis=1), jnp.concatenate([-sine, sine], axis=1)


def rotate(states, cosine, sine):
    states = states.astype(jnp.float32)
    rotated = states * cosine + pltpu.roll(states, HD // 2, 1) * sine
    return rotated.astype(jnp.bfloat16)


def pack_kernel(place, keys, values, cosine, sine, piece):
    rows = pl.ds(pl.multiple_of(place[0] * BLK, BLK), BLK)
    lane = pl.ds(pl.multiple_of(place[1] * HD, HD), HD)
    piece[:, :HD] = rotate(keys[rows, lane], cosine[rows, :], sine[rows, :])
    piece[:, HD:] = values[rows, lane]


def pack(place, key_states, value_states, cosine, sine):
    return pl.pallas_call(
        pack_kernel,
        in_specs=[SMEM] + [VMEM] * 4,
        out_specs=VMEM,
        out_shape=jax.ShapeDtypeStruct((BLK, 2 * HD), jnp.bfloat16),
        compiler_params=pltpu.CompilerParams(vmem_limit_bytes=GRANT),
        name="pack",
    )(place, key_states, value_states, cosine, sine)


def turn_kernel(queries, cosine, sine, out):
    for head in range(queries.shape[1] // HD):
        part = (slice(None), slice(head * HD, (head + 1) * HD))
        out[part] = rotate(queries[part], cosine[...], sine[...])


def turn(queries, cosine, sine):
    return pl.pallas_call(
        turn_kernel,
        in_specs=[VMEM] * 3,
        out_specs=VMEM,
        out_shape=jax.ShapeDtypeStruct(queries.shape, jnp.bfloat16),
        compiler_params=pltpu.CompilerParams(vmem_limit_bytes=GRANT),
        name="turn",
    )(queries, cosine, sine)


def attended(table, head, verticals, slashes, block, rot, keys, values, causal):
    at = head * (verticals + slashes)
    verts = [table[at + i] for i in range(verticals)]
    slots = [(block, None)] + [(v, v < block) for v in verts]
    for j in range(1, slashes):
        u = block - table[at + verticals + j]
        valid = u >= 0
        for v in verts:
            valid = jnp.logical_and(valid, u != v)
        slots.append((jnp.maximum(u, 0), valid))
    rows = [pl.ds(pl.multiple_of(u * BLK, BLK), BLK) for u, _ in slots]
    pairs = [slice(i, i + 2) for i in range(0, len(slots), 2)]
    scores = []
    for pair in pairs:
        tile = jnp.concatenate([keys[r, :] for r in rows[pair]], axis=0)
        both = lax.dot_general(
            rot, tile, (((1,), (1,)), ((), ())), preferred_element_type=jnp.float32
        )
        for i, (_, valid) in enumerate(slots[pair]):
            s = both[:, i * BLK : (i + 1) * BLK]
            scores.append(
                jnp.where(causal, s, NEG) if valid is None else s + jnp.where(valid, 0.0, NEG)
            )
    top = jnp.max(functools.reduce(jnp.maximum, scores), axis=1, keepdims=True)
    weights = [jnp.exp2((s - top) * SCALE).astype(jnp.bfloat16) for s in scores]
    total = None
    for pair in pairs:
        tile = jnp.concatenate([values[r, :] for r in rows[pair]], axis=0)
        part = jnp.dot(
            jnp.concatenate(weights[pair], axis=1), tile, preferred_element_type=jnp.float32
        )
        total = part if total is None else total + part
    return (total[:, :HD] / total[:, HD:]).astype(jnp.bfloat16)


def attention_kernel(shape, table, queries, own, other, *refs):
    verticals, slashes, at, step = shape
    *outs, keys, values = refs
    ctx, core = table[at], table[at + 1]

    @pl.when(pl.program_id(0) == 0)
    def _():
        for d in range(own.shape[0] // BLK):
            for ref, parity in ((own, core), (other, 1 - core)):
                rows = pl.ds(pl.multiple_of(((ctx ^ d) * 2 + parity) * BLK, BLK), BLK)
                keys[rows, :] = ref[d * BLK : (d + 1) * BLK, :HD]
                values[rows, :HD] = ref[d * BLK : (d + 1) * BLK, HD:]
        values[:, HD:] = jnp.ones((values.shape[0], HD), values.dtype)

    causal = lax.broadcasted_iota(jnp.int32, (BLK, BLK), 1) <= lax.broadcasted_iota(
        jnp.int32, (BLK, BLK), 0
    )
    for i in range(step):
        head = pl.program_id(0) * step + i
        lanes = slice(i * HD, (i + 1) * HD)
        for local, out in enumerate(outs):
            rot = queries[local * BLK : (local + 1) * BLK, lanes]
            index = ctx * len(outs) + local
            out[:, lanes] = attended(
                table, head, verticals, slashes, index, rot, keys, values, causal
            )


def attend(table, at, verticals, slashes, queries, own, other):
    tokens, width = queries.shape
    step = 4
    whole = lambda a: pl.BlockSpec(a.shape, lambda h, _: (0, 0))
    part = lambda rows: pl.BlockSpec((rows, step * HD), lambda h, _: (0, h))
    blocks = tokens // BLK
    keys = 2 * own.shape[0]
    return pl.pallas_call(
        functools.partial(attention_kernel, (verticals, slashes, at, step)),
        grid_spec=pltpu.PrefetchScalarGridSpec(
            num_scalar_prefetch=1,
            grid=(width // (step * HD),),
            in_specs=[part(tokens), whole(own), whole(other)],
            out_specs=[part(BLK)] * blocks,
            scratch_shapes=[
                pltpu.VMEM((keys, HD), jnp.bfloat16),
                pltpu.VMEM((keys, 2 * HD), jnp.bfloat16),
            ],
        ),
        out_shape=[jax.ShapeDtypeStruct((BLK, width), jnp.bfloat16)] * blocks,
        compiler_params=pltpu.CompilerParams(vmem_limit_bytes=GRANT),
        name="attention",
    )(table, queries, own, other)


def project_kernel(rows, own, other, out):
    depth, tile = own.shape[0], 512
    first, second = rows[:, :depth], rows[:, depth:]
    for j in range(0, own.shape[1], tile):
        part = slice(j, j + tile)
        total = jnp.dot(first, own[:, part], preferred_element_type=jnp.float32)
        total += jnp.dot(second, other[:, part], preferred_element_type=jnp.float32)
        out[:, part] = total.astype(out.dtype)


def project(rows, own, other, kind):
    count, depth = rows.shape
    width = own.shape[1]
    return pl.pallas_call(
        project_kernel,
        in_specs=[VMEM] * 3,
        out_specs=VMEM,
        out_shape=jax.ShapeDtypeStruct((count, width), kind),
        compiler_params=pltpu.CompilerParams(vmem_limit_bytes=GRANT),
        cost_estimate=pl.CostEstimate(
            flops=2 * count * depth * width,
            bytes_accessed=2 * (count * depth + count * width),
            transcendentals=0,
        ),
        name="project",
    )(rows, own, other)


def route(table):
    pairs = []
    for y in range(2):
        for x in range(2):
            for (z, c), (z2, c2) in table.items():
                if x == 1:
                    z, c, z2, c2 = 3 - z, 1 - c, 3 - z2, 1 - c2
                pairs.append((((z * 2 + y) * 2 + x) * 2 + c, ((z2 * 2 + y) * 2 + x) * 2 + c2))
    return sorted(pairs)


HOP_1 = {(2, 0): (1, 0), (3, 1): (2, 1), (0, 0): (2, 0), (1, 1): (0, 1)}
HOP_2 = {(3, 1): (1, 1), (2, 0): (3, 0), (1, 1): (2, 1), (0, 0): (1, 0)}
HOP_3 = {(1, 0): (0, 0), (1, 1): (0, 1), (2, 0): (3, 0), (2, 1): (3, 1)}


def routed(halves, out_weight, ctx_index, head_index):
    both = ("ctx", "head")
    z, y, x, core = ctx_index // 2, ctx_index % 2, head_index // 2, head_index % 2
    far = jnp.where(x == 0, z, 3 - z)
    lane = jnp.where(x == 0, core, 1 - core)
    swap_core = [(i, i ^ 1) for i in range(4)]
    swap_x = [(i, i ^ 2) for i in range(4)]
    swap_y = [(i, i ^ 1) for i in range(8)]
    weights = [
        pltpu.with_memory_space_constraint(w, pltpu.VMEM)
        for w in (out_weight, lax.ppermute(out_weight, "head", swap_core))
    ]
    home, inner, first = z % 2 == core, (far == 1) | (far == 2), far >= 2

    sent, kept = [], []
    for half in halves:
        block = jnp.concatenate([half, lax.ppermute(half, "head", swap_core)], axis=1)
        hop_1 = lax.ppermute(block, both, route(HOP_1))
        hop_2 = lax.ppermute(block, both, route(HOP_2))
        passed = jnp.where(lane == 0, hop_1, hop_2)
        hop_3 = lax.ppermute(passed, both, route(HOP_3))
        early = jnp.where(home, block, jnp.where(lane == 0, hop_2, hop_1))
        late = jnp.where(inner, passed, hop_3)
        sent.append(jnp.where(first, early, late))
        kept.append(jnp.where(first, late, early))
    sent += [lax.ppermute(rows, "ctx", swap_y) for rows in sent]
    kept += [lax.ppermute(rows, "ctx", swap_y) for rows in kept]
    parts = [project(rows, *weights, jnp.bfloat16) for rows in sent]
    come = [lax.ppermute(part, "head", swap_x) for part in parts]
    kept, parts = lax.optimization_barrier((kept, parts))
    own = [project(rows, *weights, jnp.float32) for rows in kept]
    rows = BLK * len(halves)
    out = jnp.zeros((2 * rows, out_weight.shape[1]), jnp.bfloat16)
    for i, (mine, theirs) in enumerate(zip(own, come)):
        total = (mine + theirs.astype(jnp.float32)).astype(jnp.bfloat16)
        local, other_y = i % len(halves), i // len(halves)
        at = jnp.where(other_y == 0, y, 1 - y) * rows + local * BLK
        out = lax.dynamic_update_slice(out, total, (at, 0))
    return out


def collected(head_out, out_weight):
    rows = lax.all_gather(head_out, "ctx", axis=0, tiled=True)
    partial_terms = jnp.dot(rows, out_weight, preferred_element_type=jnp.float32)
    return lax.psum_scatter(
        partial_terms.astype(jnp.bfloat16), "head", scatter_dimension=0, tiled=True
    )


def per_device(
    ctx_size,
    head_size,
    queries,
    key_states,
    value_states,
    vertical_blocks,
    slash_offsets,
    positions,
    out_weight,
):
    local_heads = queries.shape[1] // HD
    head_index = lax.axis_index("head")
    ctx_index = lax.axis_index("ctx")
    core = head_index % 2
    shared_head = head_index * local_heads // GROUP
    counts = (vertical_blocks.shape[1], slash_offsets.shape[1])
    swap_core = [(i, i ^ 1) for i in range(head_size)]
    table = jnp.concatenate([vertical_blocks, slash_offsets], axis=1).reshape(-1)
    at = table.shape[0]
    table = jnp.concatenate([table, jnp.stack([ctx_index, core])])
    cosine, sine = rotation_tables(positions)
    piece = pack(jnp.stack([core, shared_head]), key_states, value_states, cosine, sine)
    pieces = [piece] + [
        lax.ppermute(piece, "ctx", [(i, i ^ d) for i in range(ctx_size)])
        for d in range(1, ctx_size)
    ]
    rotated = turn(queries, cosine, sine)
    own, rotated, table = lax.optimization_barrier(
        (jnp.concatenate(pieces, axis=0), rotated, table)
    )
    other = lax.ppermute(own, "head", swap_core)
    halves = attend(table, at, *counts, rotated, own, other)
    if (ctx_size, head_size) == (8, 4):
        return routed(halves, out_weight, ctx_index, head_index)
    return collected(jnp.concatenate(halves, axis=0), out_weight)


def solution(mesh):
    placed = (
        P("ctx", "head"),
        P("ctx", None),
        P("ctx", None),
        P("head", None),
        P("head", None),
        P("ctx"),
        P("head", "ctx"),
    )
    return jax.shard_map(
        functools.partial(per_device, mesh.shape["ctx"], mesh.shape["head"]),
        mesh=mesh,
        in_specs=placed,
        out_specs=P("head", "ctx"),
        check_vma=False,
    )
```

time: 158 us -> 130 us (0.82)
  waiting for transfers between devices: 87.2 us -> 50.1 us
  Pallas kernels: 14.4 us -> 33 us
  matrix products: 16.5 us -> 0 us
  starting transfers between devices: 21.9 us -> 34 us
  local copies, waits for them, and re-layouts: 10.8 us -> 5.99 us
    ppermute x7 -> x13, waiting for transfers between devices: 57.9 us -> 28.2 us  [the longest x2 9.84 us: routed(): hop_3 = lax.ppermute(passed, both, route(HOP_3))]
    pallas_call x2 -> x11, Pallas kernels: 14.4 us -> 33 us  [the longest x8 27.9 us: project(): pl.pallas_call(project_kernel, in_specs=[VMEM] * 3, out_specs=VMEM, out_s...]
    dot_general x4 -> x0, matrix products: 16.5 us -> none  [project(): return jnp.dot(rows, weight, preferred_element_type=jnp.float32)]
    ppermute x7 -> x13, starting transfers between devices: 3.78 us -> 12 us  [the longest x4 4.73 us: routed(): come = [lax.ppermute(part, 'head', swap_x) for part in parts]]
    ppermute x1 -> x2, waiting for transfers between devices: 10.9 us -> 4.36 us  [routed(): hop_1 = lax.ppermute(block, both, route(HOP_1))]
    unnamed x32 -> x29, local copies, waits for them, and re-layouts: 8.06 us -> 4.8 us
    ppermute x1 -> x2, starting transfers between devices: 3.76 us -> 6.28 us  [routed(): hop_1 = lax.ppermute(block, both, route(HOP_1))]
    concatenate x2 -> x4, local copies, waits for them, and re-layouts: 2.5 us -> 0.86 us  [the longest x2 0.79 us: routed(): jnp.concatenate([half, lax.ppermute(half, 'head', swap_core)], axis=1)]
  transfers between devices with their start and end apart: 17 -> 25, of which waited for: 10 -> 14; matrix products, arithmetic and copies ran while one was open for 16% -> 4% of each run, Pallas kernels for 8% -> 25%
where the time goes in v2:
time: 130 us; the launch traced here: 129 us
  waiting for transfers between devices  50.1 us (39%)
  starting transfers between devices  34 us (26%)
  Pallas kernels  33 us (25%)
  local copies, waits for them, and re-layouts  5.99 us (5%)
  other arithmetic  5.51 us (4%)
    pallas_call x8, Pallas kernels, project(): pl.pallas_call(project_kernel, in_specs=[VMEM] * 3, out_specs=VMEM, out_s...  27.9 us
    ppermute x7, starting transfers between devices, per_device(): lax.ppermute(piece, 'ctx', [(i, i ^ d) for i in range(ctx_size)])  12.6 us
    ppermute x2, waiting for transfers between devices, routed(): hop_2 = lax.ppermute(block, both, route(HOP_2))  10.6 us
    ppermute x2, waiting for transfers between devices, routed(): hop_3 = lax.ppermute(passed, both, route(HOP_3))  9.84 us
    ppermute x2, waiting for transfers between devices, routed(): sent += [lax.ppermute(rows, 'ctx', swap_y) for rows in sent]  8.77 us
    ppermute x7, waiting for transfers between devices, per_device(): lax.ppermute(piece, 'ctx', [(i, i ^ d) for i in range(ctx_size)])  6.97 us
    ppermute x2, starting transfers between devices, routed(): hop_1 = lax.ppermute(block, both, route(HOP_1))  6.28 us
    unnamed x29, local copies, waits for them, and re-layouts  4.8 us
  transfers between devices with their start and end apart: 25, of which 14 were waited for; matrix products, arithmetic and copies ran while one was open for 4% of the time, Pallas kernels for 25%

profile of v2, /device:TPU:0, one launch (start us, length us, event | category | flops | bytes accessed | tf_op | source)
XLA Modules:
  0.0 129.2 jit_solution(16590133515912673146)
XLA Ops:
  0.0 0.7 convert_element_type.27
  1.5 0.9 copy-done.2
  2.4 0.9 copy-done.3
  3.3 0.6 pack.1
  4.0 3.0 %collective-permute-start = (bf16[128,256]{1,0:T(8,128)(2,1)S(1)}, bf16[128,256]{1,0:T(8,128)(2,1)S(1)}, u32[]{:S(2)}, u32[]{:S(2)}) collective-permute-start(bf16[128,256]{1,0:T(8,128)(2,1)S(1)} %pack.1), channel_id=1, source_target_pairs={{0,4},{4,0},{8,12},{12,8},{16,20},{20,16},{24,28},{28,24},{1,5},{5... | collective-permute-start | bytes 196616 | tf_op jit(solution)/shard_map/ppermute | solution.py:276
  7.0 1.6 %collective-permute-start.1 = (bf16[128,256]{1,0:T(8,128)(2,1)S(1)}, bf16[128,256]{1,0:T(8,128)(2,1)S(1)}, u32[]{:S(2)}, u32[]{:S(2)}) collective-permute-start(bf16[128,256]{1,0:T(8,128)(2,1)S(1)} %pack.1), channel_id=1, source_target_pairs={{0,8},{4,12},{8,0},{12,4},{16,24},{20,28},{24,16},{28,20},{1,9},{5... | collective-permute-start | bytes 196616 | tf_op jit(solution)/shard_map/ppermute | solution.py:276
  8.6 3.0 %collective-permute-start.3 = (bf16[128,256]{1,0:T(8,128)(2,1)S(1)}, bf16[128,256]{1,0:T(8,128)(2,1)S(1)}, u32[]{:S(2)}, u32[]{:S(2)}) collective-permute-start(bf16[128,256]{1,0:T(8,128)(2,1)S(1)} %pack.1), channel_id=1, source_target_pairs={{0,16},{4,20},{8,24},{12,28},{16,0},{20,4},{24,8},{28,12},{1,17},{... | collective-permute-start | bytes 196616 | tf_op jit(solution)/shard_map/ppermute | solution.py:276
  11.6 1.3 %collective-permute-start.4 = (bf16[128,256]{1,0:T(8,128)(2,1)S(1)}, bf16[128,256]{1,0:T(8,128)(2,1)S(1)}, u32[]{:S(2)}, u32[]{:S(2)}) collective-permute-start(bf16[128,256]{1,0:T(8,128)(2,1)S(1)} %pack.1), channel_id=1, source_target_pairs={{0,20},{4,16},{8,28},{12,24},{16,4},{20,0},{24,12},{28,8},{1,21},{... | collective-permute-start | bytes 196616 | tf_op jit(solution)/shard_map/ppermute | solution.py:276
  13.5 3.6 %collective-permute-start.5 = (bf16[128,256]{1,0:T(8,128)(2,1)S(1)}, bf16[128,256]{1,0:T(8,128)(2,1)S(1)}, u32[]{:S(2)}, u32[]{:S(2)}) collective-permute-start(bf16[128,256]{1,0:T(8,128)(2,1)S(1)} %pack.1), channel_id=1, source_target_pairs={{0,24},{4,28},{8,16},{12,20},{16,8},{20,12},{24,0},{28,4},{1,25},{... | collective-permute-start | bytes 196616 | tf_op jit(solution)/shard_map/ppermute | solution.py:276
  17.2 4.6 %collective-permute-done.4 = bf16[128,256]{1,0:T(8,128)(2,1)S(1)} collective-permute-done((bf16[128,256]{1,0:T(8,128)(2,1)S(1)}, bf16[128,256]{1,0:T(8,128)(2,1)S(1)}, u32[]{:S(2)}, u32[]{:S(2)}) %collective-permute-start.4) | collective-permute-done | bytes 65568 | tf_op jit(solution)/shard_map/ppermute | solution.py:276
  21.8 2.4 %collective-permute-done.6 = bf16[128,256]{1,0:T(8,128)(2,1)S(1)} collective-permute-done((bf16[128,256]{1,0:T(8,128)(2,1)S(1)}, bf16[128,256]{1,0:T(8,128)(2,1)S(1)}, u32[]{:S(2)}, u32[]{:S(2)}) %collective-permute-start.6) | collective-permute-done | bytes 65568 | tf_op jit(solution)/shard_map/ppermute | solution.py:276
  24.7 1.4 %collective-permute-done.7.other = bf16[1024,256]{1,0:T(8,128)(2,1)S(1)} collective-permute-done((bf16[1024,256]{1,0:T(8,128)(2,1)S(1)}, bf16[1024,256]{1,0:T(8,128)(2,1)S(1)}, u32[]{:S(2)}, u32[]{:S(2)}) %collective-permute-start.7) | collective-permute-done | bytes 524320 | tf_op jit(solution)/shard_map/ppermute | solution.py:283
  26.1 4.2 %attention.1 = (bf16[128,1024]{1,0:T(8,128)(2,1)S(1)}, bf16[128,1024]{1,0:T(8,128)(2,1)S(1)}) custom-call(s32[66]{0:T(128)S(1)} %pad_add_fusion.2.table, bf16[256,1024]{1,0:T(8,128)(2,1)S(1)} %turn.1.queries, bf16[1024,256]{1,0:T(8,128)(2,1)S(1)} %constant_dynamic-update-slice_fusion.own, bf16[1024,256]{1,0:T(8,128)(2,1)S(1)} %collective-permute-done.7.other), custom_call_target="tpu_custom_call" | custom-call | tf_op jit(solution)/shard_map/attention/pallas_call | solution.py:141
  30.6 1.9 %collective-permute-done.8 = bf16[128,1024]{1,0:T(8,128)(2,1)S(1)} collective-permute-done((bf16[128,1024]{1,0:T(8,128)(2,1)S(1)}, bf16[128,1024]{1,0:T(8,128)(2,1)S(1)}, u32[]{:S(2)}, u32[]{:S(2)}) %collective-permute-start.8) | collective-permute-done | bytes 262176 | tf_op jit(solution)/shard_map/ppermute | solution.py:219
  32.5 4.0 %collective-permute-start.9 = (bf16[128,2048]{1,0:T(8,128)(2,1)S(1)}, bf16[128,2048]{1,0:T(8,128)(2,1)S(1)}, u32[]{:S(2)}, u32[]{:S(2)}) collective-permute-start(bf16[128,2048]{1,0:T(8,128)(2,1)S(1)} %constant_dynamic-update-slice_fusion.8), channel_id=1, source_target_pairs={{0,16},{2,10},{4,20},{6,14},{9,1},{11,19},{13,5},{15,23},{16,8},{1... | collective-permute-start | bytes 1572872 | tf_op jit(solution)/shard_map/ppermute | solution.py:220
  36.6 1.3 %collective-permute-start.10 = (bf16[128,2048]{1,0:T(8,128)(2,1)S(1)}, bf16[128,2048]{1,0:T(8,128)(2,1)S(1)}, u32[]{:S(2)}, u32[]{:S(2)}) collective-permute-start(bf16[128,2048]{1,0:T(8,128)(2,1)S(1)} %constant_dynamic-update-slice_fusion.8), channel_id=1, source_target_pairs={{0,8},{2,18},{4,12},{6,22},{9,17},{11,3},{13,21},{15,7},{16,24},{1... | collective-permute-start | bytes 1572872 | tf_op jit(solution)/shard_map/ppermute | solution.py:221
  38.0 0.7 constant_dynamic-update-slice_fusion.11
  38.7 0.8 collective-permute-done.12
  39.5 0.8 constant_dynamic-update-slice_fusion.10
  40.3 2.3 %collective-permute-start.13 = (bf16[128,2048]{1,0:T(8,128)(2,1)}, bf16[128,2048]{1,0:T(8,128)(2,1)S(1)}, u32[]{:S(2)}, u32[]{:S(2)}) collective-permute-start(bf16[128,2048]{1,0:T(8,128)(2,1)} %constant_dynamic-update-slice_fusion.10), channel_id=1, source_target_pairs={{0,16},{2,10},{4,20},{6,14},{9,1},{11,19},{13,5},{15,23},{16,8},{1... | collective-permute-start | bytes 1572872 | tf_op jit(solution)/shard_map/ppermute | solution.py:220
  42.5 1.3 %collective-permute-start.14 = (bf16[128,2048]{1,0:T(8,128)(2,1)}, bf16[128,2048]{1,0:T(8,128)(2,1)S(1)}, u32[]{:S(2)}, u32[]{:S(2)}) collective-permute-start(bf16[128,2048]{1,0:T(8,128)(2,1)} %constant_dynamic-update-slice_fusion.10), channel_id=1, source_target_pairs={{0,8},{2,18},{4,12},{6,22},{9,17},{11,3},{13,21},{15,7},{16,24},{1... | collective-permute-start | bytes 1572872 | tf_op jit(solution)/shard_map/ppermute | solution.py:221
  43.9 5.0 %collective-permute-done.10 = bf16[128,2048]{1,0:T(8,128)(2,1)S(1)} collective-permute-done((bf16[128,2048]{1,0:T(8,128)(2,1)S(1)}, bf16[128,2048]{1,0:T(8,128)(2,1)S(1)}, u32[]{:S(2)}, u32[]{:S(2)}) %collective-permute-start.10) | collective-permute-done | bytes 524320 | tf_op jit(solution)/shard_map/ppermute | solution.py:221
  48.9 1.3 %collective-permute-start.11 = (bf16[128,2048]{1,0:T(8,128)(2,1)S(1)}, bf16[128,2048]{1,0:T(8,128)(2,1)S(1)}, u32[]{:S(2)}, u32[]{:S(2)}) collective-permute-start(bf16[128,2048]{1,0:T(8,128)(2,1)S(1)} %broadcast_select_fusion.1), channel_id=1, source_target_pairs={{8,0},{9,1},{10,2},{11,3},{12,4},{13,5},{14,6},{15,7},{16,24},{17,... | collective-permute-start | bytes 1572872 | tf_op jit(solution)/shard_map/ppermute | solution.py:223
  50.3 4.4 %collective-permute-done.13 = bf16[128,2048]{1,0:T(8,128)(2,1)S(1)} collective-permute-done((bf16[128,2048]{1,0:T(8,128)(2,1)}, bf16[128,2048]{1,0:T(8,128)(2,1)S(1)}, u32[]{:S(2)}, u32[]{:S(2)}) %collective-permute-start.13) | collective-permute-done | bytes 524320 | tf_op jit(solution)/shard_map/ppermute | solution.py:220
  54.6 5.6 %collective-permute-done.14 = bf16[128,2048]{1,0:T(8,128)(2,1)S(1)} collective-permute-done((bf16[128,2048]{1,0:T(8,128)(2,1)}, bf16[128,2048]{1,0:T(8,128)(2,1)S(1)}, u32[]{:S(2)}, u32[]{:S(2)}) %collective-permute-start.14) | collective-permute-done | bytes 524320 | tf_op jit(solution)/shard_map/ppermute | solution.py:221
  60.3 1.5 %collective-permute-start.15 = (bf16[128,2048]{1,0:T(8,128)(2,1)S(1)}, bf16[128,2048]{1,0:T(8,128)(2,1)S(1)}, u32[]{:S(2)}, u32[]{:S(2)}) collective-permute-start(bf16[128,2048]{1,0:T(8,128)(2,1)S(1)} %broadcast_select_fusion), channel_id=1, source_target_pairs={{8,0},{9,1},{10,2},{11,3},{12,4},{13,5},{14,6},{15,7},{16,24},{17,... | collective-permute-start | bytes 1572872 | tf_op jit(solution)/shard_map/ppermute | solution.py:223
  61.8 2.0 %collective-permute-done.11 = bf16[128,2048]{1,0:T(8,128)(2,1)S(1)} collective-permute-done((bf16[128,2048]{1,0:T(8,128)(2,1)S(1)}, bf16[128,2048]{1,0:T(8,128)(2,1)S(1)}, u32[]{:S(2)}, u32[]{:S(2)}) %collective-permute-start.11) | collective-permute-done | bytes 524320 | tf_op jit(solution)/shard_map/ppermute | solution.py:223
  63.8 1.2 broadcast_select_fusion.5
  65.7 1.5 %collective-permute-start.19 = (bf16[128,2048]{1,0:T(8,128)(2,1)S(1)}, bf16[128,2048]{1,0:T(8,128)(2,1)}, u32[]{:S(2)}, u32[]{:S(2)}) collective-permute-start(bf16[128,2048]{1,0:T(8,128)(2,1)S(1)} %get-tuple-element.25.rows), channel_id=1, source_target_pairs={{0,4},{4,0},{8,12},{12,8},{16,20},{20,16},{24,28},{28,24},{1,5},{5... | collective-permute-start | bytes 1572872 | tf_op jit(solution)/shard_map/ppermute | solution.py:228
  67.2 7.8 %collective-permute-done.15 = bf16[128,2048]{1,0:T(8,128)(2,1)S(1)} collective-permute-done((bf16[128,2048]{1,0:T(8,128)(2,1)S(1)}, bf16[128,2048]{1,0:T(8,128)(2,1)S(1)}, u32[]{:S(2)}, u32[]{:S(2)}) %collective-permute-start.15) | collective-permute-done | bytes 524320 | tf_op jit(solution)/shard_map/ppermute | solution.py:223
  75.1 1.2 broadcast_select_fusion.4
  77.0 1.6 %collective-permute-start.17 = (bf16[128,2048]{1,0:T(8,128)(2,1)S(1)}, bf16[128,2048]{1,0:T(8,128)(2,1)S(1)}, u32[]{:S(2)}, u32[]{:S(2)}) collective-permute-start(bf16[128,2048]{1,0:T(8,128)(2,1)S(1)} %broadcast_select_fusion.6.rows), channel_id=1, source_target_pairs={{0,4},{4,0},{8,12},{12,8},{16,20},{20,16},{24,28},{28,24},{1,5},{5... | collective-permute-start | bytes 1572872 | tf_op jit(solution)/shard_map/ppermute | solution.py:229
  78.5 2.2 %copy-done = bf16[1024,2048]{1,0:T(8,128)(2,1)S(1)} copy-done((bf16[1024,2048]{1,0:T(8,128)(2,1)S(1)}, bf16[1024,2048]{1,0:T(8,128)(2,1)}, u32[]{:S(2)}) %copy-start) | copy-done | bytes 4194328
  80.7 3.4 %project.8 = bf16[128,2048]{1,0:T(8,128)(2,1)S(1)} custom-call(bf16[128,2048]{1,0:T(8,128)(2,1)S(1)} %get-tuple-element.25.rows, bf16[1024,2048]{1,0:T(8,128)(2,1)S(1)} %copy-done, bf16[1024,2048]{1,0:T(8,128)(2,1)} %collective-permute-done.18.other), custom_call_target="tpu_custom_call" | custom-call | flops 1073741824 | bytes 1048576 | tf_op jit(solution)/shard_map/project/pallas_call | solution.py:172
  84.5 3.4 %project.9 = bf16[128,2048]{1,0:T(8,128)(2,1)S(1)} custom-call(bf16[128,2048]{1,0:T(8,128)(2,1)S(1)} %get-tuple-element.23.rows, bf16[1024,2048]{1,0:T(8,128)(2,1)S(1)} %copy-done, bf16[1024,2048]{1,0:T(8,128)(2,1)} %collective-permute-done.18.other), custom_call_target="tpu_custom_call" | custom-call | flops 1073741824 | bytes 1048576 | tf_op jit(solution)/shard_map/project/pallas_call | solution.py:172
  88.0 3.4 %collective-permute-done.19.rows = bf16[128,2048]{1,0:T(8,128)(2,1)} collective-permute-done((bf16[128,2048]{1,0:T(8,128)(2,1)S(1)}, bf16[128,2048]{1,0:T(8,128)(2,1)}, u32[]{:S(2)}, u32[]{:S(2)}) %collective-permute-start.19) | collective-permute-done | bytes 524320 | tf_op jit(solution)/shard_map/ppermute | solution.py:228
  91.4 2.3 %collective-permute-start.22 = (bf16[128,2048]{1,0:T(8,128)(2,1)S(1)}, bf16[128,2048]{1,0:T(8,128)(2,1)S(1)}, u32[]{:S(2)}, u32[]{:S(2)}) collective-permute-start(bf16[128,2048]{1,0:T(8,128)(2,1)S(1)} %project.9), channel_id=1, source_target_pairs={{0,2},{1,3},{2,0},{3,1},{4,6},{5,7},{6,4},{7,5},{8,10},{9,11},{10,... | collective-permute-start | bytes 1572872 | tf_op jit(solution)/shard_map/ppermute | solution.py:231
  93.7 3.6 %project.10 = bf16[128,2048]{1,0:T(8,128)(2,1)S(1)} custom-call(bf16[128,2048]{1,0:T(8,128)(2,1)} %collective-permute-done.19.rows, bf16[1024,2048]{1,0:T(8,128)(2,1)S(1)} %copy-done, bf16[1024,2048]{1,0:T(8,128)(2,1)} %collective-permute-done.18.other), custom_call_target="tpu_custom_call" | custom-call | flops 1073741824 | bytes 1048576 | tf_op jit(solution)/shard_map/project/pallas_call | solution.py:172
  97.3 5.4 %collective-permute-done.20.rows = bf16[128,2048]{1,0:T(8,128)(2,1)} collective-permute-done((bf16[128,2048]{1,0:T(8,128)(2,1)S(1)}, bf16[128,2048]{1,0:T(8,128)(2,1)}, u32[]{:S(2)}, u32[]{:S(2)}) %collective-permute-start.20) | collective-permute-done | bytes 524320 | tf_op jit(solution)/shard_map/ppermute | solution.py:228
  102.6 2.0 %collective-permute-start.23 = (bf16[128,2048]{1,0:T(8,128)(2,1)S(1)}, bf16[128,2048]{1,0:T(8,128)(2,1)S(1)}, u32[]{:S(2)}, u32[]{:S(2)}) collective-permute-start(bf16[128,2048]{1,0:T(8,128)(2,1)S(1)} %project.10), channel_id=1, source_target_pairs={{0,2},{1,3},{2,0},{3,1},{4,6},{5,7},{6,4},{7,5},{8,10},{9,11},{10,... | collective-permute-start | bytes 1572872 | tf_op jit(solution)/shard_map/ppermute | solution.py:231
  104.6 3.6 %project.11 = bf16[128,2048]{1,0:T(8,128)(2,1)S(1)} custom-call(bf16[128,2048]{1,0:T(8,128)(2,1)} %collective-permute-done.20.rows, bf16[1024,2048]{1,0:T(8,128)(2,1)S(1)} %copy-done, bf16[1024,2048]{1,0:T(8,128)(2,1)} %collective-permute-done.18.other), custom_call_target="tpu_custom_call" | custom-call | flops 1073741824 | bytes 1048576 | tf_op jit(solution)/shard_map/project/pallas_call | solution.py:172
  108.4 1.5 %collective-permute-done.17.rows = bf16[128,2048]{1,0:T(8,128)(2,1)S(1)} collective-permute-done((bf16[128,2048]{1,0:T(8,128)(2,1)S(1)}, bf16[128,2048]{1,0:T(8,128)(2,1)S(1)}, u32[]{:S(2)}, u32[]{:S(2)}) %collective-permute-start.17) | collective-permute-done | bytes 524320 | tf_op jit(solution)/shard_map/ppermute | solution.py:229
  109.9 3.4 %project.12 = f32[128,2048]{1,0:T(8,128)S(1)} custom-call(bf16[128,2048]{1,0:T(8,128)(2,1)S(1)} %broadcast_select_fusion.7.rows, bf16[1024,2048]{1,0:T(8,128)(2,1)S(1)} %copy-done, bf16[1024,2048]{1,0:T(8,128)(2,1)} %collective-permute-done.18.other), custom_call_target="tpu_custom_call" | custom-call | flops 1073741824 | bytes 1048576 | tf_op jit(solution)/shard_map/project/pallas_call | solution.py:172
  113.3 3.4 %project.13 = f32[128,2048]{1,0:T(8,128)S(1)} custom-call(bf16[128,2048]{1,0:T(8,128)(2,1)S(1)} %broadcast_select_fusion.6.rows, bf16[1024,2048]{1,0:T(8,128)(2,1)S(1)} %copy-done, bf16[1024,2048]{1,0:T(8,128)(2,1)} %collective-permute-done.18.other), custom_call_target="tpu_custom_call" | custom-call | flops 1073741824 | bytes 1048576 | tf_op jit(solution)/shard_map/project/pallas_call | solution.py:172
  116.8 3.4 %project.14 = f32[128,2048]{1,0:T(8,128)S(1)} custom-call(bf16[128,2048]{1,0:T(8,128)(2,1)S(1)} %collective-permute-done.16.rows, bf16[1024,2048]{1,0:T(8,128)(2,1)S(1)} %copy-done, bf16[1024,2048]{1,0:T(8,128)(2,1)} %collective-permute-done.18.other), custom_call_target="tpu_custom_call" | custom-call | flops 1073741824 | bytes 1048576 | tf_op jit(solution)/shard_map/project/pallas_call | solution.py:172
  120.2 3.4 %project.15 = f32[128,2048]{1,0:T(8,128)S(1)} custom-call(bf16[128,2048]{1,0:T(8,128)(2,1)S(1)} %collective-permute-done.17.rows, bf16[1024,2048]{1,0:T(8,128)(2,1)S(1)} %copy-done, bf16[1024,2048]{1,0:T(8,128)(2,1)} %collective-permute-done.18.other), custom_call_target="tpu_custom_call" | custom-call | flops 1073741824 | bytes 1048576 | tf_op jit(solution)/shard_map/project/pallas_call | solution.py:172
  124.3 3.9 %collective-permute-done.24 = bf16[128,2048]{1,0:T(8,128)(2,1)S(1)} collective-permute-done((bf16[128,2048]{1,0:T(8,128)(2,1)S(1)}, bf16[128,2048]{1,0:T(8,128)(2,1)S(1)}, u32[]{:S(2)}, u32[]{:S(2)}) %collective-permute-start.24) | collective-permute-done | bytes 524320 | tf_op jit(solution)/shard_map/ppermute | solution.py:231
  128.2 0.9 fusion.3
  (65 shorter events, 4.8 us)
Async XLA Ops:
  0.0 12.9 %copy-start.1 = (bf16[256,1024]{1,0:T(8,128)(2,1)S(1)}, bf16[256,1024]{1,0:T(8,128)(2,1)}, u32[]{:S(2)}) copy-start(bf16[256,1024]{1,0:T(8,128)(2,1)} %queries.1) | copy-start | bytes 1572868
  0.0 13.2 %copy-start.8 = (s32[8,4]{0,1:T(4,128)S(1)}, s32[8,4]{0,1:T(4,128)}, u32[]{:S(2)}) copy-start(s32[8,4]{0,1:T(4,128)} %param.11) | copy-start | bytes 388
  0.0 13.2 %copy-start.9 = (s32[8,4]{0,1:T(4,128)S(1)}, s32[8,4]{0,1:T(4,128)}, u32[]{:S(2)}) copy-start(s32[8,4]{0,1:T(4,128)} %param.10) | copy-start | bytes 388
  1.5 0.9 copy-start.2
  2.4 0.9 copy-start.3
  4.0 9.5 %collective-permute-start = (bf16[128,256]{1,0:T(8,128)(2,1)S(1)}, bf16[128,256]{1,0:T(8,128)(2,1)S(1)}, u32[]{:S(2)}, u32[]{:S(2)}) collective-permute-start(bf16[128,256]{1,0:T(8,128)(2,1)S(1)} %pack.1), channel_id=1, source_target_pairs={{0,4},{4,0},{8,12},{12,8},{16,20},{20,16},{24,28},{28,24},{1,5},{5... | collective-permute-start | bytes 196616 | tf_op jit(solution)/shard_map/ppermute | solution.py:276
  7.0 10.1 %collective-permute-start.1 = (bf16[128,256]{1,0:T(8,128)(2,1)S(1)}, bf16[128,256]{1,0:T(8,128)(2,1)S(1)}, u32[]{:S(2)}, u32[]{:S(2)}) collective-permute-start(bf16[128,256]{1,0:T(8,128)(2,1)S(1)} %pack.1), channel_id=1, source_target_pairs={{0,8},{4,12},{8,0},{12,4},{16,24},{20,28},{24,16},{28,20},{1,9},{5... | collective-permute-start | bytes 196616 | tf_op jit(solution)/shard_map/ppermute | solution.py:276
  8.6 8.6 %collective-permute-start.2 = (bf16[128,256]{1,0:T(8,128)(2,1)S(1)}, bf16[128,256]{1,0:T(8,128)(2,1)S(1)}, u32[]{:S(2)}, u32[]{:S(2)}) collective-permute-start(bf16[128,256]{1,0:T(8,128)(2,1)S(1)} %pack.1), channel_id=1, source_target_pairs={{0,12},{4,8},{8,4},{12,0},{16,28},{20,24},{24,20},{28,16},{1,13},{... | collective-permute-start | bytes 196616 | tf_op jit(solution)/shard_map/ppermute | solution.py:276
  8.6 8.6 %collective-permute-start.3 = (bf16[128,256]{1,0:T(8,128)(2,1)S(1)}, bf16[128,256]{1,0:T(8,128)(2,1)S(1)}, u32[]{:S(2)}, u32[]{:S(2)}) collective-permute-start(bf16[128,256]{1,0:T(8,128)(2,1)S(1)} %pack.1), channel_id=1, source_target_pairs={{0,16},{4,20},{8,24},{12,28},{16,0},{20,4},{24,8},{28,12},{1,17},{... | collective-permute-start | bytes 196616 | tf_op jit(solution)/shard_map/ppermute | solution.py:276
  11.6 10.2 %collective-permute-start.4 = (bf16[128,256]{1,0:T(8,128)(2,1)S(1)}, bf16[128,256]{1,0:T(8,128)(2,1)S(1)}, u32[]{:S(2)}, u32[]{:S(2)}) collective-permute-start(bf16[128,256]{1,0:T(8,128)(2,1)S(1)} %pack.1), channel_id=1, source_target_pairs={{0,20},{4,16},{8,28},{12,24},{16,4},{20,0},{24,12},{28,8},{1,21},{... | collective-permute-start | bytes 196616 | tf_op jit(solution)/shard_map/ppermute | solution.py:276
  13.5 8.3 %collective-permute-start.5 = (bf16[128,256]{1,0:T(8,128)(2,1)S(1)}, bf16[128,256]{1,0:T(8,128)(2,1)S(1)}, u32[]{:S(2)}, u32[]{:S(2)}) collective-permute-start(bf16[128,256]{1,0:T(8,128)(2,1)S(1)} %pack.1), channel_id=1, source_target_pairs={{0,24},{4,28},{8,16},{12,20},{16,8},{20,12},{24,0},{28,4},{1,25},{... | collective-permute-start | bytes 196616 | tf_op jit(solution)/shard_map/ppermute | solution.py:276
  17.1 7.1 %collective-permute-start.6 = (bf16[128,256]{1,0:T(8,128)(2,1)S(1)}, bf16[128,256]{1,0:T(8,128)(2,1)S(1)}, u32[]{:S(2)}, u32[]{:S(2)}) collective-permute-start(bf16[128,256]{1,0:T(8,128)(2,1)S(1)} %pack.1), channel_id=1, source_target_pairs={{0,28},{4,24},{8,20},{12,16},{16,12},{20,8},{24,4},{28,0},{1,29},{... | collective-permute-start | bytes 196616 | tf_op jit(solution)/shard_map/ppermute | solution.py:276
  24.2 1.9 %collective-permute-start.7 = (bf16[1024,256]{1,0:T(8,128)(2,1)S(1)}, bf16[1024,256]{1,0:T(8,128)(2,1)S(1)}, u32[]{:S(2)}, u32[]{:S(2)}) collective-permute-start(bf16[1024,256]{1,0:T(8,128)(2,1)S(1)} %constant_dynamic-update-slice_fusion.own), channel_id=1, source_target_pairs={{0,1},{1,0},{2,3},{3,2},{4,5},{5,4},{6,7},{7,6},{8,9},{9,8},{10,11... | collective-permute-start | bytes 1572872 | tf_op jit(solution)/shard_map/ppermute | solution.py:283
  24.2 54.3 %collective-permute-start.18 = (bf16[1024,2048]{1,0:T(8,128)(2,1)}, bf16[1024,2048]{1,0:T(8,128)(2,1)}, u32[]{:S(2)}, u32[]{:S(2)}) collective-permute-start(bf16[1024,2048]{1,0:T(8,128)(2,1)} %own.15), channel_id=1, source_target_pairs={{0,1},{1,0},{2,3},{3,2},{4,5},{5,4},{6,7},{7,6},{8,9},{9,8},{10,11... | collective-permute-start | bytes 12582920 | tf_op jit(solution)/shard_map/ppermute | solution.py:213
  30.3 2.2 %collective-permute-start.8 = (bf16[128,1024]{1,0:T(8,128)(2,1)S(1)}, bf16[128,1024]{1,0:T(8,128)(2,1)S(1)}, u32[]{:S(2)}, u32[]{:S(2)}) collective-permute-start(bf16[128,1024]{1,0:T(8,128)(2,1)S(1)} %get-tuple-element.17), channel_id=1, source_target_pairs={{0,1},{1,0},{2,3},{3,2},{4,5},{5,4},{6,7},{7,6},{8,9},{9,8},{10,11... | collective-permute-start | bytes 786440 | tf_op jit(solution)/shard_map/ppermute | solution.py:219
  32.5 16.4 %copy-start.7 = (bf16[128,2048]{1,0:T(8,128)(2,1)}, bf16[128,2048]{1,0:T(8,128)(2,1)S(1)}, u32[]{:S(2)}) copy-start(bf16[128,2048]{1,0:T(8,128)(2,1)S(1)} %constant_dynamic-update-slice_fusion.8) | copy-start | bytes 1572868
  32.5 11.3 %collective-permute-start.9 = (bf16[128,2048]{1,0:T(8,128)(2,1)S(1)}, bf16[128,2048]{1,0:T(8,128)(2,1)S(1)}, u32[]{:S(2)}, u32[]{:S(2)}) collective-permute-start(bf16[128,2048]{1,0:T(8,128)(2,1)S(1)} %constant_dynamic-update-slice_fusion.8), channel_id=1, source_target_pairs={{0,16},{2,10},{4,20},{6,14},{9,1},{11,19},{13,5},{15,23},{16,8},{1... | collective-permute-start | bytes 1572872 | tf_op jit(solution)/shard_map/ppermute | solution.py:220
  36.6 12.3 %collective-permute-start.10 = (bf16[128,2048]{1,0:T(8,128)(2,1)S(1)}, bf16[128,2048]{1,0:T(8,128)(2,1)S(1)}, u32[]{:S(2)}, u32[]{:S(2)}) collective-permute-start(bf16[128,2048]{1,0:T(8,128)(2,1)S(1)} %constant_dynamic-update-slice_fusion.8), channel_id=1, source_target_pairs={{0,8},{2,18},{4,12},{6,22},{9,17},{11,3},{13,21},{15,7},{16,24},{1... | collective-permute-start | bytes 1572872 | tf_op jit(solution)/shard_map/ppermute | solution.py:221
  37.9 1.6 %collective-permute-start.12 = (bf16[128,1024]{1,0:T(8,128)(2,1)S(1)}, bf16[128,1024]{1,0:T(8,128)(2,1)S(1)}, u32[]{:S(2)}, u32[]{:S(2)}) collective-permute-start(bf16[128,1024]{1,0:T(8,128)(2,1)S(1)} %get-tuple-element.18), channel_id=1, source_target_pairs={{0,1},{1,0},{2,3},{3,2},{4,5},{5,4},{6,7},{7,6},{8,9},{9,8},{10,11... | collective-permute-start | bytes 786440 | tf_op jit(solution)/shard_map/ppermute | solution.py:219
  40.3 14.4 %collective-permute-start.13 = (bf16[128,2048]{1,0:T(8,128)(2,1)}, bf16[128,2048]{1,0:T(8,128)(2,1)S(1)}, u32[]{:S(2)}, u32[]{:S(2)}) collective-permute-start(bf16[128,2048]{1,0:T(8,128)(2,1)} %constant_dynamic-update-slice_fusion.10), channel_id=1, source_target_pairs={{0,16},{2,10},{4,20},{6,14},{9,1},{11,19},{13,5},{15,23},{16,8},{1... | collective-permute-start | bytes 1572872 | tf_op jit(solution)/shard_map/ppermute | solution.py:220
  42.5 17.7 %collective-permute-start.14 = (bf16[128,2048]{1,0:T(8,128)(2,1)}, bf16[128,2048]{1,0:T(8,128)(2,1)S(1)}, u32[]{:S(2)}, u32[]{:S(2)}) collective-permute-start(bf16[128,2048]{1,0:T(8,128)(2,1)} %constant_dynamic-update-slice_fusion.10), channel_id=1, source_target_pairs={{0,8},{2,18},{4,12},{6,22},{9,17},{11,3},{13,21},{15,7},{16,24},{1... | collective-permute-start | bytes 1572872 | tf_op jit(solution)/shard_map/ppermute | solution.py:221
  48.9 14.9 %collective-permute-start.11 = (bf16[128,2048]{1,0:T(8,128)(2,1)S(1)}, bf16[128,2048]{1,0:T(8,128)(2,1)S(1)}, u32[]{:S(2)}, u32[]{:S(2)}) collective-permute-start(bf16[128,2048]{1,0:T(8,128)(2,1)S(1)} %broadcast_select_fusion.1), channel_id=1, source_target_pairs={{8,0},{9,1},{10,2},{11,3},{12,4},{13,5},{14,6},{15,7},{16,24},{17,... | collective-permute-start | bytes 1572872 | tf_op jit(solution)/shard_map/ppermute | solution.py:223
  60.3 1.5 %copy-start.4 = (bf16[128,2048]{1,0:T(8,128)(2,1)}, bf16[128,2048]{1,0:T(8,128)(2,1)S(1)}, u32[]{:S(2)}) copy-start(bf16[128,2048]{1,0:T(8,128)(2,1)S(1)} %collective-permute-done.14) | copy-start | bytes 1572868
  60.3 14.7 %collective-permute-start.15 = (bf16[128,2048]{1,0:T(8,128)(2,1)S(1)}, bf16[128,2048]{1,0:T(8,128)(2,1)S(1)}, u32[]{:S(2)}, u32[]{:S(2)}) collective-permute-start(bf16[128,2048]{1,0:T(8,128)(2,1)S(1)} %broadcast_select_fusion), channel_id=1, source_target_pairs={{8,0},{9,1},{10,2},{11,3},{12,4},{13,5},{14,6},{15,7},{16,24},{17,... | collective-permute-start | bytes 1572872 | tf_op jit(solution)/shard_map/ppermute | solution.py:223
  63.8 11.2 %copy-start.5 = (bf16[128,2048]{1,0:T(8,128)(2,1)S(1)}, bf16[128,2048]{1,0:T(8,128)(2,1)}, u32[]{:S(2)}) copy-start(bf16[128,2048]{1,0:T(8,128)(2,1)} %copy-done.4) | copy-start | bytes 1572868
  65.1 43.1 %collective-permute-start.16 = (bf16[128,2048]{1,0:T(8,128)(2,1)S(1)}, bf16[128,2048]{1,0:T(8,128)(2,1)S(1)}, u32[]{:S(2)}, u32[]{:S(2)}) collective-permute-start(bf16[128,2048]{1,0:T(8,128)(2,1)S(1)} %broadcast_select_fusion.7.rows), channel_id=1, source_target_pairs={{0,4},{4,0},{8,12},{12,8},{16,20},{20,16},{24,28},{28,24},{1,5},{5... | collective-permute-start | bytes 1572872 | tf_op jit(solution)/shard_map/ppermute | solution.py:229
  65.7 25.7 %collective-permute-start.19 = (bf16[128,2048]{1,0:T(8,128)(2,1)S(1)}, bf16[128,2048]{1,0:T(8,128)(2,1)}, u32[]{:S(2)}, u32[]{:S(2)}) collective-permute-start(bf16[128,2048]{1,0:T(8,128)(2,1)S(1)} %get-tuple-element.25.rows), channel_id=1, source_target_pairs={{0,4},{4,0},{8,12},{12,8},{16,20},{20,16},{24,28},{28,24},{1,5},{5... | collective-permute-start | bytes 1572872 | tf_op jit(solution)/shard_map/ppermute | solution.py:228
  76.3 26.4 %collective-permute-start.20 = (bf16[128,2048]{1,0:T(8,128)(2,1)S(1)}, bf16[128,2048]{1,0:T(8,128)(2,1)}, u32[]{:S(2)}, u32[]{:S(2)}) collective-permute-start(bf16[128,2048]{1,0:T(8,128)(2,1)S(1)} %get-tuple-element.23.rows), channel_id=1, source_target_pairs={{0,4},{4,0},{8,12},{12,8},{16,20},{20,16},{24,28},{28,24},{1,5},{5... | collective-permute-start | bytes 1572872 | tf_op jit(solution)/shard_map/ppermute | solution.py:228
  77.0 32.9 %collective-permute-start.17 = (bf16[128,2048]{1,0:T(8,128)(2,1)S(1)}, bf16[128,2048]{1,0:T(8,128)(2,1)S(1)}, u32[]{:S(2)}, u32[]{:S(2)}) collective-permute-start(bf16[128,2048]{1,0:T(8,128)(2,1)S(1)} %broadcast_select_fusion.6.rows), channel_id=1, source_target_pairs={{0,4},{4,0},{8,12},{12,8},{16,20},{20,16},{24,28},{28,24},{1,5},{5... | collective-permute-start | bytes 1572872 | tf_op jit(solution)/shard_map/ppermute | solution.py:229
  78.5 2.2 %copy-start = (bf16[1024,2048]{1,0:T(8,128)(2,1)S(1)}, bf16[1024,2048]{1,0:T(8,128)(2,1)}, u32[]{:S(2)}) copy-start(bf16[1024,2048]{1,0:T(8,128)(2,1)} %own.15) | copy-start | bytes 12582916
  84.2 39.5 %collective-permute-start.21 = (bf16[128,2048]{1,0:T(8,128)(2,1)S(1)}, bf16[128,2048]{1,0:T(8,128)(2,1)S(1)}, u32[]{:S(2)}, u32[]{:S(2)}) collective-permute-start(bf16[128,2048]{1,0:T(8,128)(2,1)S(1)} %project.8), channel_id=1, source_target_pairs={{0,2},{1,3},{2,0},{3,1},{4,6},{5,7},{6,4},{7,5},{8,10},{9,11},{10,... | collective-permute-start | bytes 1572872 | tf_op jit(solution)/shard_map/ppermute | solution.py:231
  91.4 32.7 %collective-permute-start.22 = (bf16[128,2048]{1,0:T(8,128)(2,1)S(1)}, bf16[128,2048]{1,0:T(8,128)(2,1)S(1)}, u32[]{:S(2)}, u32[]{:S(2)}) collective-permute-start(bf16[128,2048]{1,0:T(8,128)(2,1)S(1)} %project.9), channel_id=1, source_target_pairs={{0,2},{1,3},{2,0},{3,1},{4,6},{5,7},{6,4},{7,5},{8,10},{9,11},{10,... | collective-permute-start | bytes 1572872 | tf_op jit(solution)/shard_map/ppermute | solution.py:231
  102.6 21.6 %collective-permute-start.23 = (bf16[128,2048]{1,0:T(8,128)(2,1)S(1)}, bf16[128,2048]{1,0:T(8,128)(2,1)S(1)}, u32[]{:S(2)}, u32[]{:S(2)}) collective-permute-start(bf16[128,2048]{1,0:T(8,128)(2,1)S(1)} %project.10), channel_id=1, source_target_pairs={{0,2},{1,3},{2,0},{3,1},{4,6},{5,7},{6,4},{7,5},{8,10},{9,11},{10,... | collective-permute-start | bytes 1572872 | tf_op jit(solution)/shard_map/ppermute | solution.py:231
  108.2 20.0 %collective-permute-start.24 = (bf16[128,2048]{1,0:T(8,128)(2,1)S(1)}, bf16[128,2048]{1,0:T(8,128)(2,1)S(1)}, u32[]{:S(2)}, u32[]{:S(2)}) collective-permute-start(bf16[128,2048]{1,0:T(8,128)(2,1)S(1)} %project.11), channel_id=1, source_target_pairs={{0,2},{1,3},{2,0},{3,1},{4,6},{5,7},{6,4},{7,5},{8,10},{9,11},{10,... | collective-permute-start | bytes 1572872 | tf_op jit(solution)/shard_map/ppermute | solution.py:231
  124.3 3.9 %copy-start.6 = (bf16[512,2048]{1,0:T(8,128)(2,1)}, bf16[512,2048]{1,0:T(8,128)(2,1)S(1)}, u32[]{:S(2)}) copy-start(bf16[512,2048]{1,0:T(8,128)(2,1)S(1)} %fusion.2) | copy-start | bytes 6291460

commit v3 on v2

--- a/solution.py
+++ b/solution.py
@@ -214,23 +214,33 @@
     ]
     home, inner, first = z % 2 == core, (far == 1) | (far == 2), far >= 2
 
-    sent, kept = [], []
+    sent, kept, parts = [], [], []
+    hops = []
     for half in halves:
         block = jnp.concatenate([half, lax.ppermute(half, "head", swap_core)], axis=1)
         hop_1 = lax.ppermute(block, both, route(HOP_1))
         hop_2 = lax.ppermute(block, both, route(HOP_2))
+        hops.append((block, hop_1, hop_2))
+    for block, hop_1, hop_2 in hops:
         passed = jnp.where(lane == 0, hop_1, hop_2)
         hop_3 = lax.ppermute(passed, both, route(HOP_3))
+        if parts:
+            hop_3, _ = lax.optimization_barrier((hop_3, parts[-1]))
         early = jnp.where(home, block, jnp.where(lane == 0, hop_2, hop_1))
         late = jnp.where(inner, passed, hop_3)
         sent.append(jnp.where(first, early, late))
         kept.append(jnp.where(first, late, early))
-    sent += [lax.ppermute(rows, "ctx", swap_y) for rows in sent]
-    kept += [lax.ppermute(rows, "ctx", swap_y) for rows in kept]
-    parts = [project(rows, *weights, jnp.bfloat16) for rows in sent]
+        parts.append(project(sent[-1], *weights, jnp.bfloat16))
+    after = lambda rows, *others: lax.optimization_barrier((rows, others))[0]
+    sent_y = [lax.ppermute(rows, "ctx", swap_y) for rows in sent]
     come = [lax.ppermute(part, "head", swap_x) for part in parts]
-    kept, parts = lax.optimization_barrier((kept, parts))
-    own = [project(rows, *weights, jnp.float32) for rows in kept]
+    for i, rows in enumerate(sent_y):
+        parts.append(project(after(rows, come[i], parts[-1]), *weights, jnp.bfloat16))
+        come.append(lax.ppermute(parts[-1], "head", swap_x))
+    kept_y = [lax.ppermute(after(rows, parts[1]), "ctx", swap_y) for rows in kept]
+    own = [project(after(jnp.concatenate(kept, axis=0), parts[3]), *weights, jnp.float32)]
+    own.append(project(after(jnp.concatenate(kept_y, axis=0), own[0]), *weights, jnp.float32))
+    own = [o[i * BLK : (i + 1) * BLK] for o in own for i in range(len(halves))]
     rows = BLK * len(halves)
     out = jnp.zeros((2 * rows, out_weight.shape[1]), jnp.bfloat16)
     for i, (mine, theirs) in enumerate(zip(own, come)):

time: 130 us -> 119 us (0.915)
  waiting for transfers between devices: 50.1 us -> 37.4 us
  starting transfers between devices: 34 us -> 42.2 us
  Pallas kernels: 33 us -> 28 us
  local copies, waits for them, and re-layouts: 5.99 us -> 3.77 us
    ppermute x4 -> x6, waiting for transfers between devices: 10.3 us -> 2.54 us  [the longest x2 2.53 us: routed(): come.append(lax.ppermute(parts[-1], 'head', swap_x))]
    ppermute x2, waiting for transfers between devices: 9.84 us -> 2.35 us  [routed(): hop_3 = lax.ppermute(passed, both, route(HOP_3))]
    pallas_call x8 -> x6, Pallas kernels: 27.9 us -> 22.8 us  [project(): pl.pallas_call(project_kernel, in_specs=[VMEM] * 3, out_specs=VMEM, out_s...]
    ppermute x2, waiting for transfers between devices: 10.6 us -> 5.62 us  [routed(): hop_2 = lax.ppermute(block, both, route(HOP_2))]
    ppermute x4 -> x2, waiting for transfers between devices: 3.91 us -> 8.71 us  [routed(): come = [lax.ppermute(part, 'head', swap_x) for part in parts]]
    ppermute x4 -> x6, starting transfers between devices: 4.25 us -> 8.86 us  [the longest x2 5.08 us: routed(): come.append(lax.ppermute(parts[-1], 'head', swap_x))]
    ppermute x4 -> x2, starting transfers between devices: 4.73 us -> 9.01 us  [routed(): come = [lax.ppermute(part, 'head', swap_x) for part in parts]]
    ppermute x2, waiting for transfers between devices: 4.36 us -> 7.2 us  [routed(): hop_1 = lax.ppermute(block, both, route(HOP_1))]
  transfers between devices with their start and end apart: 25 -> 25, of which waited for: 14 -> 12; matrix products, arithmetic and copies ran while one was open for 4% -> 5% of each run, Pallas kernels for 25% -> 23%
where the time goes in v3:
time: 119 us; the launch traced here: 118 us
  starting transfers between devices  42.2 us (35%)
  waiting for transfers between devices  37.4 us (31%)
  Pallas kernels  28 us (24%)
  other arithmetic  6.3 us (5%)
  local copies, waits for them, and re-layouts  3.77 us (3%)
    pallas_call x6, Pallas kernels, project(): pl.pallas_call(project_kernel, in_specs=[VMEM] * 3, out_specs=VMEM, out_s...  22.8 us
    ppermute x7, starting transfers between devices, per_device(): lax.ppermute(piece, 'ctx', [(i, i ^ d) for i in range(ctx_size)])  12.6 us
    ppermute x2, starting transfers between devices, routed(): come = [lax.ppermute(part, 'head', swap_x) for part in parts]  9.01 us
    ppermute x2, waiting for transfers between devices, routed(): come = [lax.ppermute(part, 'head', swap_x) for part in parts]  8.71 us
    ppermute x2, waiting for transfers between devices, routed(): hop_1 = lax.ppermute(block, both, route(HOP_1))  7.2 us
    ppermute x7, waiting for transfers between devices, per_device(): lax.ppermute(piece, 'ctx', [(i, i ^ d) for i in range(ctx_size)])  6.91 us
    ppermute x2, starting transfers between devices, routed(): hop_1 = lax.ppermute(block, both, route(HOP_1))  5.71 us
    ppermute x2, waiting for transfers between devices, routed(): hop_2 = lax.ppermute(block, both, route(HOP_2))  5.62 us
  transfers between devices with their start and end apart: 25, of which 12 were waited for; matrix products, arithmetic and copies ran while one was open for 5% of the time, Pallas kernels for 23%

profile of v3, /device:TPU:0, one launch (start us, length us, event | category | flops | bytes accessed | tf_op | source)
XLA Modules:
  0.0 118.1 jit_solution(15067495421513602074)
XLA Ops:
  0.0 0.7 convert_element_type.27
  0.8 0.5 fusion.8
  1.5 0.9 copy-done.2
  2.4 0.9 copy-done.3
  3.3 0.6 pack.1
  4.0 3.0 %collective-permute-start = (bf16[128,256]{1,0:T(8,128)(2,1)S(1)}, bf16[128,256]{1,0:T(8,128)(2,1)S(1)}, u32[]{:S(2)}, u32[]{:S(2)}) collective-permute-start(bf16[128,256]{1,0:T(8,128)(2,1)S(1)} %pack.1), channel_id=1, source_target_pairs={{0,4},{4,0},{8,12},{12,8},{16,20},{20,16},{24,28},{28,24},{1,5},{5... | collective-permute-start | bytes 196616 | tf_op jit(solution)/shard_map/ppermute | solution.py:286
  7.0 1.6 %collective-permute-start.1 = (bf16[128,256]{1,0:T(8,128)(2,1)S(1)}, bf16[128,256]{1,0:T(8,128)(2,1)S(1)}, u32[]{:S(2)}, u32[]{:S(2)}) collective-permute-start(bf16[128,256]{1,0:T(8,128)(2,1)S(1)} %pack.1), channel_id=1, source_target_pairs={{0,8},{4,12},{8,0},{12,4},{16,24},{20,28},{24,16},{28,20},{1,9},{5... | collective-permute-start | bytes 196616 | tf_op jit(solution)/shard_map/ppermute | solution.py:286
  8.6 3.0 %collective-permute-start.3 = (bf16[128,256]{1,0:T(8,128)(2,1)S(1)}, bf16[128,256]{1,0:T(8,128)(2,1)S(1)}, u32[]{:S(2)}, u32[]{:S(2)}) collective-permute-start(bf16[128,256]{1,0:T(8,128)(2,1)S(1)} %pack.1), channel_id=1, source_target_pairs={{0,16},{4,20},{8,24},{12,28},{16,0},{20,4},{24,8},{28,12},{1,17},{... | collective-permute-start | bytes 196616 | tf_op jit(solution)/shard_map/ppermute | solution.py:286
  11.6 1.3 %collective-permute-start.4 = (bf16[128,256]{1,0:T(8,128)(2,1)S(1)}, bf16[128,256]{1,0:T(8,128)(2,1)S(1)}, u32[]{:S(2)}, u32[]{:S(2)}) collective-permute-start(bf16[128,256]{1,0:T(8,128)(2,1)S(1)} %pack.1), channel_id=1, source_target_pairs={{0,20},{4,16},{8,28},{12,24},{16,4},{20,0},{24,12},{28,8},{1,21},{... | collective-permute-start | bytes 196616 | tf_op jit(solution)/shard_map/ppermute | solution.py:286
  12.9 0.7 pad_add_fusion
  14.2 3.7 %collective-permute-start.5 = (bf16[128,256]{1,0:T(8,128)(2,1)S(1)}, bf16[128,256]{1,0:T(8,128)(2,1)S(1)}, u32[]{:S(2)}, u32[]{:S(2)}) collective-permute-start(bf16[128,256]{1,0:T(8,128)(2,1)S(1)} %pack.1), channel_id=1, source_target_pairs={{0,24},{4,28},{8,16},{12,20},{16,8},{20,12},{24,0},{28,4},{1,25},{... | collective-permute-start | bytes 196616 | tf_op jit(solution)/shard_map/ppermute | solution.py:286
  18.0 2.6 %collective-permute-done.4 = bf16[128,256]{1,0:T(8,128)(2,1)S(1)} collective-permute-done((bf16[128,256]{1,0:T(8,128)(2,1)S(1)}, bf16[128,256]{1,0:T(8,128)(2,1)S(1)}, u32[]{:S(2)}, u32[]{:S(2)}) %collective-permute-start.4) | collective-permute-done | bytes 65568 | tf_op jit(solution)/shard_map/ppermute | solution.py:286
  20.6 4.2 %collective-permute-done.6 = bf16[128,256]{1,0:T(8,128)(2,1)S(1)} collective-permute-done((bf16[128,256]{1,0:T(8,128)(2,1)S(1)}, bf16[128,256]{1,0:T(8,128)(2,1)S(1)}, u32[]{:S(2)}, u32[]{:S(2)}) %collective-permute-start.6) | collective-permute-done | bytes 65568 | tf_op jit(solution)/shard_map/ppermute | solution.py:286
  24.9 1.9 %collective-permute-done.7.other = bf16[1024,256]{1,0:T(8,128)(2,1)S(1)} collective-permute-done((bf16[1024,256]{1,0:T(8,128)(2,1)S(1)}, bf16[1024,256]{1,0:T(8,128)(2,1)S(1)}, u32[]{:S(2)}, u32[]{:S(2)}) %collective-permute-start.7) | collective-permute-done | bytes 524320 | tf_op jit(solution)/shard_map/ppermute | solution.py:293
  26.8 4.2 %attention.1 = (bf16[128,1024]{1,0:T(8,128)(2,1)S(1)}, bf16[128,1024]{1,0:T(8,128)(2,1)S(1)}) custom-call(s32[66]{0:T(128)S(1)} %pad_add_fusion.2.table, bf16[256,1024]{1,0:T(8,128)(2,1)S(1)} %turn.1.queries, bf16[1024,256]{1,0:T(8,128)(2,1)S(1)} %constant_dynamic-update-slice_fusion.own, bf16[1024,256]{1,0:T(8,128)(2,1)S(1)} %collective-permute-done.7.other), custom_call_target="tpu_custom_call" | custom-call | tf_op jit(solution)/shard_map/attention/pallas_call | solution.py:141
  31.2 1.4 %collective-permute-done.8 = bf16[128,1024]{1,0:T(8,128)(2,1)S(1)} collective-permute-done((bf16[128,1024]{1,0:T(8,128)(2,1)S(1)}, bf16[128,1024]{1,0:T(8,128)(2,1)S(1)}, u32[]{:S(2)}, u32[]{:S(2)}) %collective-permute-start.8) | collective-permute-done | bytes 262176 | tf_op jit(solution)/shard_map/ppermute | solution.py:220
  32.6 1.3 %collective-permute-start.10 = (bf16[128,2048]{1,0:T(8,128)(2,1)S(1)}, bf16[128,2048]{1,0:T(8,128)(2,1)S(1)}, u32[]{:S(2)}, u32[]{:S(2)}) collective-permute-start(bf16[128,2048]{1,0:T(8,128)(2,1)S(1)} %constant_dynamic-update-slice_fusion.8), channel_id=1, source_target_pairs={{0,8},{2,18},{4,12},{6,22},{9,17},{11,3},{13,21},{15,7},{16,24},{1... | collective-permute-start | bytes 1572872 | tf_op jit(solution)/shard_map/ppermute | solution.py:222
  34.0 3.8 %collective-permute-start.9 = (bf16[128,2048]{1,0:T(8,128)(2,1)S(1)}, bf16[128,2048]{1,0:T(8,128)(2,1)S(1)}, u32[]{:S(2)}, u32[]{:S(2)}) collective-permute-start(bf16[128,2048]{1,0:T(8,128)(2,1)S(1)} %constant_dynamic-update-slice_fusion.8), channel_id=1, source_target_pairs={{0,16},{2,10},{4,20},{6,14},{9,1},{11,19},{13,5},{15,23},{16,8},{1... | collective-permute-start | bytes 1572872 | tf_op jit(solution)/shard_map/ppermute | solution.py:221
  37.9 0.7 constant_dynamic-update-slice_fusion.11
  38.6 0.8 collective-permute-done.12
  39.4 0.7 constant_dynamic-update-slice_fusion.10
  40.1 1.9 %collective-permute-start.13 = (bf16[128,2048]{1,0:T(8,128)(2,1)}, bf16[128,2048]{1,0:T(8,128)(2,1)S(1)}, u32[]{:S(2)}, u32[]{:S(2)}) collective-permute-start(bf16[128,2048]{1,0:T(8,128)(2,1)} %constant_dynamic-update-slice_fusion.10), channel_id=1, source_target_pairs={{0,16},{2,10},{4,20},{6,14},{9,1},{11,19},{13,5},{15,23},{16,8},{1... | collective-permute-start | bytes 1572872 | tf_op jit(solution)/shard_map/ppermute | solution.py:221
  42.0 1.3 %collective-permute-start.14 = (bf16[128,2048]{1,0:T(8,128)(2,1)}, bf16[128,2048]{1,0:T(8,128)(2,1)S(1)}, u32[]{:S(2)}, u32[]{:S(2)}) collective-permute-start(bf16[128,2048]{1,0:T(8,128)(2,1)} %constant_dynamic-update-slice_fusion.10), channel_id=1, source_target_pairs={{0,8},{2,18},{4,12},{6,22},{9,17},{11,3},{13,21},{15,7},{16,24},{1... | collective-permute-start | bytes 1572872 | tf_op jit(solution)/shard_map/ppermute | solution.py:222
  43.4 2.9 %collective-permute-done.9 = bf16[128,2048]{1,0:T(8,128)(2,1)S(1)} collective-permute-done((bf16[128,2048]{1,0:T(8,128)(2,1)S(1)}, bf16[128,2048]{1,0:T(8,128)(2,1)S(1)}, u32[]{:S(2)}, u32[]{:S(2)}) %collective-permute-start.9) | collective-permute-done | bytes 524320 | tf_op jit(solution)/shard_map/ppermute | solution.py:221
  46.3 1.3 %collective-permute-start.11 = (bf16[128,2048]{1,0:T(8,128)(2,1)S(1)}, bf16[128,2048]{1,0:T(8,128)(2,1)S(1)}, u32[]{:S(2)}, u32[]{:S(2)}) collective-permute-start(bf16[128,2048]{1,0:T(8,128)(2,1)S(1)} %broadcast_select_fusion.1), channel_id=1, source_target_pairs={{8,0},{9,1},{10,2},{11,3},{12,4},{13,5},{14,6},{15,7},{16,24},{17,... | collective-permute-start | bytes 1572872 | tf_op jit(solution)/shard_map/ppermute | solution.py:226
  47.7 4.3 %collective-permute-done.13 = bf16[128,2048]{1,0:T(8,128)(2,1)S(1)} collective-permute-done((bf16[128,2048]{1,0:T(8,128)(2,1)}, bf16[128,2048]{1,0:T(8,128)(2,1)S(1)}, u32[]{:S(2)}, u32[]{:S(2)}) %collective-permute-start.13) | collective-permute-done | bytes 524320 | tf_op jit(solution)/shard_map/ppermute | solution.py:221
  52.0 5.6 %collective-permute-done.14 = bf16[128,2048]{1,0:T(8,128)(2,1)S(1)} collective-permute-done((bf16[128,2048]{1,0:T(8,128)(2,1)}, bf16[128,2048]{1,0:T(8,128)(2,1)S(1)}, u32[]{:S(2)}, u32[]{:S(2)}) %collective-permute-start.14) | collective-permute-done | bytes 524320 | tf_op jit(solution)/shard_map/ppermute | solution.py:222
  57.7 1.7 %collective-permute-start.15 = (bf16[128,2048]{1,0:T(8,128)(2,1)S(1)}, bf16[128,2048]{1,0:T(8,128)(2,1)S(1)}, u32[]{:S(2)}, u32[]{:S(2)}) collective-permute-start(bf16[128,2048]{1,0:T(8,128)(2,1)S(1)} %broadcast_select_fusion), channel_id=1, source_target_pairs={{8,0},{9,1},{10,2},{11,3},{12,4},{13,5},{14,6},{15,7},{16,24},{17,... | collective-permute-start | bytes 1572872 | tf_op jit(solution)/shard_map/ppermute | solution.py:226
  59.4 2.3 %collective-permute-done.11 = bf16[128,2048]{1,0:T(8,128)(2,1)S(1)} collective-permute-done((bf16[128,2048]{1,0:T(8,128)(2,1)S(1)}, bf16[128,2048]{1,0:T(8,128)(2,1)S(1)}, u32[]{:S(2)}, u32[]{:S(2)}) %collective-permute-start.11) | collective-permute-done | bytes 524320 | tf_op jit(solution)/shard_map/ppermute | solution.py:226
  61.8 1.2 broadcast_select_fusion.7
  63.0 1.6 %collective-permute-start.19 = (bf16[128,2048]{1,0:T(8,128)(2,1)S(1)}, bf16[128,2048]{1,0:T(8,128)(2,1)S(1)}, u32[]{:S(2)}, u32[]{:S(2)}) collective-permute-start(bf16[128,2048]{1,0:T(8,128)(2,1)S(1)} %broadcast_select_fusion.6.rows), channel_id=1, source_target_pairs={{0,4},{4,0},{8,12},{12,8},{16,20},{20,16},{24,28},{28,24},{1,5},{5... | collective-permute-start | bytes 1572872 | tf_op jit(solution)/shard_map/ppermute | solution.py:235
  64.6 3.4 %project.6 = bf16[128,2048]{1,0:T(8,128)(2,1)S(1)} custom-call(bf16[128,2048]{1,0:T(8,128)(2,1)S(1)} %broadcast_select_fusion.6.rows, bf16[1024,2048]{1,0:T(8,128)(2,1)S(1)} %copy-done, bf16[1024,2048]{1,0:T(8,128)(2,1)} %collective-permute-done.16.other), custom_call_target="tpu_custom_call" | custom-call | flops 1073741824 | bytes 1048576 | tf_op jit(solution)/shard_map/project/pallas_call | solution.py:172
  68.1 8.2 %collective-permute-start.20 = (bf16[128,2048]{1,0:T(8,128)(2,1)S(1)}, bf16[128,2048]{1,0:T(8,128)(2,1)S(1)}, u32[]{:S(2)}, u32[]{:S(2)}) collective-permute-start(bf16[128,2048]{1,0:T(8,128)(2,1)S(1)} %project.6), channel_id=1, source_target_pairs={{0,2},{1,3},{2,0},{3,1},{4,6},{5,7},{6,4},{7,5},{8,10},{9,11},{10,... | collective-permute-start | bytes 1572872 | tf_op jit(solution)/shard_map/ppermute | solution.py:236
  76.3 1.2 broadcast_select_fusion.4
  77.6 3.4 %project.7 = bf16[128,2048]{1,0:T(8,128)(2,1)S(1)} custom-call(bf16[128,2048]{1,0:T(8,128)(2,1)S(1)} %get-tuple-element.29.rows, bf16[1024,2048]{1,0:T(8,128)(2,1)S(1)} %copy-done, bf16[1024,2048]{1,0:T(8,128)(2,1)} %collective-permute-done.16.other), custom_call_target="tpu_custom_call" | custom-call | flops 1073741824 | bytes 1048576 | tf_op jit(solution)/shard_map/project/pallas_call | solution.py:172
  81.0 0.8 collective-permute-start.18
  81.8 1.3 %collective-permute-start.21 = (bf16[128,2048]{1,0:T(8,128)(2,1)S(1)}, bf16[128,2048]{1,0:T(8,128)(2,1)S(1)}, u32[]{:S(2)}, u32[]{:S(2)}) collective-permute-start(bf16[128,2048]{1,0:T(8,128)(2,1)S(1)} %get-tuple-element.26), channel_id=1, source_target_pairs={{0,4},{4,0},{8,12},{12,8},{16,20},{20,16},{24,28},{28,24},{1,5},{5... | collective-permute-start | bytes 1572872 | tf_op jit(solution)/shard_map/ppermute | solution.py:240
  83.2 0.8 collective-permute-start.22
  84.1 3.5 %collective-permute-done.20 = bf16[128,2048]{1,0:T(8,128)(2,1)S(1)} collective-permute-done((bf16[128,2048]{1,0:T(8,128)(2,1)S(1)}, bf16[128,2048]{1,0:T(8,128)(2,1)S(1)}, u32[]{:S(2)}, u32[]{:S(2)}) %collective-permute-start.20) | collective-permute-done | bytes 524320 | tf_op jit(solution)/shard_map/ppermute | solution.py:236
  87.6 3.5 %project.8 = bf16[128,2048]{1,0:T(8,128)(2,1)S(1)} custom-call(bf16[128,2048]{1,0:T(8,128)(2,1)S(1)} %collective-permute-done.19.rows, bf16[1024,2048]{1,0:T(8,128)(2,1)S(1)} %copy-done, bf16[1024,2048]{1,0:T(8,128)(2,1)} %collective-permute-done.16.other), custom_call_target="tpu_custom_call" | custom-call | flops 1073741824 | bytes 1048576 | tf_op jit(solution)/shard_map/project/pallas_call | solution.py:172
  91.1 2.5 %collective-permute-start.23 = (bf16[128,2048]{1,0:T(8,128)(2,1)S(1)}, bf16[128,2048]{1,0:T(8,128)(2,1)S(1)}, u32[]{:S(2)}, u32[]{:S(2)}) collective-permute-start(bf16[128,2048]{1,0:T(8,128)(2,1)S(1)} %project.8), channel_id=1, source_target_pairs={{0,2},{1,3},{2,0},{3,1},{4,6},{5,7},{6,4},{7,5},{8,10},{9,11},{10,... | collective-permute-start | bytes 1572872 | tf_op jit(solution)/shard_map/ppermute | solution.py:239
  93.6 5.2 %collective-permute-done.18 = bf16[128,2048]{1,0:T(8,128)(2,1)S(1)} collective-permute-done((bf16[128,2048]{1,0:T(8,128)(2,1)S(1)}, bf16[128,2048]{1,0:T(8,128)(2,1)S(1)}, u32[]{:S(2)}, u32[]{:S(2)}) %collective-permute-start.18) | collective-permute-done | bytes 524320 | tf_op jit(solution)/shard_map/ppermute | solution.py:236
  98.8 3.4 %project.9 = bf16[128,2048]{1,0:T(8,128)(2,1)S(1)} custom-call(bf16[128,2048]{1,0:T(8,128)(2,1)S(1)} %collective-permute-done.17.rows, bf16[1024,2048]{1,0:T(8,128)(2,1)S(1)} %copy-done, bf16[1024,2048]{1,0:T(8,128)(2,1)} %collective-permute-done.16.other), custom_call_target="tpu_custom_call" | custom-call | flops 1073741824 | bytes 1048576 | tf_op jit(solution)/shard_map/project/pallas_call | solution.py:172
  102.3 2.5 %collective-permute-start.24 = (bf16[128,2048]{1,0:T(8,128)(2,1)S(1)}, bf16[128,2048]{1,0:T(8,128)(2,1)S(1)}, u32[]{:S(2)}, u32[]{:S(2)}) collective-permute-start(bf16[128,2048]{1,0:T(8,128)(2,1)S(1)} %project.9), channel_id=1, source_target_pairs={{0,2},{1,3},{2,0},{3,1},{4,6},{5,7},{6,4},{7,5},{8,10},{9,11},{10,... | collective-permute-start | bytes 1572872 | tf_op jit(solution)/shard_map/ppermute | solution.py:239
  104.8 4.5 %project.10 = f32[256,2048]{1,0:T(8,128)S(1)} custom-call(bf16[256,2048]{1,0:T(8,128)(2,1)S(1)} %pad_maximum_fusion.rows, bf16[1024,2048]{1,0:T(8,128)(2,1)S(1)} %copy-done, bf16[1024,2048]{1,0:T(8,128)(2,1)} %collective-permute-done.16.other), custom_call_target="tpu_custom_call" | custom-call | flops 2147483648 | bytes 2097152 | tf_op jit(solution)/shard_map/project/pallas_call | solution.py:172
  110.0 4.5 %project.11 = f32[256,2048]{1,0:T(8,128)S(1)} custom-call(bf16[256,2048]{1,0:T(8,128)(2,1)S(1)} %pad_maximum_fusion.1.rows, bf16[1024,2048]{1,0:T(8,128)(2,1)S(1)} %copy-done, bf16[1024,2048]{1,0:T(8,128)(2,1)} %collective-permute-done.16.other), custom_call_target="tpu_custom_call" | custom-call | flops 2147483648 | bytes 2097152 | tf_op jit(solution)/shard_map/project/pallas_call | solution.py:172
  114.6 2.5 %collective-permute-done.24 = bf16[128,2048]{1,0:T(8,128)(2,1)S(1)} collective-permute-done((bf16[128,2048]{1,0:T(8,128)(2,1)S(1)}, bf16[128,2048]{1,0:T(8,128)(2,1)S(1)}, u32[]{:S(2)}, u32[]{:S(2)}) %collective-permute-start.24) | collective-permute-done | bytes 524320 | tf_op jit(solution)/shard_map/ppermute | solution.py:239
  117.2 0.9 fusion.7
  (57 shorter events, 2.4 us)
Async XLA Ops:
  0.0 13.7 %copy-start.1 = (bf16[256,1024]{1,0:T(8,128)(2,1)S(1)}, bf16[256,1024]{1,0:T(8,128)(2,1)}, u32[]{:S(2)}) copy-start(bf16[256,1024]{1,0:T(8,128)(2,1)} %queries.1) | copy-start | bytes 1572868
  1.5 0.9 copy-start.2
  2.4 0.9 copy-start.3
  4.0 10.1 %collective-permute-start = (bf16[128,256]{1,0:T(8,128)(2,1)S(1)}, bf16[128,256]{1,0:T(8,128)(2,1)S(1)}, u32[]{:S(2)}, u32[]{:S(2)}) collective-permute-start(bf16[128,256]{1,0:T(8,128)(2,1)S(1)} %pack.1), channel_id=1, source_target_pairs={{0,4},{4,0},{8,12},{12,8},{16,20},{20,16},{24,28},{28,24},{1,5},{5... | collective-permute-start | bytes 196616 | tf_op jit(solution)/shard_map/ppermute | solution.py:286
  7.0 7.2 %collective-permute-start.1 = (bf16[128,256]{1,0:T(8,128)(2,1)S(1)}, bf16[128,256]{1,0:T(8,128)(2,1)S(1)}, u32[]{:S(2)}, u32[]{:S(2)}) collective-permute-start(bf16[128,256]{1,0:T(8,128)(2,1)S(1)} %pack.1), channel_id=1, source_target_pairs={{0,8},{4,12},{8,0},{12,4},{16,24},{20,28},{24,16},{28,20},{1,9},{5... | collective-permute-start | bytes 196616 | tf_op jit(solution)/shard_map/ppermute | solution.py:286
  8.6 9.3 %collective-permute-start.2 = (bf16[128,256]{1,0:T(8,128)(2,1)S(1)}, bf16[128,256]{1,0:T(8,128)(2,1)S(1)}, u32[]{:S(2)}, u32[]{:S(2)}) collective-permute-start(bf16[128,256]{1,0:T(8,128)(2,1)S(1)} %pack.1), channel_id=1, source_target_pairs={{0,12},{4,8},{8,4},{12,0},{16,28},{20,24},{24,20},{28,16},{1,13},{... | collective-permute-start | bytes 196616 | tf_op jit(solution)/shard_map/ppermute | solution.py:286
  8.6 9.4 %collective-permute-start.3 = (bf16[128,256]{1,0:T(8,128)(2,1)S(1)}, bf16[128,256]{1,0:T(8,128)(2,1)S(1)}, u32[]{:S(2)}, u32[]{:S(2)}) collective-permute-start(bf16[128,256]{1,0:T(8,128)(2,1)S(1)} %pack.1), channel_id=1, source_target_pairs={{0,16},{4,20},{8,24},{12,28},{16,0},{20,4},{24,8},{28,12},{1,17},{... | collective-permute-start | bytes 196616 | tf_op jit(solution)/shard_map/ppermute | solution.py:286
  11.6 9.0 %collective-permute-start.4 = (bf16[128,256]{1,0:T(8,128)(2,1)S(1)}, bf16[128,256]{1,0:T(8,128)(2,1)S(1)}, u32[]{:S(2)}, u32[]{:S(2)}) collective-permute-start(bf16[128,256]{1,0:T(8,128)(2,1)S(1)} %pack.1), channel_id=1, source_target_pairs={{0,20},{4,16},{8,28},{12,24},{16,4},{20,0},{24,12},{28,8},{1,21},{... | collective-permute-start | bytes 196616 | tf_op jit(solution)/shard_map/ppermute | solution.py:286
  14.1 50.5 %collective-permute-start.16 = (bf16[1024,2048]{1,0:T(8,128)(2,1)}, bf16[1024,2048]{1,0:T(8,128)(2,1)}, u32[]{:S(2)}, u32[]{:S(2)}) collective-permute-start(bf16[1024,2048]{1,0:T(8,128)(2,1)} %own.11), channel_id=1, source_target_pairs={{0,1},{1,0},{2,3},{3,2},{4,5},{5,4},{6,7},{7,6},{8,9},{9,8},{10,11... | collective-permute-start | bytes 12582920 | tf_op jit(solution)/shard_map/ppermute | solution.py:213
  14.2 6.5 %collective-permute-start.5 = (bf16[128,256]{1,0:T(8,128)(2,1)S(1)}, bf16[128,256]{1,0:T(8,128)(2,1)S(1)}, u32[]{:S(2)}, u32[]{:S(2)}) collective-permute-start(bf16[128,256]{1,0:T(8,128)(2,1)S(1)} %pack.1), channel_id=1, source_target_pairs={{0,24},{4,28},{8,16},{12,20},{16,8},{20,12},{24,0},{28,4},{1,25},{... | collective-permute-start | bytes 196616 | tf_op jit(solution)/shard_map/ppermute | solution.py:286
  17.8 7.0 %collective-permute-start.6 = (bf16[128,256]{1,0:T(8,128)(2,1)S(1)}, bf16[128,256]{1,0:T(8,128)(2,1)S(1)}, u32[]{:S(2)}, u32[]{:S(2)}) collective-permute-start(bf16[128,256]{1,0:T(8,128)(2,1)S(1)} %pack.1), channel_id=1, source_target_pairs={{0,28},{4,24},{8,20},{12,16},{16,12},{20,8},{24,4},{28,0},{1,29},{... | collective-permute-start | bytes 196616 | tf_op jit(solution)/shard_map/ppermute | solution.py:286
  24.9 1.9 %collective-permute-start.7 = (bf16[1024,256]{1,0:T(8,128)(2,1)S(1)}, bf16[1024,256]{1,0:T(8,128)(2,1)S(1)}, u32[]{:S(2)}, u32[]{:S(2)}) collective-permute-start(bf16[1024,256]{1,0:T(8,128)(2,1)S(1)} %constant_dynamic-update-slice_fusion.own), channel_id=1, source_target_pairs={{0,1},{1,0},{2,3},{3,2},{4,5},{5,4},{6,7},{7,6},{8,9},{9,8},{10,11... | collective-permute-start | bytes 1572872 | tf_op jit(solution)/shard_map/ppermute | solution.py:293
  31.0 1.6 %collective-permute-start.8 = (bf16[128,1024]{1,0:T(8,128)(2,1)S(1)}, bf16[128,1024]{1,0:T(8,128)(2,1)S(1)}, u32[]{:S(2)}, u32[]{:S(2)}) collective-permute-start(bf16[128,1024]{1,0:T(8,128)(2,1)S(1)} %get-tuple-element.20), channel_id=1, source_target_pairs={{0,1},{1,0},{2,3},{3,2},{4,5},{5,4},{6,7},{7,6},{8,9},{9,8},{10,11... | collective-permute-start | bytes 786440 | tf_op jit(solution)/shard_map/ppermute | solution.py:220
  32.6 10.7 %copy-start.5 = (bf16[128,2048]{1,0:T(8,128)(2,1)}, bf16[128,2048]{1,0:T(8,128)(2,1)S(1)}, u32[]{:S(2)}) copy-start(bf16[128,2048]{1,0:T(8,128)(2,1)S(1)} %constant_dynamic-update-slice_fusion.8) | copy-start | bytes 1572868
  32.6 10.7 %collective-permute-start.10 = (bf16[128,2048]{1,0:T(8,128)(2,1)S(1)}, bf16[128,2048]{1,0:T(8,128)(2,1)S(1)}, u32[]{:S(2)}, u32[]{:S(2)}) collective-permute-start(bf16[128,2048]{1,0:T(8,128)(2,1)S(1)} %constant_dynamic-update-slice_fusion.8), channel_id=1, source_target_pairs={{0,8},{2,18},{4,12},{6,22},{9,17},{11,3},{13,21},{15,7},{16,24},{1... | collective-permute-start | bytes 1572872 | tf_op jit(solution)/shard_map/ppermute | solution.py:222
  34.0 12.3 %collective-permute-start.9 = (bf16[128,2048]{1,0:T(8,128)(2,1)S(1)}, bf16[128,2048]{1,0:T(8,128)(2,1)S(1)}, u32[]{:S(2)}, u32[]{:S(2)}) collective-permute-start(bf16[128,2048]{1,0:T(8,128)(2,1)S(1)} %constant_dynamic-update-slice_fusion.8), channel_id=1, source_target_pairs={{0,16},{2,10},{4,20},{6,14},{9,1},{11,19},{13,5},{15,23},{16,8},{1... | collective-permute-start | bytes 1572872 | tf_op jit(solution)/shard_map/ppermute | solution.py:221
  37.8 1.6 %collective-permute-start.12 = (bf16[128,1024]{1,0:T(8,128)(2,1)S(1)}, bf16[128,1024]{1,0:T(8,128)(2,1)S(1)}, u32[]{:S(2)}, u32[]{:S(2)}) collective-permute-start(bf16[128,1024]{1,0:T(8,128)(2,1)S(1)} %get-tuple-element.21), channel_id=1, source_target_pairs={{0,1},{1,0},{2,3},{3,2},{4,5},{5,4},{6,7},{7,6},{8,9},{9,8},{10,11... | collective-permute-start | bytes 786440 | tf_op jit(solution)/shard_map/ppermute | solution.py:220
  40.1 11.9 %collective-permute-start.13 = (bf16[128,2048]{1,0:T(8,128)(2,1)}, bf16[128,2048]{1,0:T(8,128)(2,1)S(1)}, u32[]{:S(2)}, u32[]{:S(2)}) collective-permute-start(bf16[128,2048]{1,0:T(8,128)(2,1)} %constant_dynamic-update-slice_fusion.10), channel_id=1, source_target_pairs={{0,16},{2,10},{4,20},{6,14},{9,1},{11,19},{13,5},{15,23},{16,8},{1... | collective-permute-start | bytes 1572872 | tf_op jit(solution)/shard_map/ppermute | solution.py:221
  42.0 15.6 %collective-permute-start.14 = (bf16[128,2048]{1,0:T(8,128)(2,1)}, bf16[128,2048]{1,0:T(8,128)(2,1)S(1)}, u32[]{:S(2)}, u32[]{:S(2)}) collective-permute-start(bf16[128,2048]{1,0:T(8,128)(2,1)} %constant_dynamic-update-slice_fusion.10), channel_id=1, source_target_pairs={{0,8},{2,18},{4,12},{6,22},{9,17},{11,3},{13,21},{15,7},{16,24},{1... | collective-permute-start | bytes 1572872 | tf_op jit(solution)/shard_map/ppermute | solution.py:222
  46.3 15.4 %collective-permute-start.11 = (bf16[128,2048]{1,0:T(8,128)(2,1)S(1)}, bf16[128,2048]{1,0:T(8,128)(2,1)S(1)}, u32[]{:S(2)}, u32[]{:S(2)}) collective-permute-start(bf16[128,2048]{1,0:T(8,128)(2,1)S(1)} %broadcast_select_fusion.1), channel_id=1, source_target_pairs={{8,0},{9,1},{10,2},{11,3},{12,4},{13,5},{14,6},{15,7},{16,24},{17,... | collective-permute-start | bytes 1572872 | tf_op jit(solution)/shard_map/ppermute | solution.py:226
  57.7 6.9 %copy-start = (bf16[1024,2048]{1,0:T(8,128)(2,1)S(1)}, bf16[1024,2048]{1,0:T(8,128)(2,1)}, u32[]{:S(2)}) copy-start(bf16[1024,2048]{1,0:T(8,128)(2,1)} %own.11) | copy-start | bytes 12582916
  57.7 18.6 %collective-permute-start.15 = (bf16[128,2048]{1,0:T(8,128)(2,1)S(1)}, bf16[128,2048]{1,0:T(8,128)(2,1)S(1)}, u32[]{:S(2)}, u32[]{:S(2)}) collective-permute-start(bf16[128,2048]{1,0:T(8,128)(2,1)S(1)} %broadcast_select_fusion), channel_id=1, source_target_pairs={{8,0},{9,1},{10,2},{11,3},{12,4},{13,5},{14,6},{15,7},{16,24},{17,... | collective-permute-start | bytes 1572872 | tf_op jit(solution)/shard_map/ppermute | solution.py:226
  63.0 20.2 %collective-permute-start.19 = (bf16[128,2048]{1,0:T(8,128)(2,1)S(1)}, bf16[128,2048]{1,0:T(8,128)(2,1)S(1)}, u32[]{:S(2)}, u32[]{:S(2)}) collective-permute-start(bf16[128,2048]{1,0:T(8,128)(2,1)S(1)} %broadcast_select_fusion.6.rows), channel_id=1, source_target_pairs={{0,4},{4,0},{8,12},{12,8},{16,20},{20,16},{24,28},{28,24},{1,5},{5... | collective-permute-start | bytes 1572872 | tf_op jit(solution)/shard_map/ppermute | solution.py:235
  68.1 19.5 %collective-permute-start.20 = (bf16[128,2048]{1,0:T(8,128)(2,1)S(1)}, bf16[128,2048]{1,0:T(8,128)(2,1)S(1)}, u32[]{:S(2)}, u32[]{:S(2)}) collective-permute-start(bf16[128,2048]{1,0:T(8,128)(2,1)S(1)} %project.6), channel_id=1, source_target_pairs={{0,2},{1,3},{2,0},{3,1},{4,6},{5,7},{6,4},{7,5},{8,10},{9,11},{10,... | collective-permute-start | bytes 1572872 | tf_op jit(solution)/shard_map/ppermute | solution.py:236
  77.5 21.4 %collective-permute-start.17 = (bf16[128,2048]{1,0:T(8,128)(2,1)S(1)}, bf16[128,2048]{1,0:T(8,128)(2,1)S(1)}, u32[]{:S(2)}, u32[]{:S(2)}) collective-permute-start(bf16[128,2048]{1,0:T(8,128)(2,1)S(1)} %get-tuple-element.29.rows), channel_id=1, source_target_pairs={{0,4},{4,0},{8,12},{12,8},{16,20},{20,16},{24,28},{28,24},{1,5},{5... | collective-permute-start | bytes 1572872 | tf_op jit(solution)/shard_map/ppermute | solution.py:235
  81.0 17.8 %collective-permute-start.18 = (bf16[128,2048]{1,0:T(8,128)(2,1)S(1)}, bf16[128,2048]{1,0:T(8,128)(2,1)S(1)}, u32[]{:S(2)}, u32[]{:S(2)}) collective-permute-start(bf16[128,2048]{1,0:T(8,128)(2,1)S(1)} %project.7), channel_id=1, source_target_pairs={{0,2},{1,3},{2,0},{3,1},{4,6},{5,7},{6,4},{7,5},{8,10},{9,11},{10,... | collective-permute-start | bytes 1572872 | tf_op jit(solution)/shard_map/ppermute | solution.py:236
  81.8 27.5 %collective-permute-start.21 = (bf16[128,2048]{1,0:T(8,128)(2,1)S(1)}, bf16[128,2048]{1,0:T(8,128)(2,1)S(1)}, u32[]{:S(2)}, u32[]{:S(2)}) collective-permute-start(bf16[128,2048]{1,0:T(8,128)(2,1)S(1)} %get-tuple-element.26), channel_id=1, source_target_pairs={{0,4},{4,0},{8,12},{12,8},{16,20},{20,16},{24,28},{28,24},{1,5},{5... | collective-permute-start | bytes 1572872 | tf_op jit(solution)/shard_map/ppermute | solution.py:240
  83.2 26.1 %collective-permute-start.22 = (bf16[128,2048]{1,0:T(8,128)(2,1)S(1)}, bf16[128,2048]{1,0:T(8,128)(2,1)S(1)}, u32[]{:S(2)}, u32[]{:S(2)}) collective-permute-start(bf16[128,2048]{1,0:T(8,128)(2,1)S(1)} %broadcast_select_fusion.5), channel_id=1, source_target_pairs={{0,4},{4,0},{8,12},{12,8},{16,20},{20,16},{24,28},{28,24},{1,5},{5... | collective-permute-start | bytes 1572872 | tf_op jit(solution)/shard_map/ppermute | solution.py:240
  91.1 23.4 %collective-permute-start.23 = (bf16[128,2048]{1,0:T(8,128)(2,1)S(1)}, bf16[128,2048]{1,0:T(8,128)(2,1)S(1)}, u32[]{:S(2)}, u32[]{:S(2)}) collective-permute-start(bf16[128,2048]{1,0:T(8,128)(2,1)S(1)} %project.8), channel_id=1, source_target_pairs={{0,2},{1,3},{2,0},{3,1},{4,6},{5,7},{6,4},{7,5},{8,10},{9,11},{10,... | collective-permute-start | bytes 1572872 | tf_op jit(solution)/shard_map/ppermute | solution.py:239
  102.3 14.9 %collective-permute-start.24 = (bf16[128,2048]{1,0:T(8,128)(2,1)S(1)}, bf16[128,2048]{1,0:T(8,128)(2,1)S(1)}, u32[]{:S(2)}, u32[]{:S(2)}) collective-permute-start(bf16[128,2048]{1,0:T(8,128)(2,1)S(1)} %project.9), channel_id=1, source_target_pairs={{0,2},{1,3},{2,0},{3,1},{4,6},{5,7},{6,4},{7,5},{8,10},{9,11},{10,... | collective-permute-start | bytes 1572872 | tf_op jit(solution)/shard_map/ppermute | solution.py:239
  114.6 2.5 %copy-start.4 = (bf16[512,2048]{1,0:T(8,128)(2,1)}, bf16[512,2048]{1,0:T(8,128)(2,1)S(1)}, u32[]{:S(2)}) copy-start(bf16[512,2048]{1,0:T(8,128)(2,1)S(1)} %fusion.6) | copy-start | bytes 6291460

commit v4 on v2

--- a/solution.py
+++ b/solution.py
@@ -13,9 +13,30 @@
 BLK = 128
 NEG = -1e30
 GRANT = 20 << 20
+BEFORE = {'hop_3_out_1': ('part_0',),
+ 'kept_out_0': ('part_1',),
+ 'kept_out_1': ('part_1',),
+ 'own_0': ('part_3',),
+ 'own_1': ('own_done_0',),
+ 'sent_2': ('come_0', 'part_1'),
+ 'sent_3': ('come_1', 'part_2'),
+ 'sent_out_1': ('sent_y_0',)}
 SCALE = math.log2(math.e) / math.sqrt(HD)
 VMEM = pl.BlockSpec(memory_space=pltpu.VMEM)
 SMEM = pl.BlockSpec(memory_space=pltpu.SMEM)
+
+
+class Ordered:
+    def __init__(self):
+        self.made = {}
+
+    def put(self, name, value):
+        self.made[name] = value
+        return value
+
+    def get(self, name, value):
+        others = [self.made[other] for other in BEFORE.get(name, ()) if other in self.made]
+        return lax.optimization_barrier((value, others))[0] if others else value
 
 
 def rotation_tables(positions):
@@ -156,6 +177,29 @@
     )(table, queries, own, other)
 
 
+def hold_kernel(own, other, own_out, other_out, semaphores):
+    copies = [
+        pltpu.make_async_copy(source, target, semaphores.at[i])
+        for i, (source, target) in enumerate(((own, own_out), (other, other_out)))
+    ]
+    for copy in copies:
+        copy.start()
+    for copy in copies:
+        copy.wait()
+
+
+def hold(own, other):
+    return pl.pallas_call(
+        hold_kernel,
+        in_specs=[pl.BlockSpec(memory_space=pl.ANY)] * 2,
+        out_specs=[VMEM] * 2,
+        out_shape=[pltpu.VMEM(own.shape, own.dtype), pltpu.VMEM(other.shape, other.dtype)],
+        scratch_shapes=[pltpu.SemaphoreType.DMA((2,))],
+        compiler_params=pltpu.CompilerParams(vmem_limit_bytes=GRANT),
+        name="hold",
+    )(own, other)
+
+
 def project_kernel(rows, own, other, out):
     depth, tile = own.shape[0], 512
     first, second = rows[:, :depth], rows[:, depth:]
@@ -200,7 +244,7 @@
 HOP_3 = {(1, 0): (0, 0), (1, 1): (0, 1), (2, 0): (3, 0), (2, 1): (3, 1)}
 
 
-def routed(halves, out_weight, ctx_index, head_index):
+def routed(order, halves, out_weight, ctx_index, head_index):
     both = ("ctx", "head")
     z, y, x, core = ctx_index // 2, ctx_index % 2, head_index // 2, head_index % 2
     far = jnp.where(x == 0, z, 3 - z)
@@ -208,35 +252,59 @@
     swap_core = [(i, i ^ 1) for i in range(4)]
     swap_x = [(i, i ^ 2) for i in range(4)]
     swap_y = [(i, i ^ 1) for i in range(8)]
-    weights = [
-        pltpu.with_memory_space_constraint(w, pltpu.VMEM)
-        for w in (out_weight, lax.ppermute(out_weight, "head", swap_core))
-    ]
     home, inner, first = z % 2 == core, (far == 1) | (far == 2), far >= 2
-
-    sent, kept = [], []
-    for half in halves:
+    count = len(halves)
+
+    hops, sent, kept, parts, come = [], [], [], [], []
+    for i, half in enumerate(halves):
+        half = order.get(f"half_{i}", half)
         block = jnp.concatenate([half, lax.ppermute(half, "head", swap_core)], axis=1)
+        order.put(f"block_{i}", block)
+        block = order.get(f"block_{i}", block)
         hop_1 = lax.ppermute(block, both, route(HOP_1))
         hop_2 = lax.ppermute(block, both, route(HOP_2))
-        passed = jnp.where(lane == 0, hop_1, hop_2)
-        hop_3 = lax.ppermute(passed, both, route(HOP_3))
+        order.put(f"hop_1_{i}", hop_1)
+        order.put(f"hop_2_{i}", hop_2)
+        hops.append((block, hop_1, hop_2))
+    other = lax.ppermute(order.get("weight", out_weight), "head", swap_core)
+    weights = [out_weight, order.put("weight", other)]
+    weights = hold(*order.get("hold", weights))
+    order.put("weights", weights)
+
+    def partial(rows, slot):
+        part = project(order.get(f"sent_{slot}", rows), *weights, jnp.bfloat16)
+        order.put(f"part_{slot}", part)
+        out = order.get(f"part_out_{slot}", part)
+        come.append(order.put(f"come_{slot}", lax.ppermute(out, "head", swap_x)))
+
+    for i, (block, hop_1, hop_2) in enumerate(hops):
+        passed = order.get(f"pass_{i}", jnp.where(lane == 0, hop_1, hop_2))
+        hop_3 = order.put(f"hop_3_{i}", lax.ppermute(passed, both, route(HOP_3)))
+        hop_3 = order.get(f"hop_3_out_{i}", hop_3)
         early = jnp.where(home, block, jnp.where(lane == 0, hop_2, hop_1))
         late = jnp.where(inner, passed, hop_3)
-        sent.append(jnp.where(first, early, late))
-        kept.append(jnp.where(first, late, early))
-    sent += [lax.ppermute(rows, "ctx", swap_y) for rows in sent]
-    kept += [lax.ppermute(rows, "ctx", swap_y) for rows in kept]
-    parts = [project(rows, *weights, jnp.bfloat16) for rows in sent]
-    come = [lax.ppermute(part, "head", swap_x) for part in parts]
-    kept, parts = lax.optimization_barrier((kept, parts))
-    own = [project(rows, *weights, jnp.float32) for rows in kept]
-    rows = BLK * len(halves)
-    out = jnp.zeros((2 * rows, out_weight.shape[1]), jnp.bfloat16)
-    for i, (mine, theirs) in enumerate(zip(own, come)):
+        sent.append(order.put(f"rows_{i}", jnp.where(first, early, late)))
+        kept.append(order.put(f"kept_{i}", jnp.where(first, late, early)))
+        partial(sent[i], i)
+    sent_y, kept_y = [], []
+    for i, rows in enumerate(sent):
+        out = order.get(f"sent_out_{i}", rows)
+        sent_y.append(order.put(f"sent_y_{i}", lax.ppermute(out, "ctx", swap_y)))
+    for i, rows in enumerate(kept):
+        out = order.get(f"kept_out_{i}", rows)
+        kept_y.append(order.put(f"kept_y_{i}", lax.ppermute(out, "ctx", swap_y)))
+    for i, rows in enumerate(sent_y):
+        partial(rows, count + i)
+    own = []
+    for i, rows in enumerate((kept, kept_y)):
+        rows = order.get(f"own_{i}", jnp.concatenate(rows, axis=0))
+        own.append(order.put(f"own_done_{i}", project(rows, *weights, jnp.float32)))
+    out = jnp.zeros((2 * count * BLK, out_weight.shape[1]), jnp.bfloat16)
+    for i, theirs in enumerate(come):
+        local, other_y = i % count, i // count
+        mine = own[other_y][local * BLK : (local + 1) * BLK]
         total = (mine + theirs.astype(jnp.float32)).astype(jnp.bfloat16)
-        local, other_y = i % len(halves), i // len(halves)
-        at = jnp.where(other_y == 0, y, 1 - y) * rows + local * BLK
+        at = (jnp.where(other_y == 0, y, 1 - y) * count + local) * BLK
         out = lax.dynamic_update_slice(out, total, (at, 0))
     return out
 
@@ -283,7 +351,7 @@
     other = lax.ppermute(own, "head", swap_core)
     halves = attend(table, at, *counts, rotated, own, other)
     if (ctx_size, head_size) == (8, 4):
-        return routed(halves, out_weight, ctx_index, head_index)
+        return routed(Ordered(), halves, out_weight, ctx_index, head_index)
     return collected(jnp.concatenate(halves, axis=0), out_weight)
 
 

time: 130 us -> 117 us (0.900)
  Pallas kernels: 33 us -> 17.3 us
  starting transfers between devices: 34 us -> 40.8 us
  local copies, waits for them, and re-layouts: 5.99 us -> 3.76 us
  waiting for transfers between devices: 50.1 us -> 48 us
    pallas_call x8 -> x6, Pallas kernels: 27.9 us -> 9.68 us  [project(): pl.pallas_call(project_kernel, in_specs=[VMEM] * 3, out_specs=VMEM, out_s...]
    ppermute x11, starting transfers between devices: 12.2 us -> 19.6 us  [the longest x4 12.4 us: partial(): come.append(order.put(f'come_{slot}', lax.ppermute(out, 'head', swap_x)))]
    ppermute x2, waiting for transfers between devices: 10.6 us -> 5.62 us  [routed(): hop_2 = lax.ppermute(block, both, route(HOP_2))]
    ppermute x2, waiting for transfers between devices: 4.36 us -> 7.21 us  [routed(): hop_1 = lax.ppermute(block, both, route(HOP_1))]
    pallas_call x0 -> x1, Pallas kernels: none -> 2.48 us  [hold(): pl.pallas_call(hold_kernel, in_specs=[pl.BlockSpec(memory_space=pl.ANY)]...]
    unnamed x29 -> x21, local copies, waits for them, and re-layouts: 4.8 us -> 2.62 us
  transfers between devices with their start and end apart: 25 -> 25, of which waited for: 14 -> 14; matrix products, arithmetic and copies ran while one was open for 4% -> 5% of each run, Pallas kernels for 25% -> 14%
where the time goes in v4:
time: 117 us
  waiting for transfers between devices  48 us (41%)
  starting transfers between devices  40.8 us (35%)
  Pallas kernels  17.3 us (15%)
  other arithmetic  6.3 us (5%)
  local copies, waits for them, and re-layouts  3.76 us (3%)
    ppermute x4, waiting for transfers between devices, partial(): come.append(order.put(f'come_{slot}', lax.ppermute(out, 'head', swap_x)))  14.8 us
    ppermute x7, starting transfers between devices, per_device(): lax.ppermute(piece, 'ctx', [(i, i ^ d) for i in range(ctx_size)])  12.6 us
    ppermute x4, starting transfers between devices, partial(): come.append(order.put(f'come_{slot}', lax.ppermute(out, 'head', swap_x)))  12.4 us
    pallas_call x6, Pallas kernels, project(): pl.pallas_call(project_kernel, in_specs=[VMEM] * 3, out_specs=VMEM, out_s...  9.68 us
    ppermute x2, waiting for transfers between devices, routed(): hop_1 = lax.ppermute(block, both, route(HOP_1))  7.21 us
    ppermute x7, waiting for transfers between devices, per_device(): lax.ppermute(piece, 'ctx', [(i, i ^ d) for i in range(ctx_size)])  6.91 us
    ppermute x2, waiting for transfers between devices, routed(): sent_y.append(order.put(f'sent_y_{i}', lax.ppermute(out, 'ctx', swap_y)))  6.65 us
    ppermute x2, starting transfers between devices, routed(): hop_1 = lax.ppermute(block, both, route(HOP_1))  5.71 us
  transfers between devices with their start and end apart: 25, of which 14 were waited for; matrix products, arithmetic and copies ran while one was open for 5% of the time, Pallas kernels for 14%

profile of v4, /device:TPU:0, one launch (start us, length us, event | category | flops | bytes accessed | tf_op | source)
XLA Modules:
  0.0 116.7 jit_solution(13367790524568873998)
XLA Ops:
  0.0 0.7 convert_element_type.27
  0.8 0.5 fusion.8
  1.5 0.9 copy-done.2
  2.4 0.9 copy-done.3
  3.3 0.6 pack.1
  4.0 3.0 %collective-permute-start = (bf16[128,256]{1,0:T(8,128)(2,1)S(1)}, bf16[128,256]{1,0:T(8,128)(2,1)S(1)}, u32[]{:S(2)}, u32[]{:S(2)}) collective-permute-start(bf16[128,256]{1,0:T(8,128)(2,1)S(1)} %pack.1), channel_id=1, source_target_pairs={{0,4},{4,0},{8,12},{12,8},{16,20},{20,16},{24,28},{28,24},{1,5},{5... | collective-permute-start | bytes 196616 | tf_op jit(solution)/shard_map/ppermute | solution.py:344
  7.0 1.6 %collective-permute-start.1 = (bf16[128,256]{1,0:T(8,128)(2,1)S(1)}, bf16[128,256]{1,0:T(8,128)(2,1)S(1)}, u32[]{:S(2)}, u32[]{:S(2)}) collective-permute-start(bf16[128,256]{1,0:T(8,128)(2,1)S(1)} %pack.1), channel_id=1, source_target_pairs={{0,8},{4,12},{8,0},{12,4},{16,24},{20,28},{24,16},{28,20},{1,9},{5... | collective-permute-start | bytes 196616 | tf_op jit(solution)/shard_map/ppermute | solution.py:344
  8.6 3.0 %collective-permute-start.3 = (bf16[128,256]{1,0:T(8,128)(2,1)S(1)}, bf16[128,256]{1,0:T(8,128)(2,1)S(1)}, u32[]{:S(2)}, u32[]{:S(2)}) collective-permute-start(bf16[128,256]{1,0:T(8,128)(2,1)S(1)} %pack.1), channel_id=1, source_target_pairs={{0,16},{4,20},{8,24},{12,28},{16,0},{20,4},{24,8},{28,12},{1,17},{... | collective-permute-start | bytes 196616 | tf_op jit(solution)/shard_map/ppermute | solution.py:344
  11.6 1.3 %collective-permute-start.4 = (bf16[128,256]{1,0:T(8,128)(2,1)S(1)}, bf16[128,256]{1,0:T(8,128)(2,1)S(1)}, u32[]{:S(2)}, u32[]{:S(2)}) collective-permute-start(bf16[128,256]{1,0:T(8,128)(2,1)S(1)} %pack.1), channel_id=1, source_target_pairs={{0,20},{4,16},{8,28},{12,24},{16,4},{20,0},{24,12},{28,8},{1,21},{... | collective-permute-start | bytes 196616 | tf_op jit(solution)/shard_map/ppermute | solution.py:344
  12.9 0.7 pad_add_fusion
  14.2 3.7 %collective-permute-start.5 = (bf16[128,256]{1,0:T(8,128)(2,1)S(1)}, bf16[128,256]{1,0:T(8,128)(2,1)S(1)}, u32[]{:S(2)}, u32[]{:S(2)}) collective-permute-start(bf16[128,256]{1,0:T(8,128)(2,1)S(1)} %pack.1), channel_id=1, source_target_pairs={{0,24},{4,28},{8,16},{12,20},{16,8},{20,12},{24,0},{28,4},{1,25},{... | collective-permute-start | bytes 196616 | tf_op jit(solution)/shard_map/ppermute | solution.py:344
  18.0 2.6 %collective-permute-done.4 = bf16[128,256]{1,0:T(8,128)(2,1)S(1)} collective-permute-done((bf16[128,256]{1,0:T(8,128)(2,1)S(1)}, bf16[128,256]{1,0:T(8,128)(2,1)S(1)}, u32[]{:S(2)}, u32[]{:S(2)}) %collective-permute-start.4) | collective-permute-done | bytes 65568 | tf_op jit(solution)/shard_map/ppermute | solution.py:344
  20.6 4.2 %collective-permute-done.6 = bf16[128,256]{1,0:T(8,128)(2,1)S(1)} collective-permute-done((bf16[128,256]{1,0:T(8,128)(2,1)S(1)}, bf16[128,256]{1,0:T(8,128)(2,1)S(1)}, u32[]{:S(2)}, u32[]{:S(2)}) %collective-permute-start.6) | collective-permute-done | bytes 65568 | tf_op jit(solution)/shard_map/ppermute | solution.py:344
  24.9 1.9 %collective-permute-done.7.other = bf16[1024,256]{1,0:T(8,128)(2,1)S(1)} collective-permute-done((bf16[1024,256]{1,0:T(8,128)(2,1)S(1)}, bf16[1024,256]{1,0:T(8,128)(2,1)S(1)}, u32[]{:S(2)}, u32[]{:S(2)}) %collective-permute-start.7) | collective-permute-done | bytes 524320 | tf_op jit(solution)/shard_map/ppermute | solution.py:351
  26.8 4.2 %attention.1 = (bf16[128,1024]{1,0:T(8,128)(2,1)S(1)}, bf16[128,1024]{1,0:T(8,128)(2,1)S(1)}) custom-call(s32[66]{0:T(128)S(1)} %pad_add_fusion.2.table, bf16[256,1024]{1,0:T(8,128)(2,1)S(1)} %turn.1.queries, bf16[1024,256]{1,0:T(8,128)(2,1)S(1)} %constant_dynamic-update-slice_fusion.own, bf16[1024,256]{1,0:T(8,128)(2,1)S(1)} %collective-permute-done.7.other), custom_call_target="tpu_custom_call" | custom-call | tf_op jit(solution)/shard_map/attention/pallas_call | solution.py:162
  31.2 1.4 %collective-permute-done.8 = bf16[128,1024]{1,0:T(8,128)(2,1)S(1)} collective-permute-done((bf16[128,1024]{1,0:T(8,128)(2,1)S(1)}, bf16[128,1024]{1,0:T(8,128)(2,1)S(1)}, u32[]{:S(2)}, u32[]{:S(2)}) %collective-permute-start.8) | collective-permute-done | bytes 262176 | tf_op jit(solution)/shard_map/ppermute | solution.py:261
  32.6 1.3 %collective-permute-start.10 = (bf16[128,2048]{1,0:T(8,128)(2,1)S(1)}, bf16[128,2048]{1,0:T(8,128)(2,1)S(1)}, u32[]{:S(2)}, u32[]{:S(2)}) collective-permute-start(bf16[128,2048]{1,0:T(8,128)(2,1)S(1)} %constant_dynamic-update-slice_fusion.8), channel_id=1, source_target_pairs={{0,8},{2,18},{4,12},{6,22},{9,17},{11,3},{13,21},{15,7},{16,24},{1... | collective-permute-start | bytes 1572872 | tf_op jit(solution)/shard_map/ppermute | solution.py:265
  34.0 3.8 %collective-permute-start.9 = (bf16[128,2048]{1,0:T(8,128)(2,1)S(1)}, bf16[128,2048]{1,0:T(8,128)(2,1)S(1)}, u32[]{:S(2)}, u32[]{:S(2)}) collective-permute-start(bf16[128,2048]{1,0:T(8,128)(2,1)S(1)} %constant_dynamic-update-slice_fusion.8), channel_id=1, source_target_pairs={{0,16},{2,10},{4,20},{6,14},{9,1},{11,19},{13,5},{15,23},{16,8},{1... | collective-permute-start | bytes 1572872 | tf_op jit(solution)/shard_map/ppermute | solution.py:264
  37.9 0.7 constant_dynamic-update-slice_fusion.11
  38.6 0.8 collective-permute-done.12
  39.4 0.7 constant_dynamic-update-slice_fusion.10
  40.1 1.9 %collective-permute-start.13 = (bf16[128,2048]{1,0:T(8,128)(2,1)}, bf16[128,2048]{1,0:T(8,128)(2,1)S(1)}, u32[]{:S(2)}, u32[]{:S(2)}) collective-permute-start(bf16[128,2048]{1,0:T(8,128)(2,1)} %constant_dynamic-update-slice_fusion.10), channel_id=1, source_target_pairs={{0,16},{2,10},{4,20},{6,14},{9,1},{11,19},{13,5},{15,23},{16,8},{1... | collective-permute-start | bytes 1572872 | tf_op jit(solution)/shard_map/ppermute | solution.py:264
  42.0 1.3 %collective-permute-start.14 = (bf16[128,2048]{1,0:T(8,128)(2,1)}, bf16[128,2048]{1,0:T(8,128)(2,1)S(1)}, u32[]{:S(2)}, u32[]{:S(2)}) collective-permute-start(bf16[128,2048]{1,0:T(8,128)(2,1)} %constant_dynamic-update-slice_fusion.10), channel_id=1, source_target_pairs={{0,8},{2,18},{4,12},{6,22},{9,17},{11,3},{13,21},{15,7},{16,24},{1... | collective-permute-start | bytes 1572872 | tf_op jit(solution)/shard_map/ppermute | solution.py:265
  43.4 2.9 %collective-permute-done.9 = bf16[128,2048]{1,0:T(8,128)(2,1)S(1)} collective-permute-done((bf16[128,2048]{1,0:T(8,128)(2,1)S(1)}, bf16[128,2048]{1,0:T(8,128)(2,1)S(1)}, u32[]{:S(2)}, u32[]{:S(2)}) %collective-permute-start.9) | collective-permute-done | bytes 524320 | tf_op jit(solution)/shard_map/ppermute | solution.py:264
  46.3 1.3 %collective-permute-start.11 = (bf16[128,2048]{1,0:T(8,128)(2,1)S(1)}, bf16[128,2048]{1,0:T(8,128)(2,1)S(1)}, u32[]{:S(2)}, u32[]{:S(2)}) collective-permute-start(bf16[128,2048]{1,0:T(8,128)(2,1)S(1)} %broadcast_select_fusion.1), channel_id=1, source_target_pairs={{8,0},{9,1},{10,2},{11,3},{12,4},{13,5},{14,6},{15,7},{16,24},{17,... | collective-permute-start | bytes 1572872 | tf_op jit(solution)/shard_map/ppermute | solution.py:282
  47.7 4.3 %collective-permute-done.13 = bf16[128,2048]{1,0:T(8,128)(2,1)S(1)} collective-permute-done((bf16[128,2048]{1,0:T(8,128)(2,1)}, bf16[128,2048]{1,0:T(8,128)(2,1)S(1)}, u32[]{:S(2)}, u32[]{:S(2)}) %collective-permute-start.13) | collective-permute-done | bytes 524320 | tf_op jit(solution)/shard_map/ppermute | solution.py:264
  52.0 5.6 %collective-permute-done.14 = bf16[128,2048]{1,0:T(8,128)(2,1)S(1)} collective-permute-done((bf16[128,2048]{1,0:T(8,128)(2,1)}, bf16[128,2048]{1,0:T(8,128)(2,1)S(1)}, u32[]{:S(2)}, u32[]{:S(2)}) %collective-permute-start.14) | collective-permute-done | bytes 524320 | tf_op jit(solution)/shard_map/ppermute | solution.py:265
  57.7 1.7 %collective-permute-start.15 = (bf16[128,2048]{1,0:T(8,128)(2,1)S(1)}, bf16[128,2048]{1,0:T(8,128)(2,1)S(1)}, u32[]{:S(2)}, u32[]{:S(2)}) collective-permute-start(bf16[128,2048]{1,0:T(8,128)(2,1)S(1)} %broadcast_select_fusion), channel_id=1, source_target_pairs={{8,0},{9,1},{10,2},{11,3},{12,4},{13,5},{14,6},{15,7},{16,24},{17,... | collective-permute-start | bytes 1572872 | tf_op jit(solution)/shard_map/ppermute | solution.py:282
  59.4 2.3 %collective-permute-done.11 = bf16[128,2048]{1,0:T(8,128)(2,1)S(1)} collective-permute-done((bf16[128,2048]{1,0:T(8,128)(2,1)S(1)}, bf16[128,2048]{1,0:T(8,128)(2,1)S(1)}, u32[]{:S(2)}, u32[]{:S(2)}) %collective-permute-start.11) | collective-permute-done | bytes 524320 | tf_op jit(solution)/shard_map/ppermute | solution.py:282
  61.8 1.2 broadcast_select_fusion.7
  63.0 1.6 %collective-permute-start.17 = (bf16[128,2048]{1,0:T(8,128)(2,1)S(1)}, bf16[128,2048]{1,0:T(8,128)(2,1)S(1)}, u32[]{:S(2)}, u32[]{:S(2)}) collective-permute-start(bf16[128,2048]{1,0:T(8,128)(2,1)S(1)} %broadcast_select_fusion.6.rows), channel_id=1, source_target_pairs={{0,4},{4,0},{8,12},{12,8},{16,20},{20,16},{24,28},{28,24},{1,5},{5... | collective-permute-start | bytes 1572872 | tf_op jit(solution)/shard_map/ppermute | solution.py:292
  64.6 2.5 %hold.1 = (bf16[1024,2048]{1,0:T(8,128)(2,1)S(1)}, bf16[1024,2048]{1,0:T(8,128)(2,1)S(1)}) custom-call(bf16[1024,2048]{1,0:T(8,128)(2,1)S(1)} %copy-done, bf16[1024,2048]{1,0:T(8,128)(2,1)} %collective-permute-done.16.other), custom_call_target="tpu_custom_call" | custom-call | tf_op jit(solution)/shard_map/hold/pallas_call | solution.py:192
  67.1 1.3 %project.6 = bf16[128,2048]{1,0:T(8,128)(2,1)S(1)} custom-call(bf16[128,2048]{1,0:T(8,128)(2,1)S(1)} %broadcast_select_fusion.6.rows, bf16[1024,2048]{1,0:T(8,128)(2,1)S(1)} %get-tuple-element.25.own, bf16[1024,2048]{1,0:T(8,128)(2,1)S(1)} %get-tuple-element.26.other), custom_call_target="tpu_custom_call" | custom-call | flops 1073741824 | bytes 1048576 | tf_op jit(solution)/shard_map/project/pallas_call | solution.py:216
  68.4 8.2 %collective-permute-start.20 = (bf16[128,2048]{1,0:T(8,128)(2,1)S(1)}, bf16[128,2048]{1,0:T(8,128)(2,1)S(1)}, u32[]{:S(2)}, u32[]{:S(2)}) collective-permute-start(bf16[128,2048]{1,0:T(8,128)(2,1)S(1)} %project.6), channel_id=1, source_target_pairs={{0,2},{1,3},{2,0},{3,1},{4,6},{5,7},{6,4},{7,5},{8,10},{9,11},{10,... | collective-permute-start | bytes 1572872 | tf_op jit(solution)/shard_map/ppermute | solution.py:278
  76.6 1.2 %broadcast_select_fusion.4 = (bf16[128,2048]{1,0:T(8,128)(2,1)S(1)}, bf16[128,2048]{1,0:T(8,128)(2,1)S(1)}) fusion(pred[]{:T(512)S(6)} %ge.3, bf16[128,2048]{1,0:T(8,128)(2,1)S(1)} %broadcast_select_fusion, bf16[128,2048]{1,0:T(8,128)(2,1)S(1)} %collective-permute-done.15, pred[]{:T(512)S(6)} %or.3, ...), kind=kLoop, calls=%fused_computation.20 | loop fusion | flops 1048576 | bytes 3670020 | tf_op jit(solution)/shard_map/jit(_where)/select_n | solution.py:286
  77.8 1.3 %project.7 = bf16[128,2048]{1,0:T(8,128)(2,1)S(1)} custom-call(bf16[128,2048]{1,0:T(8,128)(2,1)S(1)} %get-tuple-element.28.rows, bf16[1024,2048]{1,0:T(8,128)(2,1)S(1)} %get-tuple-element.25.own, bf16[1024,2048]{1,0:T(8,128)(2,1)S(1)} %get-tuple-element.26.other), custom_call_target="tpu_custom_call" | custom-call | flops 1073741824 | bytes 1048576 | tf_op jit(solution)/shard_map/project/pallas_call | solution.py:216
  79.6 1.6 %collective-permute-start.18 = (bf16[128,2048]{1,0:T(8,128)(2,1)S(1)}, bf16[128,2048]{1,0:T(8,128)(2,1)S(1)}, u32[]{:S(2)}, u32[]{:S(2)}) collective-permute-start(bf16[128,2048]{1,0:T(8,128)(2,1)S(1)} %get-tuple-element.28.rows), channel_id=1, source_target_pairs={{0,4},{4,0},{8,12},{12,8},{16,20},{20,16},{24,28},{28,24},{1,5},{5... | collective-permute-start | bytes 1572872 | tf_op jit(solution)/shard_map/ppermute | solution.py:292
  81.8 7.6 %collective-permute-done.20 = bf16[128,2048]{1,0:T(8,128)(2,1)S(1)} collective-permute-done((bf16[128,2048]{1,0:T(8,128)(2,1)S(1)}, bf16[128,2048]{1,0:T(8,128)(2,1)S(1)}, u32[]{:S(2)}, u32[]{:S(2)}) %collective-permute-start.20) | collective-permute-done | bytes 524320 | tf_op jit(solution)/shard_map/ppermute | solution.py:278
  89.4 1.3 %project.8 = bf16[128,2048]{1,0:T(8,128)(2,1)S(1)} custom-call(bf16[128,2048]{1,0:T(8,128)(2,1)S(1)} %collective-permute-done.17.rows, bf16[1024,2048]{1,0:T(8,128)(2,1)S(1)} %get-tuple-element.25.own, bf16[1024,2048]{1,0:T(8,128)(2,1)S(1)} %get-tuple-element.26.other), custom_call_target="tpu_custom_call" | custom-call | flops 1073741824 | bytes 1048576 | tf_op jit(solution)/shard_map/project/pallas_call | solution.py:216
  90.7 2.1 %collective-permute-start.23 = (bf16[128,2048]{1,0:T(8,128)(2,1)S(1)}, bf16[128,2048]{1,0:T(8,128)(2,1)S(1)}, u32[]{:S(2)}, u32[]{:S(2)}) collective-permute-start(bf16[128,2048]{1,0:T(8,128)(2,1)S(1)} %project.8), channel_id=1, source_target_pairs={{0,2},{1,3},{2,0},{3,1},{4,6},{5,7},{6,4},{7,5},{8,10},{9,11},{10,... | collective-permute-start | bytes 1572872 | tf_op jit(solution)/shard_map/ppermute | solution.py:278
  92.8 5.8 %collective-permute-done.19 = bf16[128,2048]{1,0:T(8,128)(2,1)S(1)} collective-permute-done((bf16[128,2048]{1,0:T(8,128)(2,1)S(1)}, bf16[128,2048]{1,0:T(8,128)(2,1)S(1)}, u32[]{:S(2)}, u32[]{:S(2)}) %collective-permute-start.19) | collective-permute-done | bytes 524320 | tf_op jit(solution)/shard_map/ppermute | solution.py:278
  98.6 6.6 %collective-permute-done.18.rows = bf16[128,2048]{1,0:T(8,128)(2,1)S(1)} collective-permute-done((bf16[128,2048]{1,0:T(8,128)(2,1)S(1)}, bf16[128,2048]{1,0:T(8,128)(2,1)S(1)}, u32[]{:S(2)}, u32[]{:S(2)}) %collective-permute-start.18) | collective-permute-done | bytes 524320 | tf_op jit(solution)/shard_map/ppermute | solution.py:292
  105.3 1.3 %project.9 = bf16[128,2048]{1,0:T(8,128)(2,1)S(1)} custom-call(bf16[128,2048]{1,0:T(8,128)(2,1)S(1)} %collective-permute-done.18.rows, bf16[1024,2048]{1,0:T(8,128)(2,1)S(1)} %get-tuple-element.25.own, bf16[1024,2048]{1,0:T(8,128)(2,1)S(1)} %get-tuple-element.26.other), custom_call_target="tpu_custom_call" | custom-call | flops 1073741824 | bytes 1048576 | tf_op jit(solution)/shard_map/project/pallas_call | solution.py:216
  106.5 2.0 %collective-permute-start.24 = (bf16[128,2048]{1,0:T(8,128)(2,1)S(1)}, bf16[128,2048]{1,0:T(8,128)(2,1)S(1)}, u32[]{:S(2)}, u32[]{:S(2)}) collective-permute-start(bf16[128,2048]{1,0:T(8,128)(2,1)S(1)} %project.9), channel_id=1, source_target_pairs={{0,2},{1,3},{2,0},{3,1},{4,6},{5,7},{6,4},{7,5},{8,10},{9,11},{10,... | collective-permute-start | bytes 1572872 | tf_op jit(solution)/shard_map/ppermute | solution.py:278
  108.6 2.3 %project.10 = f32[256,2048]{1,0:T(8,128)S(1)} custom-call(bf16[256,2048]{1,0:T(8,128)(2,1)S(1)} %pad_maximum_fusion.rows, bf16[1024,2048]{1,0:T(8,128)(2,1)S(1)} %get-tuple-element.25.own, bf16[1024,2048]{1,0:T(8,128)(2,1)S(1)} %get-tuple-element.26.other), custom_call_target="tpu_custom_call" | custom-call | flops 2147483648 | bytes 2097152 | tf_op jit(solution)/shard_map/project/pallas_call | solution.py:216
  111.9 2.3 %project.11 = f32[256,2048]{1,0:T(8,128)S(1)} custom-call(bf16[256,2048]{1,0:T(8,128)(2,1)S(1)} %pad_maximum_fusion.1.rows, bf16[1024,2048]{1,0:T(8,128)(2,1)S(1)} %get-tuple-element.25.own, bf16[1024,2048]{1,0:T(8,128)(2,1)S(1)} %get-tuple-element.26.other), custom_call_target="tpu_custom_call" | custom-call | flops 2147483648 | bytes 2097152 | tf_op jit(solution)/shard_map/project/pallas_call | solution.py:216
  114.4 1.4 %collective-permute-done.24 = bf16[128,2048]{1,0:T(8,128)(2,1)S(1)} collective-permute-done((bf16[128,2048]{1,0:T(8,128)(2,1)S(1)}, bf16[128,2048]{1,0:T(8,128)(2,1)S(1)}, u32[]{:S(2)}, u32[]{:S(2)}) %collective-permute-start.24) | collective-permute-done | bytes 524320 | tf_op jit(solution)/shard_map/ppermute | solution.py:278
  115.8 0.9 fusion.7
  (58 shorter events, 3.8 us)
Async XLA Ops:
  0.0 13.7 %copy-start.1 = (bf16[256,1024]{1,0:T(8,128)(2,1)S(1)}, bf16[256,1024]{1,0:T(8,128)(2,1)}, u32[]{:S(2)}) copy-start(bf16[256,1024]{1,0:T(8,128)(2,1)} %queries.1) | copy-start | bytes 1572868
  1.5 0.9 copy-start.2
  2.4 0.9 copy-start.3
  4.0 10.1 %collective-permute-start = (bf16[128,256]{1,0:T(8,128)(2,1)S(1)}, bf16[128,256]{1,0:T(8,128)(2,1)S(1)}, u32[]{:S(2)}, u32[]{:S(2)}) collective-permute-start(bf16[128,256]{1,0:T(8,128)(2,1)S(1)} %pack.1), channel_id=1, source_target_pairs={{0,4},{4,0},{8,12},{12,8},{16,20},{20,16},{24,28},{28,24},{1,5},{5... | collective-permute-start | bytes 196616 | tf_op jit(solution)/shard_map/ppermute | solution.py:344
  7.0 7.2 %collective-permute-start.1 = (bf16[128,256]{1,0:T(8,128)(2,1)S(1)}, bf16[128,256]{1,0:T(8,128)(2,1)S(1)}, u32[]{:S(2)}, u32[]{:S(2)}) collective-permute-start(bf16[128,256]{1,0:T(8,128)(2,1)S(1)} %pack.1), channel_id=1, source_target_pairs={{0,8},{4,12},{8,0},{12,4},{16,24},{20,28},{24,16},{28,20},{1,9},{5... | collective-permute-start | bytes 196616 | tf_op jit(solution)/shard_map/ppermute | solution.py:344
  8.6 9.3 %collective-permute-start.2 = (bf16[128,256]{1,0:T(8,128)(2,1)S(1)}, bf16[128,256]{1,0:T(8,128)(2,1)S(1)}, u32[]{:S(2)}, u32[]{:S(2)}) collective-permute-start(bf16[128,256]{1,0:T(8,128)(2,1)S(1)} %pack.1), channel_id=1, source_target_pairs={{0,12},{4,8},{8,4},{12,0},{16,28},{20,24},{24,20},{28,16},{1,13},{... | collective-permute-start | bytes 196616 | tf_op jit(solution)/shard_map/ppermute | solution.py:344
  8.6 9.4 %collective-permute-start.3 = (bf16[128,256]{1,0:T(8,128)(2,1)S(1)}, bf16[128,256]{1,0:T(8,128)(2,1)S(1)}, u32[]{:S(2)}, u32[]{:S(2)}) collective-permute-start(bf16[128,256]{1,0:T(8,128)(2,1)S(1)} %pack.1), channel_id=1, source_target_pairs={{0,16},{4,20},{8,24},{12,28},{16,0},{20,4},{24,8},{28,12},{1,17},{... | collective-permute-start | bytes 196616 | tf_op jit(solution)/shard_map/ppermute | solution.py:344
  11.6 9.0 %collective-permute-start.4 = (bf16[128,256]{1,0:T(8,128)(2,1)S(1)}, bf16[128,256]{1,0:T(8,128)(2,1)S(1)}, u32[]{:S(2)}, u32[]{:S(2)}) collective-permute-start(bf16[128,256]{1,0:T(8,128)(2,1)S(1)} %pack.1), channel_id=1, source_target_pairs={{0,20},{4,16},{8,28},{12,24},{16,4},{20,0},{24,12},{28,8},{1,21},{... | collective-permute-start | bytes 196616 | tf_op jit(solution)/shard_map/ppermute | solution.py:344
  14.1 50.5 %collective-permute-start.16 = (bf16[1024,2048]{1,0:T(8,128)(2,1)}, bf16[1024,2048]{1,0:T(8,128)(2,1)}, u32[]{:S(2)}, u32[]{:S(2)}) collective-permute-start(bf16[1024,2048]{1,0:T(8,128)(2,1)} %own.1), channel_id=1, source_target_pairs={{0,1},{1,0},{2,3},{3,2},{4,5},{5,4},{6,7},{7,6},{8,9},{9,8},{10,11... | collective-permute-start | bytes 12582920 | tf_op jit(solution)/shard_map/ppermute | solution.py:269
  14.2 6.5 %collective-permute-start.5 = (bf16[128,256]{1,0:T(8,128)(2,1)S(1)}, bf16[128,256]{1,0:T(8,128)(2,1)S(1)}, u32[]{:S(2)}, u32[]{:S(2)}) collective-permute-start(bf16[128,256]{1,0:T(8,128)(2,1)S(1)} %pack.1), channel_id=1, source_target_pairs={{0,24},{4,28},{8,16},{12,20},{16,8},{20,12},{24,0},{28,4},{1,25},{... | collective-permute-start | bytes 196616 | tf_op jit(solution)/shard_map/ppermute | solution.py:344
  17.8 7.0 %collective-permute-start.6 = (bf16[128,256]{1,0:T(8,128)(2,1)S(1)}, bf16[128,256]{1,0:T(8,128)(2,1)S(1)}, u32[]{:S(2)}, u32[]{:S(2)}) collective-permute-start(bf16[128,256]{1,0:T(8,128)(2,1)S(1)} %pack.1), channel_id=1, source_target_pairs={{0,28},{4,24},{8,20},{12,16},{16,12},{20,8},{24,4},{28,0},{1,29},{... | collective-permute-start | bytes 196616 | tf_op jit(solution)/shard_map/ppermute | solution.py:344
  24.9 1.9 %collective-permute-start.7 = (bf16[1024,256]{1,0:T(8,128)(2,1)S(1)}, bf16[1024,256]{1,0:T(8,128)(2,1)S(1)}, u32[]{:S(2)}, u32[]{:S(2)}) collective-permute-start(bf16[1024,256]{1,0:T(8,128)(2,1)S(1)} %constant_dynamic-update-slice_fusion.own), channel_id=1, source_target_pairs={{0,1},{1,0},{2,3},{3,2},{4,5},{5,4},{6,7},{7,6},{8,9},{9,8},{10,11... | collective-permute-start | bytes 1572872 | tf_op jit(solution)/shard_map/ppermute | solution.py:351
  31.0 1.6 %collective-permute-start.8 = (bf16[128,1024]{1,0:T(8,128)(2,1)S(1)}, bf16[128,1024]{1,0:T(8,128)(2,1)S(1)}, u32[]{:S(2)}, u32[]{:S(2)}) collective-permute-start(bf16[128,1024]{1,0:T(8,128)(2,1)S(1)} %get-tuple-element.23), channel_id=1, source_target_pairs={{0,1},{1,0},{2,3},{3,2},{4,5},{5,4},{6,7},{7,6},{8,9},{9,8},{10,11... | collective-permute-start | bytes 786440 | tf_op jit(solution)/shard_map/ppermute | solution.py:261
  32.6 10.7 %copy-start.5 = (bf16[128,2048]{1,0:T(8,128)(2,1)}, bf16[128,2048]{1,0:T(8,128)(2,1)S(1)}, u32[]{:S(2)}) copy-start(bf16[128,2048]{1,0:T(8,128)(2,1)S(1)} %constant_dynamic-update-slice_fusion.8) | copy-start | bytes 1572868
  32.6 10.7 %collective-permute-start.10 = (bf16[128,2048]{1,0:T(8,128)(2,1)S(1)}, bf16[128,2048]{1,0:T(8,128)(2,1)S(1)}, u32[]{:S(2)}, u32[]{:S(2)}) collective-permute-start(bf16[128,2048]{1,0:T(8,128)(2,1)S(1)} %constant_dynamic-update-slice_fusion.8), channel_id=1, source_target_pairs={{0,8},{2,18},{4,12},{6,22},{9,17},{11,3},{13,21},{15,7},{16,24},{1... | collective-permute-start | bytes 1572872 | tf_op jit(solution)/shard_map/ppermute | solution.py:265
  34.0 12.3 %collective-permute-start.9 = (bf16[128,2048]{1,0:T(8,128)(2,1)S(1)}, bf16[128,2048]{1,0:T(8,128)(2,1)S(1)}, u32[]{:S(2)}, u32[]{:S(2)}) collective-permute-start(bf16[128,2048]{1,0:T(8,128)(2,1)S(1)} %constant_dynamic-update-slice_fusion.8), channel_id=1, source_target_pairs={{0,16},{2,10},{4,20},{6,14},{9,1},{11,19},{13,5},{15,23},{16,8},{1... | collective-permute-start | bytes 1572872 | tf_op jit(solution)/shard_map/ppermute | solution.py:264
  37.8 1.6 %collective-permute-start.12 = (bf16[128,1024]{1,0:T(8,128)(2,1)S(1)}, bf16[128,1024]{1,0:T(8,128)(2,1)S(1)}, u32[]{:S(2)}, u32[]{:S(2)}) collective-permute-start(bf16[128,1024]{1,0:T(8,128)(2,1)S(1)} %get-tuple-element.24), channel_id=1, source_target_pairs={{0,1},{1,0},{2,3},{3,2},{4,5},{5,4},{6,7},{7,6},{8,9},{9,8},{10,11... | collective-permute-start | bytes 786440 | tf_op jit(solution)/shard_map/ppermute | solution.py:261
  40.1 11.9 %collective-permute-start.13 = (bf16[128,2048]{1,0:T(8,128)(2,1)}, bf16[128,2048]{1,0:T(8,128)(2,1)S(1)}, u32[]{:S(2)}, u32[]{:S(2)}) collective-permute-start(bf16[128,2048]{1,0:T(8,128)(2,1)} %constant_dynamic-update-slice_fusion.10), channel_id=1, source_target_pairs={{0,16},{2,10},{4,20},{6,14},{9,1},{11,19},{13,5},{15,23},{16,8},{1... | collective-permute-start | bytes 1572872 | tf_op jit(solution)/shard_map/ppermute | solution.py:264
  42.0 15.6 %collective-permute-start.14 = (bf16[128,2048]{1,0:T(8,128)(2,1)}, bf16[128,2048]{1,0:T(8,128)(2,1)S(1)}, u32[]{:S(2)}, u32[]{:S(2)}) collective-permute-start(bf16[128,2048]{1,0:T(8,128)(2,1)} %constant_dynamic-update-slice_fusion.10), channel_id=1, source_target_pairs={{0,8},{2,18},{4,12},{6,22},{9,17},{11,3},{13,21},{15,7},{16,24},{1... | collective-permute-start | bytes 1572872 | tf_op jit(solution)/shard_map/ppermute | solution.py:265
  46.3 15.4 %collective-permute-start.11 = (bf16[128,2048]{1,0:T(8,128)(2,1)S(1)}, bf16[128,2048]{1,0:T(8,128)(2,1)S(1)}, u32[]{:S(2)}, u32[]{:S(2)}) collective-permute-start(bf16[128,2048]{1,0:T(8,128)(2,1)S(1)} %broadcast_select_fusion.1), channel_id=1, source_target_pairs={{8,0},{9,1},{10,2},{11,3},{12,4},{13,5},{14,6},{15,7},{16,24},{17,... | collective-permute-start | bytes 1572872 | tf_op jit(solution)/shard_map/ppermute | solution.py:282
  57.7 6.9 %copy-start = (bf16[1024,2048]{1,0:T(8,128)(2,1)S(1)}, bf16[1024,2048]{1,0:T(8,128)(2,1)}, u32[]{:S(2)}) copy-start(bf16[1024,2048]{1,0:T(8,128)(2,1)} %own.1) | copy-start | bytes 12582916
  57.7 18.9 %collective-permute-start.15 = (bf16[128,2048]{1,0:T(8,128)(2,1)S(1)}, bf16[128,2048]{1,0:T(8,128)(2,1)S(1)}, u32[]{:S(2)}, u32[]{:S(2)}) collective-permute-start(bf16[128,2048]{1,0:T(8,128)(2,1)S(1)} %broadcast_select_fusion), channel_id=1, source_target_pairs={{8,0},{9,1},{10,2},{11,3},{12,4},{13,5},{14,6},{15,7},{16,24},{17,... | collective-permute-start | bytes 1572872 | tf_op jit(solution)/shard_map/ppermute | solution.py:282
  63.0 16.6 %collective-permute-start.17 = (bf16[128,2048]{1,0:T(8,128)(2,1)S(1)}, bf16[128,2048]{1,0:T(8,128)(2,1)S(1)}, u32[]{:S(2)}, u32[]{:S(2)}) collective-permute-start(bf16[128,2048]{1,0:T(8,128)(2,1)S(1)} %broadcast_select_fusion.6.rows), channel_id=1, source_target_pairs={{0,4},{4,0},{8,12},{12,8},{16,20},{20,16},{24,28},{28,24},{1,5},{5... | collective-permute-start | bytes 1572872 | tf_op jit(solution)/shard_map/ppermute | solution.py:292
  68.4 21.1 %collective-permute-start.20 = (bf16[128,2048]{1,0:T(8,128)(2,1)S(1)}, bf16[128,2048]{1,0:T(8,128)(2,1)S(1)}, u32[]{:S(2)}, u32[]{:S(2)}) collective-permute-start(bf16[128,2048]{1,0:T(8,128)(2,1)S(1)} %project.6), channel_id=1, source_target_pairs={{0,2},{1,3},{2,0},{3,1},{4,6},{5,7},{6,4},{7,5},{8,10},{9,11},{10,... | collective-permute-start | bytes 1572872 | tf_op jit(solution)/shard_map/ppermute | solution.py:278
  79.0 19.6 %collective-permute-start.19 = (bf16[128,2048]{1,0:T(8,128)(2,1)S(1)}, bf16[128,2048]{1,0:T(8,128)(2,1)S(1)}, u32[]{:S(2)}, u32[]{:S(2)}) collective-permute-start(bf16[128,2048]{1,0:T(8,128)(2,1)S(1)} %project.7), channel_id=1, source_target_pairs={{0,2},{1,3},{2,0},{3,1},{4,6},{5,7},{6,4},{7,5},{8,10},{9,11},{10,... | collective-permute-start | bytes 1572872 | tf_op jit(solution)/shard_map/ppermute | solution.py:278
  79.1 31.8 %collective-permute-start.21 = (bf16[128,2048]{1,0:T(8,128)(2,1)S(1)}, bf16[128,2048]{1,0:T(8,128)(2,1)S(1)}, u32[]{:S(2)}, u32[]{:S(2)}) collective-permute-start(bf16[128,2048]{1,0:T(8,128)(2,1)S(1)} %get-tuple-element.32), channel_id=1, source_target_pairs={{0,4},{4,0},{8,12},{12,8},{16,20},{20,16},{24,28},{28,24},{1,5},{5... | collective-permute-start | bytes 1572872 | tf_op jit(solution)/shard_map/ppermute | solution.py:295
  79.6 25.7 %collective-permute-start.18 = (bf16[128,2048]{1,0:T(8,128)(2,1)S(1)}, bf16[128,2048]{1,0:T(8,128)(2,1)S(1)}, u32[]{:S(2)}, u32[]{:S(2)}) collective-permute-start(bf16[128,2048]{1,0:T(8,128)(2,1)S(1)} %get-tuple-element.28.rows), channel_id=1, source_target_pairs={{0,4},{4,0},{8,12},{12,8},{16,20},{20,16},{24,28},{28,24},{1,5},{5... | collective-permute-start | bytes 1572872 | tf_op jit(solution)/shard_map/ppermute | solution.py:292
  81.3 30.0 %collective-permute-start.22 = (bf16[128,2048]{1,0:T(8,128)(2,1)S(1)}, bf16[128,2048]{1,0:T(8,128)(2,1)S(1)}, u32[]{:S(2)}, u32[]{:S(2)}) collective-permute-start(bf16[128,2048]{1,0:T(8,128)(2,1)S(1)} %broadcast_select_fusion.5), channel_id=1, source_target_pairs={{0,4},{4,0},{8,12},{12,8},{16,20},{20,16},{24,28},{28,24},{1,5},{5... | collective-permute-start | bytes 1572872 | tf_op jit(solution)/shard_map/ppermute | solution.py:295
  90.7 23.6 %collective-permute-start.23 = (bf16[128,2048]{1,0:T(8,128)(2,1)S(1)}, bf16[128,2048]{1,0:T(8,128)(2,1)S(1)}, u32[]{:S(2)}, u32[]{:S(2)}) collective-permute-start(bf16[128,2048]{1,0:T(8,128)(2,1)S(1)} %project.8), channel_id=1, source_target_pairs={{0,2},{1,3},{2,0},{3,1},{4,6},{5,7},{6,4},{7,5},{8,10},{9,11},{10,... | collective-permute-start | bytes 1572872 | tf_op jit(solution)/shard_map/ppermute | solution.py:278
  106.5 9.2 %collective-permute-start.24 = (bf16[128,2048]{1,0:T(8,128)(2,1)S(1)}, bf16[128,2048]{1,0:T(8,128)(2,1)S(1)}, u32[]{:S(2)}, u32[]{:S(2)}) collective-permute-start(bf16[128,2048]{1,0:T(8,128)(2,1)S(1)} %project.9), channel_id=1, source_target_pairs={{0,2},{1,3},{2,0},{3,1},{4,6},{5,7},{6,4},{7,5},{8,10},{9,11},{10,... | collective-permute-start | bytes 1572872 | tf_op jit(solution)/shard_map/ppermute | solution.py:278
  114.4 1.4 %copy-start.4 = (bf16[512,2048]{1,0:T(8,128)(2,1)}, bf16[512,2048]{1,0:T(8,128)(2,1)S(1)}, u32[]{:S(2)}) copy-start(bf16[512,2048]{1,0:T(8,128)(2,1)S(1)} %fusion.6) | copy-start | bytes 6291460

commit v5 on v4

--- a/solution.py
+++ b/solution.py
@@ -14,8 +14,8 @@
 NEG = -1e30
 GRANT = 20 << 20
 BEFORE = {'hop_3_out_1': ('part_0',),
- 'kept_out_0': ('part_1',),
- 'kept_out_1': ('part_1',),
+ 'kept_out_0': ('part_0',),
+ 'kept_out_1': ('part_2',),
  'own_0': ('part_3',),
  'own_1': ('own_done_0',),
  'sent_2': ('come_0', 'part_1'),

time: 117 us -> 117 us (level)
    ppermute x2, waiting for transfers between devices: 6.65 us -> 2.02 us  [routed(): sent_y.append(order.put(f'sent_y_{i}', lax.ppermute(out, 'ctx', swap_y)))]
    ppermute x4, waiting for transfers between devices: 14.8 us -> 19.3 us  [partial(): come.append(order.put(f'come_{slot}', lax.ppermute(out, 'head', swap_x)))]
  transfers between devices with their start and end apart: 25 -> 25, of which waited for: 14 -> 13; matrix products, arithmetic and copies ran while one was open for 5% -> 5% of each run, Pallas kernels for 14% -> 14%
where the time goes in v5:
time: 117 us; the launch traced here: 116 us
  waiting for transfers between devices  47.5 us (41%)
  starting transfers between devices  41 us (35%)
  Pallas kernels  17.3 us (15%)
  other arithmetic  6.3 us (5%)
  local copies, waits for them, and re-layouts  3.76 us (3%)
    ppermute x4, waiting for transfers between devices, partial(): come.append(order.put(f'come_{slot}', lax.ppermute(out, 'head', swap_x)))  19.3 us
    ppermute x4, starting transfers between devices, partial(): come.append(order.put(f'come_{slot}', lax.ppermute(out, 'head', swap_x)))  13 us
    ppermute x7, starting transfers between devices, per_device(): lax.ppermute(piece, 'ctx', [(i, i ^ d) for i in range(ctx_size)])  12.6 us
    pallas_call x6, Pallas kernels, project(): pl.pallas_call(project_kernel, in_specs=[VMEM] * 3, out_specs=VMEM, out_s...  9.72 us
    ppermute x2, waiting for transfers between devices, routed(): hop_1 = lax.ppermute(block, both, route(HOP_1))  7.21 us
    ppermute x7, waiting for transfers between devices, per_device(): lax.ppermute(piece, 'ctx', [(i, i ^ d) for i in range(ctx_size)])  6.91 us
    ppermute x2, starting transfers between devices, routed(): hop_1 = lax.ppermute(block, both, route(HOP_1))  5.71 us
    ppermute x2, waiting for transfers between devices, routed(): hop_2 = lax.ppermute(block, both, route(HOP_2))  5.62 us
  transfers between devices with their start and end apart: 25, of which 13 were waited for; matrix products, arithmetic and copies ran while one was open for 5% of the time, Pallas kernels for 14%

profile of v5, /device:TPU:0, one launch (start us, length us, event | category | flops | bytes accessed | tf_op | source)
XLA Modules:
  0.0 116.4 jit_solution(5316138261212831876)
XLA Ops:
  0.0 0.7 convert_element_type.27
  0.8 0.5 fusion.8
  1.5 0.9 copy-done.2
  2.4 0.9 copy-done.3
  3.3 0.6 pack.1
  4.0 3.0 %collective-permute-start = (bf16[128,256]{1,0:T(8,128)(2,1)S(1)}, bf16[128,256]{1,0:T(8,128)(2,1)S(1)}, u32[]{:S(2)}, u32[]{:S(2)}) collective-permute-start(bf16[128,256]{1,0:T(8,128)(2,1)S(1)} %pack.1), channel_id=1, source_target_pairs={{0,4},{4,0},{8,12},{12,8},{16,20},{20,16},{24,28},{28,24},{1,5},{5... | collective-permute-start | bytes 196616 | tf_op jit(solution)/shard_map/ppermute | solution.py:344
  7.0 1.6 %collective-permute-start.1 = (bf16[128,256]{1,0:T(8,128)(2,1)S(1)}, bf16[128,256]{1,0:T(8,128)(2,1)S(1)}, u32[]{:S(2)}, u32[]{:S(2)}) collective-permute-start(bf16[128,256]{1,0:T(8,128)(2,1)S(1)} %pack.1), channel_id=1, source_target_pairs={{0,8},{4,12},{8,0},{12,4},{16,24},{20,28},{24,16},{28,20},{1,9},{5... | collective-permute-start | bytes 196616 | tf_op jit(solution)/shard_map/ppermute | solution.py:344
  8.6 3.0 %collective-permute-start.3 = (bf16[128,256]{1,0:T(8,128)(2,1)S(1)}, bf16[128,256]{1,0:T(8,128)(2,1)S(1)}, u32[]{:S(2)}, u32[]{:S(2)}) collective-permute-start(bf16[128,256]{1,0:T(8,128)(2,1)S(1)} %pack.1), channel_id=1, source_target_pairs={{0,16},{4,20},{8,24},{12,28},{16,0},{20,4},{24,8},{28,12},{1,17},{... | collective-permute-start | bytes 196616 | tf_op jit(solution)/shard_map/ppermute | solution.py:344
  11.6 1.3 %collective-permute-start.4 = (bf16[128,256]{1,0:T(8,128)(2,1)S(1)}, bf16[128,256]{1,0:T(8,128)(2,1)S(1)}, u32[]{:S(2)}, u32[]{:S(2)}) collective-permute-start(bf16[128,256]{1,0:T(8,128)(2,1)S(1)} %pack.1), channel_id=1, source_target_pairs={{0,20},{4,16},{8,28},{12,24},{16,4},{20,0},{24,12},{28,8},{1,21},{... | collective-permute-start | bytes 196616 | tf_op jit(solution)/shard_map/ppermute | solution.py:344
  12.9 0.7 pad_add_fusion
  14.2 3.7 %collective-permute-start.5 = (bf16[128,256]{1,0:T(8,128)(2,1)S(1)}, bf16[128,256]{1,0:T(8,128)(2,1)S(1)}, u32[]{:S(2)}, u32[]{:S(2)}) collective-permute-start(bf16[128,256]{1,0:T(8,128)(2,1)S(1)} %pack.1), channel_id=1, source_target_pairs={{0,24},{4,28},{8,16},{12,20},{16,8},{20,12},{24,0},{28,4},{1,25},{... | collective-permute-start | bytes 196616 | tf_op jit(solution)/shard_map/ppermute | solution.py:344
  18.0 2.6 %collective-permute-done.4 = bf16[128,256]{1,0:T(8,128)(2,1)S(1)} collective-permute-done((bf16[128,256]{1,0:T(8,128)(2,1)S(1)}, bf16[128,256]{1,0:T(8,128)(2,1)S(1)}, u32[]{:S(2)}, u32[]{:S(2)}) %collective-permute-start.4) | collective-permute-done | bytes 65568 | tf_op jit(solution)/shard_map/ppermute | solution.py:344
  20.6 4.2 %collective-permute-done.6 = bf16[128,256]{1,0:T(8,128)(2,1)S(1)} collective-permute-done((bf16[128,256]{1,0:T(8,128)(2,1)S(1)}, bf16[128,256]{1,0:T(8,128)(2,1)S(1)}, u32[]{:S(2)}, u32[]{:S(2)}) %collective-permute-start.6) | collective-permute-done | bytes 65568 | tf_op jit(solution)/shard_map/ppermute | solution.py:344
  24.9 1.9 %collective-permute-done.7.other = bf16[1024,256]{1,0:T(8,128)(2,1)S(1)} collective-permute-done((bf16[1024,256]{1,0:T(8,128)(2,1)S(1)}, bf16[1024,256]{1,0:T(8,128)(2,1)S(1)}, u32[]{:S(2)}, u32[]{:S(2)}) %collective-permute-start.7) | collective-permute-done | bytes 524320 | tf_op jit(solution)/shard_map/ppermute | solution.py:351
  26.8 4.2 %attention.1 = (bf16[128,1024]{1,0:T(8,128)(2,1)S(1)}, bf16[128,1024]{1,0:T(8,128)(2,1)S(1)}) custom-call(s32[66]{0:T(128)S(1)} %pad_add_fusion.2.table, bf16[256,1024]{1,0:T(8,128)(2,1)S(1)} %turn.1.queries, bf16[1024,256]{1,0:T(8,128)(2,1)S(1)} %constant_dynamic-update-slice_fusion.own, bf16[1024,256]{1,0:T(8,128)(2,1)S(1)} %collective-permute-done.7.other), custom_call_target="tpu_custom_call" | custom-call | tf_op jit(solution)/shard_map/attention/pallas_call | solution.py:162
  31.2 1.4 %collective-permute-done.8 = bf16[128,1024]{1,0:T(8,128)(2,1)S(1)} collective-permute-done((bf16[128,1024]{1,0:T(8,128)(2,1)S(1)}, bf16[128,1024]{1,0:T(8,128)(2,1)S(1)}, u32[]{:S(2)}, u32[]{:S(2)}) %collective-permute-start.8) | collective-permute-done | bytes 262176 | tf_op jit(solution)/shard_map/ppermute | solution.py:261
  32.6 1.3 %collective-permute-start.10 = (bf16[128,2048]{1,0:T(8,128)(2,1)S(1)}, bf16[128,2048]{1,0:T(8,128)(2,1)S(1)}, u32[]{:S(2)}, u32[]{:S(2)}) collective-permute-start(bf16[128,2048]{1,0:T(8,128)(2,1)S(1)} %constant_dynamic-update-slice_fusion.8), channel_id=1, source_target_pairs={{0,8},{2,18},{4,12},{6,22},{9,17},{11,3},{13,21},{15,7},{16,24},{1... | collective-permute-start | bytes 1572872 | tf_op jit(solution)/shard_map/ppermute | solution.py:265
  34.0 3.8 %collective-permute-start.9 = (bf16[128,2048]{1,0:T(8,128)(2,1)S(1)}, bf16[128,2048]{1,0:T(8,128)(2,1)S(1)}, u32[]{:S(2)}, u32[]{:S(2)}) collective-permute-start(bf16[128,2048]{1,0:T(8,128)(2,1)S(1)} %constant_dynamic-update-slice_fusion.8), channel_id=1, source_target_pairs={{0,16},{2,10},{4,20},{6,14},{9,1},{11,19},{13,5},{15,23},{16,8},{1... | collective-permute-start | bytes 1572872 | tf_op jit(solution)/shard_map/ppermute | solution.py:264
  37.9 0.7 constant_dynamic-update-slice_fusion.11
  38.6 0.8 collective-permute-done.12
  39.4 0.7 constant_dynamic-update-slice_fusion.10
  40.1 1.9 %collective-permute-start.13 = (bf16[128,2048]{1,0:T(8,128)(2,1)}, bf16[128,2048]{1,0:T(8,128)(2,1)S(1)}, u32[]{:S(2)}, u32[]{:S(2)}) collective-permute-start(bf16[128,2048]{1,0:T(8,128)(2,1)} %constant_dynamic-update-slice_fusion.10), channel_id=1, source_target_pairs={{0,16},{2,10},{4,20},{6,14},{9,1},{11,19},{13,5},{15,23},{16,8},{1... | collective-permute-start | bytes 1572872 | tf_op jit(solution)/shard_map/ppermute | solution.py:264
  42.0 1.3 %collective-permute-start.14 = (bf16[128,2048]{1,0:T(8,128)(2,1)}, bf16[128,2048]{1,0:T(8,128)(2,1)S(1)}, u32[]{:S(2)}, u32[]{:S(2)}) collective-permute-start(bf16[128,2048]{1,0:T(8,128)(2,1)} %constant_dynamic-update-slice_fusion.10), channel_id=1, source_target_pairs={{0,8},{2,18},{4,12},{6,22},{9,17},{11,3},{13,21},{15,7},{16,24},{1... | collective-permute-start | bytes 1572872 | tf_op jit(solution)/shard_map/ppermute | solution.py:265
  43.4 2.9 %collective-permute-done.9 = bf16[128,2048]{1,0:T(8,128)(2,1)S(1)} collective-permute-done((bf16[128,2048]{1,0:T(8,128)(2,1)S(1)}, bf16[128,2048]{1,0:T(8,128)(2,1)S(1)}, u32[]{:S(2)}, u32[]{:S(2)}) %collective-permute-start.9) | collective-permute-done | bytes 524320 | tf_op jit(solution)/shard_map/ppermute | solution.py:264
  46.3 1.3 %collective-permute-start.11 = (bf16[128,2048]{1,0:T(8,128)(2,1)S(1)}, bf16[128,2048]{1,0:T(8,128)(2,1)S(1)}, u32[]{:S(2)}, u32[]{:S(2)}) collective-permute-start(bf16[128,2048]{1,0:T(8,128)(2,1)S(1)} %broadcast_select_fusion.1), channel_id=1, source_target_pairs={{8,0},{9,1},{10,2},{11,3},{12,4},{13,5},{14,6},{15,7},{16,24},{17,... | collective-permute-start | bytes 1572872 | tf_op jit(solution)/shard_map/ppermute | solution.py:282
  47.7 4.3 %collective-permute-done.13 = bf16[128,2048]{1,0:T(8,128)(2,1)S(1)} collective-permute-done((bf16[128,2048]{1,0:T(8,128)(2,1)}, bf16[128,2048]{1,0:T(8,128)(2,1)S(1)}, u32[]{:S(2)}, u32[]{:S(2)}) %collective-permute-start.13) | collective-permute-done | bytes 524320 | tf_op jit(solution)/shard_map/ppermute | solution.py:264
  52.0 5.6 %collective-permute-done.14 = bf16[128,2048]{1,0:T(8,128)(2,1)S(1)} collective-permute-done((bf16[128,2048]{1,0:T(8,128)(2,1)}, bf16[128,2048]{1,0:T(8,128)(2,1)S(1)}, u32[]{:S(2)}, u32[]{:S(2)}) %collective-permute-start.14) | collective-permute-done | bytes 524320 | tf_op jit(solution)/shard_map/ppermute | solution.py:265
  57.7 1.7 %collective-permute-start.15 = (bf16[128,2048]{1,0:T(8,128)(2,1)S(1)}, bf16[128,2048]{1,0:T(8,128)(2,1)S(1)}, u32[]{:S(2)}, u32[]{:S(2)}) collective-permute-start(bf16[128,2048]{1,0:T(8,128)(2,1)S(1)} %broadcast_select_fusion), channel_id=1, source_target_pairs={{8,0},{9,1},{10,2},{11,3},{12,4},{13,5},{14,6},{15,7},{16,24},{17,... | collective-permute-start | bytes 1572872 | tf_op jit(solution)/shard_map/ppermute | solution.py:282
  59.4 2.3 %collective-permute-done.11 = bf16[128,2048]{1,0:T(8,128)(2,1)S(1)} collective-permute-done((bf16[128,2048]{1,0:T(8,128)(2,1)S(1)}, bf16[128,2048]{1,0:T(8,128)(2,1)S(1)}, u32[]{:S(2)}, u32[]{:S(2)}) %collective-permute-start.11) | collective-permute-done | bytes 524320 | tf_op jit(solution)/shard_map/ppermute | solution.py:282
  61.8 1.2 %broadcast_select_fusion.7 = (bf16[128,2048]{1,0:T(8,128)(2,1)S(1)}, bf16[128,2048]{1,0:T(8,128)(2,1)S(1)}) fusion(pred[]{:T(512)S(6)} %ge.3, bf16[128,2048]{1,0:T(8,128)(2,1)S(1)} %broadcast_select_fusion.1, bf16[128,2048]{1,0:T(8,128)(2,1)S(1)} %collective-permute-done.11, pred[]{:T(512)S(6)} %or.3, bf16[128,2048]{1,0:T(8,128)(2,1)} %copy-done.5, ...), kind=kLoop, calls=%fused_computation.23 | loop fusion | flops 1048576 | bytes 3670020 | tf_op jit(solution)/shard_map/jit(_where)/select_n | solution.py:287
  63.0 1.6 %collective-permute-start.17 = (bf16[128,2048]{1,0:T(8,128)(2,1)S(1)}, bf16[128,2048]{1,0:T(8,128)(2,1)S(1)}, u32[]{:S(2)}, u32[]{:S(2)}) collective-permute-start(bf16[128,2048]{1,0:T(8,128)(2,1)S(1)} %broadcast_select_fusion.6.rows), channel_id=1, source_target_pairs={{0,4},{4,0},{8,12},{12,8},{16,20},{20,16},{24,28},{28,24},{1,5},{5... | collective-permute-start | bytes 1572872 | tf_op jit(solution)/shard_map/ppermute | solution.py:292
  64.6 2.5 %hold.1 = (bf16[1024,2048]{1,0:T(8,128)(2,1)S(1)}, bf16[1024,2048]{1,0:T(8,128)(2,1)S(1)}) custom-call(bf16[1024,2048]{1,0:T(8,128)(2,1)S(1)} %copy-done, bf16[1024,2048]{1,0:T(8,128)(2,1)} %collective-permute-done.16.other), custom_call_target="tpu_custom_call" | custom-call | tf_op jit(solution)/shard_map/hold/pallas_call | solution.py:192
  67.1 1.3 %project.6 = bf16[128,2048]{1,0:T(8,128)(2,1)S(1)} custom-call(bf16[128,2048]{1,0:T(8,128)(2,1)S(1)} %broadcast_select_fusion.6.rows, bf16[1024,2048]{1,0:T(8,128)(2,1)S(1)} %get-tuple-element.24.own, bf16[1024,2048]{1,0:T(8,128)(2,1)S(1)} %get-tuple-element.25.other), custom_call_target="tpu_custom_call" | custom-call | flops 1073741824 | bytes 1048576 | tf_op jit(solution)/shard_map/project/pallas_call | solution.py:216
  68.4 8.2 %collective-permute-start.20 = (bf16[128,2048]{1,0:T(8,128)(2,1)S(1)}, bf16[128,2048]{1,0:T(8,128)(2,1)S(1)}, u32[]{:S(2)}, u32[]{:S(2)}) collective-permute-start(bf16[128,2048]{1,0:T(8,128)(2,1)S(1)} %project.6), channel_id=1, source_target_pairs={{0,2},{1,3},{2,0},{3,1},{4,6},{5,7},{6,4},{7,5},{8,10},{9,11},{10,... | collective-permute-start | bytes 1572872 | tf_op jit(solution)/shard_map/ppermute | solution.py:278
  76.6 1.2 %broadcast_select_fusion.4 = (bf16[128,2048]{1,0:T(8,128)(2,1)S(1)}, bf16[128,2048]{1,0:T(8,128)(2,1)S(1)}) fusion(pred[]{:T(512)S(6)} %ge.3, bf16[128,2048]{1,0:T(8,128)(2,1)S(1)} %broadcast_select_fusion, bf16[128,2048]{1,0:T(8,128)(2,1)S(1)} %collective-permute-done.15, pred[]{:T(512)S(6)} %or.3, ...), kind=kLoop, calls=%fused_computation.20 | loop fusion | flops 1048576 | bytes 3670020 | tf_op jit(solution)/shard_map/jit(_where)/select_n | solution.py:286
  77.8 1.3 %project.7 = bf16[128,2048]{1,0:T(8,128)(2,1)S(1)} custom-call(bf16[128,2048]{1,0:T(8,128)(2,1)S(1)} %get-tuple-element.27.rows, bf16[1024,2048]{1,0:T(8,128)(2,1)S(1)} %get-tuple-element.24.own, bf16[1024,2048]{1,0:T(8,128)(2,1)S(1)} %get-tuple-element.25.other), custom_call_target="tpu_custom_call" | custom-call | flops 1073741824 | bytes 1048576 | tf_op jit(solution)/shard_map/project/pallas_call | solution.py:216
  79.2 2.0 %collective-permute-start.18 = (bf16[128,2048]{1,0:T(8,128)(2,1)S(1)}, bf16[128,2048]{1,0:T(8,128)(2,1)S(1)}, u32[]{:S(2)}, u32[]{:S(2)}) collective-permute-start(bf16[128,2048]{1,0:T(8,128)(2,1)S(1)} %get-tuple-element.27.rows), channel_id=1, source_target_pairs={{0,4},{4,0},{8,12},{12,8},{16,20},{20,16},{24,28},{28,24},{1,5},{5... | collective-permute-start | bytes 1572872 | tf_op jit(solution)/shard_map/ppermute | solution.py:292
  81.5 7.9 %collective-permute-done.20 = bf16[128,2048]{1,0:T(8,128)(2,1)S(1)} collective-permute-done((bf16[128,2048]{1,0:T(8,128)(2,1)S(1)}, bf16[128,2048]{1,0:T(8,128)(2,1)S(1)}, u32[]{:S(2)}, u32[]{:S(2)}) %collective-permute-start.20) | collective-permute-done | bytes 524320 | tf_op jit(solution)/shard_map/ppermute | solution.py:278
  89.4 1.3 %project.8 = bf16[128,2048]{1,0:T(8,128)(2,1)S(1)} custom-call(bf16[128,2048]{1,0:T(8,128)(2,1)S(1)} %collective-permute-done.17.rows, bf16[1024,2048]{1,0:T(8,128)(2,1)S(1)} %get-tuple-element.24.own, bf16[1024,2048]{1,0:T(8,128)(2,1)S(1)} %get-tuple-element.25.other), custom_call_target="tpu_custom_call" | custom-call | flops 1073741824 | bytes 1048576 | tf_op jit(solution)/shard_map/project/pallas_call | solution.py:216
  90.7 2.1 %collective-permute-start.23 = (bf16[128,2048]{1,0:T(8,128)(2,1)S(1)}, bf16[128,2048]{1,0:T(8,128)(2,1)S(1)}, u32[]{:S(2)}, u32[]{:S(2)}) collective-permute-start(bf16[128,2048]{1,0:T(8,128)(2,1)S(1)} %project.8), channel_id=1, source_target_pairs={{0,2},{1,3},{2,0},{3,1},{4,6},{5,7},{6,4},{7,5},{8,10},{9,11},{10,... | collective-permute-start | bytes 1572872 | tf_op jit(solution)/shard_map/ppermute | solution.py:278
  92.8 7.9 %collective-permute-done.19 = bf16[128,2048]{1,0:T(8,128)(2,1)S(1)} collective-permute-done((bf16[128,2048]{1,0:T(8,128)(2,1)S(1)}, bf16[128,2048]{1,0:T(8,128)(2,1)S(1)}, u32[]{:S(2)}, u32[]{:S(2)}) %collective-permute-start.19) | collective-permute-done | bytes 524320 | tf_op jit(solution)/shard_map/ppermute | solution.py:278
  100.7 2.0 %collective-permute-done.18.rows = bf16[128,2048]{1,0:T(8,128)(2,1)S(1)} collective-permute-done((bf16[128,2048]{1,0:T(8,128)(2,1)S(1)}, bf16[128,2048]{1,0:T(8,128)(2,1)S(1)}, u32[]{:S(2)}, u32[]{:S(2)}) %collective-permute-start.18) | collective-permute-done | bytes 524320 | tf_op jit(solution)/shard_map/ppermute | solution.py:292
  102.7 1.3 %project.9 = bf16[128,2048]{1,0:T(8,128)(2,1)S(1)} custom-call(bf16[128,2048]{1,0:T(8,128)(2,1)S(1)} %collective-permute-done.18.rows, bf16[1024,2048]{1,0:T(8,128)(2,1)S(1)} %get-tuple-element.24.own, bf16[1024,2048]{1,0:T(8,128)(2,1)S(1)} %get-tuple-element.25.other), custom_call_target="tpu_custom_call" | custom-call | flops 1073741824 | bytes 1048576 | tf_op jit(solution)/shard_map/project/pallas_call | solution.py:216
  104.0 2.6 %collective-permute-start.24 = (bf16[128,2048]{1,0:T(8,128)(2,1)S(1)}, bf16[128,2048]{1,0:T(8,128)(2,1)S(1)}, u32[]{:S(2)}, u32[]{:S(2)}) collective-permute-start(bf16[128,2048]{1,0:T(8,128)(2,1)S(1)} %project.9), channel_id=1, source_target_pairs={{0,2},{1,3},{2,0},{3,1},{4,6},{5,7},{6,4},{7,5},{8,10},{9,11},{10,... | collective-permute-start | bytes 1572872 | tf_op jit(solution)/shard_map/ppermute | solution.py:278
  106.5 2.3 %project.10 = f32[256,2048]{1,0:T(8,128)S(1)} custom-call(bf16[256,2048]{1,0:T(8,128)(2,1)S(1)} %pad_maximum_fusion.rows, bf16[1024,2048]{1,0:T(8,128)(2,1)S(1)} %get-tuple-element.24.own, bf16[1024,2048]{1,0:T(8,128)(2,1)S(1)} %get-tuple-element.25.other), custom_call_target="tpu_custom_call" | custom-call | flops 2147483648 | bytes 2097152 | tf_op jit(solution)/shard_map/project/pallas_call | solution.py:216
  109.5 2.3 %project.11 = f32[256,2048]{1,0:T(8,128)S(1)} custom-call(bf16[256,2048]{1,0:T(8,128)(2,1)S(1)} %pad_maximum_fusion.1.rows, bf16[1024,2048]{1,0:T(8,128)(2,1)S(1)} %get-tuple-element.24.own, bf16[1024,2048]{1,0:T(8,128)(2,1)S(1)} %get-tuple-element.25.other), custom_call_target="tpu_custom_call" | custom-call | flops 2147483648 | bytes 2097152 | tf_op jit(solution)/shard_map/project/pallas_call | solution.py:216
  111.9 3.6 %collective-permute-done.24 = bf16[128,2048]{1,0:T(8,128)(2,1)S(1)} collective-permute-done((bf16[128,2048]{1,0:T(8,128)(2,1)S(1)}, bf16[128,2048]{1,0:T(8,128)(2,1)S(1)}, u32[]{:S(2)}, u32[]{:S(2)}) %collective-permute-start.24) | collective-permute-done | bytes 524320 | tf_op jit(solution)/shard_map/ppermute | solution.py:278
  115.5 0.9 fusion.7
  (58 shorter events, 2.6 us)
Async XLA Ops:
  0.0 13.7 %copy-start.1 = (bf16[256,1024]{1,0:T(8,128)(2,1)S(1)}, bf16[256,1024]{1,0:T(8,128)(2,1)}, u32[]{:S(2)}) copy-start(bf16[256,1024]{1,0:T(8,128)(2,1)} %queries.1) | copy-start | bytes 1572868
  1.5 0.9 copy-start.2
  2.4 0.9 copy-start.3
  4.0 10.1 %collective-permute-start = (bf16[128,256]{1,0:T(8,128)(2,1)S(1)}, bf16[128,256]{1,0:T(8,128)(2,1)S(1)}, u32[]{:S(2)}, u32[]{:S(2)}) collective-permute-start(bf16[128,256]{1,0:T(8,128)(2,1)S(1)} %pack.1), channel_id=1, source_target_pairs={{0,4},{4,0},{8,12},{12,8},{16,20},{20,16},{24,28},{28,24},{1,5},{5... | collective-permute-start | bytes 196616 | tf_op jit(solution)/shard_map/ppermute | solution.py:344
  7.0 7.2 %collective-permute-start.1 = (bf16[128,256]{1,0:T(8,128)(2,1)S(1)}, bf16[128,256]{1,0:T(8,128)(2,1)S(1)}, u32[]{:S(2)}, u32[]{:S(2)}) collective-permute-start(bf16[128,256]{1,0:T(8,128)(2,1)S(1)} %pack.1), channel_id=1, source_target_pairs={{0,8},{4,12},{8,0},{12,4},{16,24},{20,28},{24,16},{28,20},{1,9},{5... | collective-permute-start | bytes 196616 | tf_op jit(solution)/shard_map/ppermute | solution.py:344
  8.6 9.3 %collective-permute-start.2 = (bf16[128,256]{1,0:T(8,128)(2,1)S(1)}, bf16[128,256]{1,0:T(8,128)(2,1)S(1)}, u32[]{:S(2)}, u32[]{:S(2)}) collective-permute-start(bf16[128,256]{1,0:T(8,128)(2,1)S(1)} %pack.1), channel_id=1, source_target_pairs={{0,12},{4,8},{8,4},{12,0},{16,28},{20,24},{24,20},{28,16},{1,13},{... | collective-permute-start | bytes 196616 | tf_op jit(solution)/shard_map/ppermute | solution.py:344
  8.6 9.4 %collective-permute-start.3 = (bf16[128,256]{1,0:T(8,128)(2,1)S(1)}, bf16[128,256]{1,0:T(8,128)(2,1)S(1)}, u32[]{:S(2)}, u32[]{:S(2)}) collective-permute-start(bf16[128,256]{1,0:T(8,128)(2,1)S(1)} %pack.1), channel_id=1, source_target_pairs={{0,16},{4,20},{8,24},{12,28},{16,0},{20,4},{24,8},{28,12},{1,17},{... | collective-permute-start | bytes 196616 | tf_op jit(solution)/shard_map/ppermute | solution.py:344
  11.6 9.0 %collective-permute-start.4 = (bf16[128,256]{1,0:T(8,128)(2,1)S(1)}, bf16[128,256]{1,0:T(8,128)(2,1)S(1)}, u32[]{:S(2)}, u32[]{:S(2)}) collective-permute-start(bf16[128,256]{1,0:T(8,128)(2,1)S(1)} %pack.1), channel_id=1, source_target_pairs={{0,20},{4,16},{8,28},{12,24},{16,4},{20,0},{24,12},{28,8},{1,21},{... | collective-permute-start | bytes 196616 | tf_op jit(solution)/shard_map/ppermute | solution.py:344
  14.1 50.5 %collective-permute-start.16 = (bf16[1024,2048]{1,0:T(8,128)(2,1)}, bf16[1024,2048]{1,0:T(8,128)(2,1)}, u32[]{:S(2)}, u32[]{:S(2)}) collective-permute-start(bf16[1024,2048]{1,0:T(8,128)(2,1)} %own.1), channel_id=1, source_target_pairs={{0,1},{1,0},{2,3},{3,2},{4,5},{5,4},{6,7},{7,6},{8,9},{9,8},{10,11... | collective-permute-start | bytes 12582920 | tf_op jit(solution)/shard_map/ppermute | solution.py:269
  14.2 6.5 %collective-permute-start.5 = (bf16[128,256]{1,0:T(8,128)(2,1)S(1)}, bf16[128,256]{1,0:T(8,128)(2,1)S(1)}, u32[]{:S(2)}, u32[]{:S(2)}) collective-permute-start(bf16[128,256]{1,0:T(8,128)(2,1)S(1)} %pack.1), channel_id=1, source_target_pairs={{0,24},{4,28},{8,16},{12,20},{16,8},{20,12},{24,0},{28,4},{1,25},{... | collective-permute-start | bytes 196616 | tf_op jit(solution)/shard_map/ppermute | solution.py:344
  17.8 7.0 %collective-permute-start.6 = (bf16[128,256]{1,0:T(8,128)(2,1)S(1)}, bf16[128,256]{1,0:T(8,128)(2,1)S(1)}, u32[]{:S(2)}, u32[]{:S(2)}) collective-permute-start(bf16[128,256]{1,0:T(8,128)(2,1)S(1)} %pack.1), channel_id=1, source_target_pairs={{0,28},{4,24},{8,20},{12,16},{16,12},{20,8},{24,4},{28,0},{1,29},{... | collective-permute-start | bytes 196616 | tf_op jit(solution)/shard_map/ppermute | solution.py:344
  24.9 1.9 %collective-permute-start.7 = (bf16[1024,256]{1,0:T(8,128)(2,1)S(1)}, bf16[1024,256]{1,0:T(8,128)(2,1)S(1)}, u32[]{:S(2)}, u32[]{:S(2)}) collective-permute-start(bf16[1024,256]{1,0:T(8,128)(2,1)S(1)} %constant_dynamic-update-slice_fusion.own), channel_id=1, source_target_pairs={{0,1},{1,0},{2,3},{3,2},{4,5},{5,4},{6,7},{7,6},{8,9},{9,8},{10,11... | collective-permute-start | bytes 1572872 | tf_op jit(solution)/shard_map/ppermute | solution.py:351
  31.0 1.6 %collective-permute-start.8 = (bf16[128,1024]{1,0:T(8,128)(2,1)S(1)}, bf16[128,1024]{1,0:T(8,128)(2,1)S(1)}, u32[]{:S(2)}, u32[]{:S(2)}) collective-permute-start(bf16[128,1024]{1,0:T(8,128)(2,1)S(1)} %get-tuple-element.22), channel_id=1, source_target_pairs={{0,1},{1,0},{2,3},{3,2},{4,5},{5,4},{6,7},{7,6},{8,9},{9,8},{10,11... | collective-permute-start | bytes 786440 | tf_op jit(solution)/shard_map/ppermute | solution.py:261
  32.6 10.7 %copy-start.5 = (bf16[128,2048]{1,0:T(8,128)(2,1)}, bf16[128,2048]{1,0:T(8,128)(2,1)S(1)}, u32[]{:S(2)}) copy-start(bf16[128,2048]{1,0:T(8,128)(2,1)S(1)} %constant_dynamic-update-slice_fusion.8) | copy-start | bytes 1572868
  32.6 10.7 %collective-permute-start.10 = (bf16[128,2048]{1,0:T(8,128)(2,1)S(1)}, bf16[128,2048]{1,0:T(8,128)(2,1)S(1)}, u32[]{:S(2)}, u32[]{:S(2)}) collective-permute-start(bf16[128,2048]{1,0:T(8,128)(2,1)S(1)} %constant_dynamic-update-slice_fusion.8), channel_id=1, source_target_pairs={{0,8},{2,18},{4,12},{6,22},{9,17},{11,3},{13,21},{15,7},{16,24},{1... | collective-permute-start | bytes 1572872 | tf_op jit(solution)/shard_map/ppermute | solution.py:265
  34.0 12.3 %collective-permute-start.9 = (bf16[128,2048]{1,0:T(8,128)(2,1)S(1)}, bf16[128,2048]{1,0:T(8,128)(2,1)S(1)}, u32[]{:S(2)}, u32[]{:S(2)}) collective-permute-start(bf16[128,2048]{1,0:T(8,128)(2,1)S(1)} %constant_dynamic-update-slice_fusion.8), channel_id=1, source_target_pairs={{0,16},{2,10},{4,20},{6,14},{9,1},{11,19},{13,5},{15,23},{16,8},{1... | collective-permute-start | bytes 1572872 | tf_op jit(solution)/shard_map/ppermute | solution.py:264
  37.8 1.6 %collective-permute-start.12 = (bf16[128,1024]{1,0:T(8,128)(2,1)S(1)}, bf16[128,1024]{1,0:T(8,128)(2,1)S(1)}, u32[]{:S(2)}, u32[]{:S(2)}) collective-permute-start(bf16[128,1024]{1,0:T(8,128)(2,1)S(1)} %get-tuple-element.23), channel_id=1, source_target_pairs={{0,1},{1,0},{2,3},{3,2},{4,5},{5,4},{6,7},{7,6},{8,9},{9,8},{10,11... | collective-permute-start | bytes 786440 | tf_op jit(solution)/shard_map/ppermute | solution.py:261
  40.1 11.9 %collective-permute-start.13 = (bf16[128,2048]{1,0:T(8,128)(2,1)}, bf16[128,2048]{1,0:T(8,128)(2,1)S(1)}, u32[]{:S(2)}, u32[]{:S(2)}) collective-permute-start(bf16[128,2048]{1,0:T(8,128)(2,1)} %constant_dynamic-update-slice_fusion.10), channel_id=1, source_target_pairs={{0,16},{2,10},{4,20},{6,14},{9,1},{11,19},{13,5},{15,23},{16,8},{1... | collective-permute-start | bytes 1572872 | tf_op jit(solution)/shard_map/ppermute | solution.py:264
  42.0 15.6 %collective-permute-start.14 = (bf16[128,2048]{1,0:T(8,128)(2,1)}, bf16[128,2048]{1,0:T(8,128)(2,1)S(1)}, u32[]{:S(2)}, u32[]{:S(2)}) collective-permute-start(bf16[128,2048]{1,0:T(8,128)(2,1)} %constant_dynamic-update-slice_fusion.10), channel_id=1, source_target_pairs={{0,8},{2,18},{4,12},{6,22},{9,17},{11,3},{13,21},{15,7},{16,24},{1... | collective-permute-start | bytes 1572872 | tf_op jit(solution)/shard_map/ppermute | solution.py:265
  46.3 15.4 %collective-permute-start.11 = (bf16[128,2048]{1,0:T(8,128)(2,1)S(1)}, bf16[128,2048]{1,0:T(8,128)(2,1)S(1)}, u32[]{:S(2)}, u32[]{:S(2)}) collective-permute-start(bf16[128,2048]{1,0:T(8,128)(2,1)S(1)} %broadcast_select_fusion.1), channel_id=1, source_target_pairs={{8,0},{9,1},{10,2},{11,3},{12,4},{13,5},{14,6},{15,7},{16,24},{17,... | collective-permute-start | bytes 1572872 | tf_op jit(solution)/shard_map/ppermute | solution.py:282
  57.7 6.9 %copy-start = (bf16[1024,2048]{1,0:T(8,128)(2,1)S(1)}, bf16[1024,2048]{1,0:T(8,128)(2,1)}, u32[]{:S(2)}) copy-start(bf16[1024,2048]{1,0:T(8,128)(2,1)} %own.1) | copy-start | bytes 12582916
  57.7 18.9 %collective-permute-start.15 = (bf16[128,2048]{1,0:T(8,128)(2,1)S(1)}, bf16[128,2048]{1,0:T(8,128)(2,1)S(1)}, u32[]{:S(2)}, u32[]{:S(2)}) collective-permute-start(bf16[128,2048]{1,0:T(8,128)(2,1)S(1)} %broadcast_select_fusion), channel_id=1, source_target_pairs={{8,0},{9,1},{10,2},{11,3},{12,4},{13,5},{14,6},{15,7},{16,24},{17,... | collective-permute-start | bytes 1572872 | tf_op jit(solution)/shard_map/ppermute | solution.py:282
  63.0 16.2 %collective-permute-start.17 = (bf16[128,2048]{1,0:T(8,128)(2,1)S(1)}, bf16[128,2048]{1,0:T(8,128)(2,1)S(1)}, u32[]{:S(2)}, u32[]{:S(2)}) collective-permute-start(bf16[128,2048]{1,0:T(8,128)(2,1)S(1)} %broadcast_select_fusion.6.rows), channel_id=1, source_target_pairs={{0,4},{4,0},{8,12},{12,8},{16,20},{20,16},{24,28},{28,24},{1,5},{5... | collective-permute-start | bytes 1572872 | tf_op jit(solution)/shard_map/ppermute | solution.py:292
  68.4 21.0 %collective-permute-start.20 = (bf16[128,2048]{1,0:T(8,128)(2,1)S(1)}, bf16[128,2048]{1,0:T(8,128)(2,1)S(1)}, u32[]{:S(2)}, u32[]{:S(2)}) collective-permute-start(bf16[128,2048]{1,0:T(8,128)(2,1)S(1)} %project.6), channel_id=1, source_target_pairs={{0,2},{1,3},{2,0},{3,1},{4,6},{5,7},{6,4},{7,5},{8,10},{9,11},{10,... | collective-permute-start | bytes 1572872 | tf_op jit(solution)/shard_map/ppermute | solution.py:278
  76.6 32.2 %collective-permute-start.21 = (bf16[128,2048]{1,0:T(8,128)(2,1)S(1)}, bf16[128,2048]{1,0:T(8,128)(2,1)S(1)}, u32[]{:S(2)}, u32[]{:S(2)}) collective-permute-start(bf16[128,2048]{1,0:T(8,128)(2,1)S(1)} %get-tuple-element.31), channel_id=1, source_target_pairs={{0,4},{4,0},{8,12},{12,8},{16,20},{20,16},{24,28},{28,24},{1,5},{5... | collective-permute-start | bytes 1572872 | tf_op jit(solution)/shard_map/ppermute | solution.py:295
  79.1 21.6 %collective-permute-start.19 = (bf16[128,2048]{1,0:T(8,128)(2,1)S(1)}, bf16[128,2048]{1,0:T(8,128)(2,1)S(1)}, u32[]{:S(2)}, u32[]{:S(2)}) collective-permute-start(bf16[128,2048]{1,0:T(8,128)(2,1)S(1)} %project.7), channel_id=1, source_target_pairs={{0,2},{1,3},{2,0},{3,1},{4,6},{5,7},{6,4},{7,5},{8,10},{9,11},{10,... | collective-permute-start | bytes 1572872 | tf_op jit(solution)/shard_map/ppermute | solution.py:278
  79.2 23.5 %collective-permute-start.18 = (bf16[128,2048]{1,0:T(8,128)(2,1)S(1)}, bf16[128,2048]{1,0:T(8,128)(2,1)S(1)}, u32[]{:S(2)}, u32[]{:S(2)}) collective-permute-start(bf16[128,2048]{1,0:T(8,128)(2,1)S(1)} %get-tuple-element.27.rows), channel_id=1, source_target_pairs={{0,4},{4,0},{8,12},{12,8},{16,20},{20,16},{24,28},{28,24},{1,5},{5... | collective-permute-start | bytes 1572872 | tf_op jit(solution)/shard_map/ppermute | solution.py:292
  81.3 27.6 %collective-permute-start.22 = (bf16[128,2048]{1,0:T(8,128)(2,1)S(1)}, bf16[128,2048]{1,0:T(8,128)(2,1)S(1)}, u32[]{:S(2)}, u32[]{:S(2)}) collective-permute-start(bf16[128,2048]{1,0:T(8,128)(2,1)S(1)} %broadcast_select_fusion.5), channel_id=1, source_target_pairs={{0,4},{4,0},{8,12},{12,8},{16,20},{20,16},{24,28},{28,24},{1,5},{5... | collective-permute-start | bytes 1572872 | tf_op jit(solution)/shard_map/ppermute | solution.py:295
  90.7 21.1 %collective-permute-start.23 = (bf16[128,2048]{1,0:T(8,128)(2,1)S(1)}, bf16[128,2048]{1,0:T(8,128)(2,1)S(1)}, u32[]{:S(2)}, u32[]{:S(2)}) collective-permute-start(bf16[128,2048]{1,0:T(8,128)(2,1)S(1)} %project.8), channel_id=1, source_target_pairs={{0,2},{1,3},{2,0},{3,1},{4,6},{5,7},{6,4},{7,5},{8,10},{9,11},{10,... | collective-permute-start | bytes 1572872 | tf_op jit(solution)/shard_map/ppermute | solution.py:278
  104.0 11.5 %collective-permute-start.24 = (bf16[128,2048]{1,0:T(8,128)(2,1)S(1)}, bf16[128,2048]{1,0:T(8,128)(2,1)S(1)}, u32[]{:S(2)}, u32[]{:S(2)}) collective-permute-start(bf16[128,2048]{1,0:T(8,128)(2,1)S(1)} %project.9), channel_id=1, source_target_pairs={{0,2},{1,3},{2,0},{3,1},{4,6},{5,7},{6,4},{7,5},{8,10},{9,11},{10,... | collective-permute-start | bytes 1572872 | tf_op jit(solution)/shard_map/ppermute | solution.py:278
  111.9 3.6 %copy-start.4 = (bf16[512,2048]{1,0:T(8,128)(2,1)}, bf16[512,2048]{1,0:T(8,128)(2,1)S(1)}, u32[]{:S(2)}) copy-start(bf16[512,2048]{1,0:T(8,128)(2,1)S(1)} %fusion.6) | copy-start | bytes 6291460
